TPU v7x, 32 devices: a whole 2x2x4 slice. The times are simulated.
32 devices in a mesh: seq: 8 (over z, x), ch: 4 (over y, core).
Axes of the slice: x: 2, y: 2, z: 4, core: 2. Of those that a mesh axis runs over, the one named last changes fastest.
Arguments:
- inputs: float32 [2048, 4096], P('seq', 'ch'), may hold values from -6 to 6
- out_grads: float32 [2048, 4096], P('seq', 'ch'), may hold values from -0.12 to 0.12
- tile_order: int32 [8], replicated, may hold values from 0 to 7, each once
- lag_order: int32 [8], replicated, may hold values from 0 to 7, each once
Outputs:
- filter_grad: float32 [256, 2048], P('ch', 'seq')
Inputs may be any that keep to these rules, and one draw needn't show every extreme that they name: Row block i of inputs and out_grads holds sequence tile tile_order[i]; every tile appears once. Column block i of filter_grad holds lag block lag_order[i]; every lag block appears once.
All inputs are finite; a program needn't handle non-finite values.
Results may differ from a plain program's by a relative error of at most 0.000098.
Values sent between devices are 32-bit elements; how exact they have to be, the bound alone decides.
No kernel may reach another device: no remote copies, remote signals or barrier semaphores. Data moves between devices by JAX's collectives and lax.ppermute only.
A program may use at most 128 MiB of HBM per device.

v0:
```python
import math

import jax
import jax.numpy as jnp
from jax import lax
from jax.sharding import PartitionSpec as P

C = 4096
GROUP = 16


target_ratio = 0.5
epsilon = 1e-12
highest = lax.Precision.HIGHEST


def forward_table(tile_rows):
    double_rows = 2 * tile_rows
    frequency = lax.iota(jnp.int32, tile_rows + 1)[:, None]
    places = lax.iota(jnp.int32, tile_rows)[None, :]
    angles = (frequency * places % double_rows).astype(jnp.float32) * (math.pi / tile_rows)
    cosine_rows = jnp.cos(angles)
    sine_rows = -jnp.sin(angles[1:tile_rows])
    return jnp.concatenate([cosine_rows, sine_rows], axis=0)


def inverse_table(tile_rows):
    double_rows = 2 * tile_rows
    frequency = lax.iota(jnp.int32, tile_rows + 1)[:, None]
    lag_index = lax.iota(jnp.int32, double_rows)[None, :]
    angles = (frequency * lag_index % double_rows).astype(jnp.float32) * (math.pi / tile_rows)
    weights = jnp.where((frequency == 0) | (frequency == tile_rows), 1.0, 2.0).astype(jnp.float32)
    cosine_rows = weights * jnp.cos(angles) / double_rows
    sine_rows = -2.0 * jnp.sin(angles[1:tile_rows]) / double_rows
    return jnp.concatenate([cosine_rows, sine_rows], axis=0)


def tile_tables(tile_order, blocks):
    tile_freqs = 2 * blocks
    frequency = lax.iota(jnp.int32, tile_freqs)[:, None]
    angles = (frequency * tile_order[None, :] % tile_freqs).astype(jnp.float32) * (math.pi / blocks)
    return (jnp.cos(angles), -jnp.sin(angles))


def offset_tables(offsets, blocks):
    tile_freqs = 2 * blocks
    frequency = lax.iota(jnp.int32, tile_freqs)[None, :]
    angles = (offsets[:, None] * frequency % tile_freqs).astype(jnp.float32) * (math.pi / blocks)
    return (jnp.cos(angles) / tile_freqs, -jnp.sin(angles) / tile_freqs)


def split_packed(values, tile_rows):
    return (values[..., : tile_rows + 1], values[..., tile_rows + 1 :])


def conj_product(first_real, first_imag, second_real, second_imag):
    return (
        first_real * second_real + first_imag * second_imag,
        first_real * second_imag - first_imag * second_real,
    )


def tile_products(input_cos, input_sin, grad_cos, grad_sin, tile_rows):
    input_real_cos, input_imag_cos = split_packed(input_cos, tile_rows)
    input_real_sin, input_imag_sin = split_packed(input_sin, tile_rows)
    grad_real_cos, grad_imag_cos = split_packed(grad_cos, tile_rows)
    grad_real_sin, grad_imag_sin = split_packed(grad_sin, tile_rows)
    both_real = conj_product(input_real_cos, input_real_sin, grad_real_cos, grad_real_sin)
    both_imag = conj_product(input_imag_cos, input_imag_sin, grad_imag_cos, grad_imag_sin)
    cross_first = conj_product(
        input_real_cos[..., 1:tile_rows],
        input_real_sin[..., 1:tile_rows],
        grad_imag_cos,
        grad_imag_sin,
    )
    cross_second = conj_product(
        input_imag_cos,
        input_imag_sin,
        grad_real_cos[..., 1:tile_rows],
        grad_real_sin[..., 1:tile_rows],
    )
    pad_edges = ((0, 0), (0, 0), (1, 1))
    cosine_terms = jnp.concatenate(
        [both_real[0] + jnp.pad(both_imag[0], pad_edges), cross_first[0] - cross_second[0]], axis=-1
    )
    sine_terms = jnp.concatenate(
        [both_real[1] + jnp.pad(both_imag[1], pad_edges), cross_first[1] - cross_second[1]], axis=-1
    )
    channel_count = cosine_terms.shape[0]
    grouped_shape = (channel_count // GROUP, GROUP) + cosine_terms.shape[1:]
    return (
        cosine_terms.reshape(grouped_shape).sum(axis=1),
        sine_terms.reshape(grouped_shape).sum(axis=1),
    )


def shards(inputs, out_grads, tile_order, lag_order):
    tile_rows = inputs.shape[0]
    seq_devices = lax.axis_size("seq")
    lag_total = tile_rows * seq_devices
    forward = forward_table(tile_rows)
    inverse = inverse_table(tile_rows)
    tile_cos, tile_sin = tile_tables(tile_order, seq_devices)
    moved_inputs, moved_grads = (
        lax.all_to_all(inputs.T, "seq", split_axis=0, concat_axis=1, tiled=True),
        lax.all_to_all(out_grads.T, "seq", split_axis=0, concat_axis=1, tiled=True),
    )
    slice_channels = moved_inputs.shape[0]
    stacked = jnp.concatenate([moved_inputs, moved_grads], axis=0).reshape(
        2 * slice_channels, seq_devices, tile_rows
    )
    spectra = jnp.einsum(
        "cst,ft->csf", stacked, forward, precision=highest, preferred_element_type=jnp.float32
    )
    cosine_part = jnp.einsum(
        "ks,csf->ckf", tile_cos, spectra, precision=highest, preferred_element_type=jnp.float32
    )
    sine_part = jnp.einsum(
        "ks,csf->ckf", tile_sin, spectra, precision=highest, preferred_element_type=jnp.float32
    )
    cosine_sum, sine_sum = tile_products(
        cosine_part[:slice_channels],
        sine_part[:slice_channels],
        cosine_part[slice_channels:],
        sine_part[slice_channels:],
        tile_rows,
    )
    offsets = jnp.concatenate([lag_order, lag_order + 1], axis=0)
    offset_cos, offset_sin = offset_tables(offsets, seq_devices)
    offset_spec = jnp.einsum(
        "ik,gkf->gif", offset_cos, cosine_sum, precision=highest, preferred_element_type=jnp.float32
    )
    offset_spec = offset_spec + jnp.einsum(
        "ik,gkf->gif", offset_sin, sine_sum, precision=highest, preferred_element_type=jnp.float32
    )
    circular = jnp.einsum(
        "gif,fl->gil", offset_spec, inverse, precision=highest, preferred_element_type=jnp.float32
    )
    present = (lag_order + 1 < seq_devices).astype(jnp.float32)
    lag_values = (
        circular[:, :seq_devices, :tile_rows]
        + circular[:, seq_devices:, tile_rows:] * present[None, :, None]
    )
    groups_local = lag_values.shape[0]
    owned = lax.all_to_all(
        lag_values.reshape(groups_local, lag_total), "seq", split_axis=1, concat_axis=0, tiled=True
    )
    squares = lax.psum(jnp.sum(owned * owned), ("seq", "ch"))
    total_entries = C // GROUP * lag_total
    factor = target_ratio * math.sqrt(total_entries) / jnp.sqrt(squares + epsilon)
    return owned * factor


def solution(mesh):
    return jax.shard_map(
        shards,
        mesh=mesh,
        in_specs=(P("seq", "ch"), P("seq", "ch"), P(), P()),
        out_specs=P("ch", "seq"),
        check_vma=False,
    )
```

profile of v0, /device:TPU:0, one launch (start us, length us, event | category | flops | bytes accessed | tf_op | source)
XLA Modules:
  0.0 167.1 jit_solution(2274491869236608964)
XLA Ops:
  0.0 2.7 %copy.14 = f32[1024,256]{1,0:T(8,128)} copy(f32[1024,256]{0,1:T(8,128)} %bitcast.45) | data formatting | bytes 2097152 | tf_op jit(solution)/shard_map/transpose | solution.py:105
  2.7 7.3 %all-to-all-start = ((f32[8,128,256]{2,1,0:T(8,128)}), f32[8,128,256]{2,1,0:T(8,128)S(1)}, u32[]{:S(2)}, u32[]{:S(2)}) async-start(f32[8,128,256]{2,1,0:T(8,128)} %bitcast.1), calls=%async_computation | async-start | bytes 2097152 | tf_op jit(solution)/shard_map/all_to_all | solution.py:105
  9.9 1.3 copy.15
  11.3 24.4 %all-to-all-done = f32[8,128,256]{2,1,0:T(8,128)S(1)} async-done(((f32[8,128,256]{2,1,0:T(8,128)}), f32[8,128,256]{2,1,0:T(8,128)S(1)}, u32[]{:S(2)}, u32[]{:S(2)}) %all-to-all-start) | async-done | bytes 1048608 | tf_op jit(solution)/shard_map/all_to_all | solution.py:105
  35.7 3.6 %all-to-all-start.1 = ((f32[8,128,256]{2,1,0:T(8,128)}), f32[8,128,256]{2,1,0:T(8,128)S(1)}, u32[]{:S(2)}, u32[]{:S(2)}) async-start(f32[8,128,256]{2,1,0:T(8,128)} %bitcast.4), calls=%async_computation.1 | async-start | bytes 2097152 | tf_op jit(solution)/shard_map/all_to_all | solution.py:106
  39.3 0.1 pad_add_fusion.2
  39.4 0.1 fusion.17
  39.5 1.0 fusion.22
  40.5 0.3 fusion.8
  40.8 1.6 fusion.21
  42.4 2.0 %multiply_multiply_fusion = f32[257,512]{1,0:T(8,128)S(1)} fusion(f32[257]{0:T(512)S(1)} %fusion.56), kind=kLoop, calls=%fused_computation.27 | loop fusion | flops 2105344 | bytes 527364 | tf_op jit(solution)/shard_map/div | solution.py:33
  44.4 2.0 %fusion.12 = f32[255,512]{1,0:T(8,128)S(1)} fusion(f32[257,512]{1,0:T(8,128)S(1)} %fusion.8), kind=kLoop, calls=%fused_computation.32 | loop fusion | flops 130560 | bytes 1044480 | tf_op jit(solution)/shard_map/div | solution.py:34
  46.4 18.9 %all-to-all-done.1 = f32[8,128,256]{2,1,0:T(8,128)S(1)} async-done(((f32[8,128,256]{2,1,0:T(8,128)}), f32[8,128,256]{2,1,0:T(8,128)S(1)}, u32[]{:S(2)}, u32[]{:S(2)}) %all-to-all-start.1) | async-done | bytes 1048608 | tf_op jit(solution)/shard_map/all_to_all | solution.py:106
  65.2 0.2 pad_maximum_fusion.2
  65.5 0.7 copy-done.4
  66.2 4.7 %fusion = f32[256,8,512]{2,1,0:T(8,128)S(1)} fusion(f32[256,8,256]{2,0,1:T(8,128)S(1)} %pad_maximum_fusion.2, f32[255,256]{1,0:T(8,128)S(1)} %copy-done.4, f32[257,256]{1,0:T(8,128)S(1)} %fusion.22), kind=kOutput, calls=%fused_computation.9 | convolution fusion | flops 3221356544 | bytes 6815744 | tf_op jit(solution)/shard_map/cst,ft->csf/dot_general | solution.py:112
  70.9 8.4 %convolution_bitcast_fusion = f32[256,16,512]{2,1,0:T(8,128)S(1)} fusion(f32[256,8,512]{2,1,0:T(8,128)S(1)} %fusion, s32[8]{0:T(128)S(1)} %copy-done.5), kind=kOutput, calls=%fused_computation.4 | convolution fusion | flops 201328512 | bytes 12582944 | tf_op jit(solution)/shard_map/ks,csf->ckf/dot_general | solution.py:118
  79.3 8.6 %convolution_bitcast_fusion.1 = f32[256,16,512]{2,1,0:T(8,128)S(1)} fusion(f32[256,8,512]{2,1,0:T(8,128)S(1)} %fusion, s32[8]{0:T(128)S(1)} %copy-done.5), kind=kOutput, calls=%fused_computation.5 | convolution fusion | flops 201328384 | bytes 12582944 | tf_op jit(solution)/shard_map/ks,csf->ckf/dot_general | solution.py:115
  87.9 3.2 %copy-done = f32[256,16,512]{2,1,0:T(8,128)} copy-done((f32[256,16,512]{2,1,0:T(8,128)}, f32[256,16,512]{2,1,0:T(8,128)S(1)}, u32[]{:S(2)}) %copy-start) | copy-done | bytes 8388632
  91.1 6.1 %multiply_subtract_fusion = (f32[128,16,255]{2,1,0:T(8,128)}, f32[128,16,255]{2,1,0:T(8,128)}, f32[128,16,255]{2,1,0:T(8,128)}) fusion(f32[256,16,512]{2,1,0:T(8,128)S(1)} %convolution_bitcast_fusion, f32[256,16,512]{2,1,0:T(8,128)S(1)} %convolution_bitcast_fusion.1), kind=kLoop, calls=%fused_computation.12 | loop fusion | flops 6789120 | bytes 22978560 | tf_op jit(solution)/shard_map/sub | solution.py:59
  97.2 10.0 %subtract_subtract_fusion = f32[128,16,255]{2,1,0:T(8,128)} fusion(f32[256,16,512]{2,1,0:T(8,128)S(1)} %convolution_bitcast_fusion, f32[256,16,512]{2,1,0:T(8,128)} %copy-done), kind=kLoop, calls=%fused_computation.11 | loop fusion | flops 3655680 | bytes 18800640 | tf_op jit(solution)/shard_map/sub | solution.py:87
  107.2 5.1 %pad_add_fusion = (f32[128,16,257]{2,1,0:T(8,128)S(1)}, f32[128,16,257]{2,1,0:T(8,128)S(1)}) fusion(f32[128,16,255]{2,1,0:T(8,128)} %get-tuple-element.7, f32[256,16,512]{2,1,0:T(8,128)S(1)} %convolution_bitcast_fusion, f32[256,16,512]{2,1,0:T(8,128)} %copy-done, f32[128,16,255]{2,1,0:T(8,128)} %get-tuple-element.9), kind=kLoop, calls=%fused_computation.6 | loop fusion | flops 4210688 | bytes 16809984 | tf_op jit(solution)/shard_map/add | solution.py:87
  112.3 0.1 copy-done.2
  112.5 1.9 %bitcast_reduce_fusion = (f32[8,16,512]{2,1,0:T(8,128)S(1)}, f32[8,16,512]{2,1,0:T(8,128)S(1)}) fusion(f32[128,16,255]{2,1,0:T(8,128)S(1)} %copy-done.1, f32[128,16,257]{2,1,0:T(8,128)S(1)} %get-tuple-element.5, f32[128,16,255]{2,1,0:T(8,128)S(1)} %copy-done.2, f32[128,16,257]{2,1,0:T(8,128)S(1)} %get-tuple-element.6), kind=kLoop, calls=%fused_computation.2 | loop fusion | flops 4063232 | bytes 8912896 | tf_op jit(solution)/shard_map/reduce_sum | solution.py:93
  114.4 0.5 fusion.28
  114.8 0.5 fusion.2
  115.3 0.7 fusion.3
  116.1 0.1 fusion.23
  116.2 10.3 %all_to_all.42 = f32[8,8,256]{2,0,1:T(8,128)S(1)} all-to-all(f32[8,8,256]{2,0,1:T(8,128)S(1)} %copy.18), channel_id=1, replica_groups=mesh['seq'=8,'ch'=4] {'seq'}, dimensions={1} | all-to-all | bytes 131072 | tf_op jit(solution)/shard_map/all_to_all | solution.py:145
  126.5 0.6 multiply_reduce_fusion
  127.1 38.6 %psum.7 = f32[]{:T(128)} all-reduce(f32[]{:T(128)} %multiply_reduce_fusion), channel_id=1, replica_groups=mesh['seq'=8,'ch'=4] {'seq','ch'}, use_global_device_ids=true, to_apply=%region_3.4 | all-reduce | flops 1 | bytes 8 | tf_op jit(solution)/shard_map/psum | solution.py:148
  166.4 0.6 multiply_bitcast_fusion
  (15 shorter events, 0.1 us)
Async XLA Ops:
  0.0 9.9 %copy-start.3 = (f32[256,1024]{1,0:T(8,128)S(1)}, f32[256,1024]{1,0:T(8,128)}, u32[]{:S(2)}) copy-start(f32[256,1024]{1,0:T(8,128)} %param.5) | copy-start | bytes 3145732
  2.7 33.0 %all-to-all-start = ((f32[8,128,256]{2,1,0:T(8,128)}), f32[8,128,256]{2,1,0:T(8,128)S(1)}, u32[]{:S(2)}, u32[]{:S(2)}) async-start(f32[8,128,256]{2,1,0:T(8,128)} %bitcast.1), calls=%async_computation | async-start | bytes 2097152 | tf_op jit(solution)/shard_map/all_to_all | solution.py:105
  9.9 29.4 %copy-start.6 = (s32[8]{0:T(128)S(1)}, s32[8]{0:T(128)}, u32[]{:S(2)}) copy-start(s32[8]{0:T(128)} %param.7) | copy-start | bytes 100
  35.7 29.5 %all-to-all-start.1 = ((f32[8,128,256]{2,1,0:T(8,128)}), f32[8,128,256]{2,1,0:T(8,128)S(1)}, u32[]{:S(2)}, u32[]{:S(2)}) async-start(f32[8,128,256]{2,1,0:T(8,128)} %bitcast.4), calls=%async_computation.1 | async-start | bytes 2097152 | tf_op jit(solution)/shard_map/all_to_all | solution.py:106
  65.2 1.0 copy-start.4
  66.2 4.7 %copy-start.5 = (s32[8]{0:T(128)S(1)}, s32[8]{0:T(128)}, u32[]{:S(2)}) copy-start(s32[8]{0:T(128)} %param.6) | copy-start | bytes 100
  87.9 3.2 %copy-start = (f32[256,16,512]{2,1,0:T(8,128)}, f32[256,16,512]{2,1,0:T(8,128)S(1)}, u32[]{:S(2)}) copy-start(f32[256,16,512]{2,1,0:T(8,128)S(1)} %convolution_bitcast_fusion.1) | copy-start | bytes 25165828
  107.2 5.2 %copy-start.1 = (f32[128,16,255]{2,1,0:T(8,128)S(1)}, f32[128,16,255]{2,1,0:T(8,128)}, u32[]{:S(2)}) copy-start(f32[128,16,255]{2,1,0:T(8,128)} %subtract_subtract_fusion) | copy-start | bytes 6266884
  107.2 5.3 %copy-start.2 = (f32[128,16,255]{2,1,0:T(8,128)S(1)}, f32[128,16,255]{2,1,0:T(8,128)}, u32[]{:S(2)}) copy-start(f32[128,16,255]{2,1,0:T(8,128)} %get-tuple-element.8) | copy-start | bytes 6266884
where the time goes:
time: 168 us; the launch traced here: 167 us
  blocking collectives  49 us (29%)
  waiting for transfers between devices  43.3 us (26%)
  other arithmetic  31.7 us (19%)
  matrix products  23.4 us (14%)
  starting transfers between devices  10.8 us (6%)
  local copies, waits for them, and re-layouts  8.08 us (5%)
    psum x1, blocking collectives, shards(): squares = lax.psum(jnp.sum(owned * owned), ('seq', 'ch'))  38.6 us
    all_to_all x1, waiting for transfers between devices, shards(): lax.all_to_all(inputs.T, 'seq', split_axis=0, concat_axis=1, tiled=True)  24.4 us
    all_to_all x1, waiting for transfers between devices, shards(): lax.all_to_all(out_grads.T, 'seq', split_axis=0, concat_axis=1, tiled=True)  18.9 us
    all_to_all x1, blocking collectives, shards(): lax.all_to_all(lag_values.reshape(groups_local, lag_total), 'seq', split_...  10.3 us
    sub x1, other arithmetic, tile_products(): cross_first[1] - cross_second[1]  9.96 us
    dot_general x1, matrix products, shards(): jnp.einsum('ks,csf->ckf', tile_cos, spectra, precision=highest, preferred...  8.56 us
    dot_general x1, matrix products, shards(): jnp.einsum('ks,csf->ckf', tile_sin, spectra, precision=highest, preferred...  8.45 us
    all_to_all x1, starting transfers between devices, shards(): lax.all_to_all(inputs.T, 'seq', split_axis=0, concat_axis=1, tiled=True)  7.25 us
  transfers between devices with their start and end apart: 2, of which 2 were waited for; matrix products, arithmetic and copies ran while one was open for 5% of the time, Pallas kernels for 0%

commit v1 on v0

v1 whole, which is shorter than its diff:
```python
import functools
import math

import jax
import jax.numpy as jnp
import ml_dtypes
import numpy as np
from jax import lax
from jax.experimental import pallas as pl
from jax.experimental.pallas import tpu as pltpu
from jax.sharding import PartitionSpec as P

GROUP = 16
target_ratio = 0.5
epsilon = 1e-12


def halves(table):
    high = table.astype(ml_dtypes.bfloat16)
    low = (table - high.astype(np.float64)).astype(ml_dtypes.bfloat16)
    return high, low


def forward_table(rows):
    angles = np.outer(2 * np.arange(rows) + 1, np.arange(rows)) % (4 * rows) * (math.pi / (2 * rows))
    high, low = halves(np.concatenate([np.cos(angles), -np.sin(angles)], axis=0))
    return np.concatenate([high, low, high], axis=1)


def inverse_table(rows):
    angles = np.outer(2 * np.arange(rows) + 1, np.arange(2 * rows)) % (4 * rows) * (math.pi / (2 * rows))
    sign = np.where(np.arange(2 * rows) < rows, 1.0, -1.0) / rows
    high, low = halves(np.concatenate([np.cos(angles) * sign, -np.sin(angles) * sign], axis=0))
    return np.concatenate([high, high, low], axis=0)


def group_table(tiles, channels):
    columns = np.arange(tiles * channels)
    return (columns[:, None] // GROUP == np.arange(tiles * channels // GROUP)[None, :]).astype(ml_dtypes.bfloat16)


def split(values):
    high = values.astype(jnp.bfloat16)
    low = (values - high.astype(jnp.float32)).astype(jnp.bfloat16)
    return high, low


def lag_kernel(tiles, channels, rows, tile_ref, lag_ref, forward_ref, inverse_ref, group_ref, *refs):
    blocks, (out_ref, spectra, products, natural) = refs[:tiles], refs[tiles:]
    groups = channels // GROUP
    for slot in range(tiles):
        high, low = split(blocks[slot][...])
        spectra[tile_ref[slot]] = jnp.dot(
            forward_ref[...],
            jnp.concatenate([high, high, low], axis=0),
            preferred_element_type=jnp.float32,
        )

    def row_step(step, carry):
        real = pl.ds(pl.multiple_of(step * 8, 8), 8)
        imag = pl.ds(pl.multiple_of(rows + step * 8, 8), 8)
        input_real = [spectra[tile, real, :channels] for tile in range(tiles)]
        input_imag = [spectra[tile, imag, :channels] for tile in range(tiles)]
        grad_real = [spectra[tile, real, channels:] for tile in range(tiles)]
        grad_imag = [spectra[tile, imag, channels:] for tile in range(tiles)]
        for offset in range(tiles):
            total_real = total_imag = None
            for tile in range(tiles - offset):
                first, second = (input_real[tile], input_imag[tile]), (grad_real[tile + offset], grad_imag[tile + offset])
                term_real = first[0] * second[0] + first[1] * second[1]
                term_imag = first[0] * second[1] - first[1] * second[0]
                total_real = term_real if total_real is None else total_real + term_real
                total_imag = term_imag if total_imag is None else total_imag + term_imag
            columns = slice(offset * channels, (offset + 1) * channels)
            products[real, columns] = total_real
            products[imag, columns] = total_imag
        return carry

    lax.fori_loop(0, rows // 8, row_step, 0)
    high, low = split(products[...])
    grouped = jnp.dot(high, group_ref[...], preferred_element_type=jnp.float32)
    grouped = grouped + jnp.dot(low, group_ref[...], preferred_element_type=jnp.float32)
    high, low = split(grouped.T)
    circular = jnp.dot(
        jnp.concatenate([high, low, high], axis=1), inverse_ref[...], preferred_element_type=jnp.float32
    )
    following = jnp.concatenate([circular[groups:, rows:], jnp.zeros((groups, rows), jnp.float32)], axis=0)
    lags = circular[:, :rows] + following
    squares = jnp.broadcast_to(jnp.sum(lags * lags, keepdims=True), (8, rows))
    for offset in range(tiles):
        natural[offset] = lags[offset * groups : (offset + 1) * groups]
    for slot in range(tiles):
        out_ref[slot, :groups, :] = natural[lag_ref[slot]]
        out_ref[slot, groups:, :] = squares


def lag_values(blocks, block_tiles, lag_order):
    tiles = len(blocks)
    rows, channels = blocks[0].shape[0], blocks[0].shape[1] // 2
    groups = channels // GROUP
    vmem = pl.BlockSpec(memory_space=pltpu.VMEM)
    smem = pl.BlockSpec(memory_space=pltpu.SMEM)
    return pl.pallas_call(
        functools.partial(lag_kernel, tiles, channels, rows),
        out_shape=jax.ShapeDtypeStruct((tiles, groups + 8, rows), jnp.float32),
        in_specs=[smem, smem] + [vmem] * (3 + tiles),
        out_specs=vmem,
        scratch_shapes=[
            pltpu.VMEM((tiles, 2 * rows, 2 * channels), jnp.float32),
            pltpu.VMEM((2 * rows, tiles * channels), jnp.float32),
            pltpu.VMEM((tiles, groups, rows), jnp.float32),
        ],
        compiler_params=pltpu.CompilerParams(vmem_limit_bytes=48 * 2**20),
        cost_estimate=pl.CostEstimate(
            flops=12 * tiles * rows * rows * channels, bytes_accessed=tiles * rows * channels * 8, transcendentals=0
        ),
    )(
        block_tiles,
        lag_order,
        jnp.asarray(forward_table(rows)),
        jnp.asarray(inverse_table(rows)),
        jnp.asarray(group_table(tiles, channels)),
        *blocks,
    )


def exchanges(count, place):
    if count & (count - 1) == 0:
        return [([(here, here ^ step) for here in range(count)], place ^ step, place ^ step) for step in range(count)]
    return [
        ([(here, (here + step) % count) for here in range(count)], (place + step) % count, (place - step) % count)
        for step in range(count)
    ]


def shards(inputs, out_grads, tile_order, lag_order):
    count = lax.axis_size("seq")
    rows = inputs.shape[0]
    channels = inputs.shape[1] // count
    blocks, sources = [], []
    for step, (pairs, target, source) in enumerate(exchanges(count, lax.axis_index("seq"))):
        block = jnp.concatenate(
            [
                lax.dynamic_slice_in_dim(inputs, target * channels, channels, 1),
                lax.dynamic_slice_in_dim(out_grads, target * channels, channels, 1),
            ],
            axis=1,
        )
        blocks.append(lax.ppermute(block, "seq", pairs) if step else block)
        sources.append(source)
    block_tiles = tile_order[jnp.stack(sources)]
    sent = lag_values(blocks, block_tiles, lag_order)
    groups = channels // GROUP
    owned = lax.all_to_all(sent, "seq", split_axis=0, concat_axis=0, tiled=True)
    squares = jnp.sum(owned[:, groups, :128], axis=0)
    ways = lax.axis_size("ch")
    total = squares
    for step in range(1, ways):
        total = total + lax.ppermute(squares, "ch", [(place, (place + step) % ways) for place in range(ways)])
    lags = owned[:, :groups, :].reshape(count * groups, rows)
    entries = ways * count * groups * count * rows
    factor = target_ratio * math.sqrt(entries) / jnp.sqrt(total[:1] + epsilon)
    return lags * factor


def solution(mesh):
    return jax.shard_map(
        shards,
        mesh=mesh,
        in_specs=(P("seq", "ch"), P("seq", "ch"), P(), P()),
        out_specs=P("ch", "seq"),
        check_vma=False,
    )
```

time: 168 us -> 76.8 us (0.46)
  blocking collectives: 49 us -> 14.6 us
  matrix products: 23.4 us -> 0 us
  other arithmetic: 31.7 us -> 8.62 us
  waiting for transfers between devices: 43.3 us -> 26.5 us
  Pallas kernels: 0 us -> 6.79 us
  starting transfers between devices: 10.8 us -> 16.5 us
  local copies, waits for them, and re-layouts: 8.08 us -> 3.31 us
    all_to_all x2 -> x0, waiting for transfers between devices: 43.3 us -> none  [the longest x1 24.4 us: shards(): lax.all_to_all(inputs.T, 'seq', split_axis=0, concat_axis=1, tiled=True)]
    psum x1 -> x0, blocking collectives: 38.6 us -> none  [shards(): squares = lax.psum(jnp.sum(owned * owned), ('seq', 'ch'))]
    ppermute x0 -> x10, waiting for transfers between devices: none -> 26.5 us  [the longest x7 23.7 us: shards(): blocks.append(lax.ppermute(block, 'seq', pairs) if step else block)]
    dot_general x6 -> x0, matrix products: 23.4 us -> none  [the longest x1 8.56 us: shards(): jnp.einsum('ks,csf->ckf', tile_cos, spectra, precision=highest, preferred...]
    ppermute x0 -> x10, starting transfers between devices: none -> 16.5 us  [the longest x7 14.7 us: shards(): blocks.append(lax.ppermute(block, 'seq', pairs) if step else block)]
    sub x2 -> x0, other arithmetic: 16 us -> none  [the longest x1 9.96 us: tile_products(): cross_first[1] - cross_second[1]]
    all_to_all x2 -> x0, starting transfers between devices: 10.8 us -> none  [the longest x1 7.25 us: shards(): lax.all_to_all(inputs.T, 'seq', split_axis=0, concat_axis=1, tiled=True)]
    concatenate x2 -> x8, other arithmetic: 0.3 us -> 7.94 us  [shards(): jnp.concatenate([lax.dynamic_slice_in_dim(inputs, target * channels, chan...]
  transfers between devices with their start and end apart: 2 -> 10, of which waited for: 2 -> 6; matrix products, arithmetic and copies ran while one was open for 5% -> 10% of each run, Pallas kernels for 0% -> 0%
where the time goes in v1:
time: 76.8 us; the launch traced here: 76.6 us
  waiting for transfers between devices  26.5 us (35%)
  starting transfers between devices  16.5 us (21%)
  blocking collectives  14.6 us (19%)
  other arithmetic  8.62 us (11%)
  Pallas kernels  6.79 us (9%)
  local copies, waits for them, and re-layouts  3.31 us (4%)
    ppermute x7, waiting for transfers between devices, shards(): blocks.append(lax.ppermute(block, 'seq', pairs) if step else block)  23.7 us
    ppermute x7, starting transfers between devices, shards(): blocks.append(lax.ppermute(block, 'seq', pairs) if step else block)  14.7 us
    all_to_all x1, blocking collectives, shards(): owned = lax.all_to_all(sent, 'seq', split_axis=0, concat_axis=0, tiled=True)  14.6 us
    concatenate x8, other arithmetic, shards(): jnp.concatenate([lax.dynamic_slice_in_dim(inputs, target * channels, chan...  7.94 us
    pallas_call x1, Pallas kernels, lag_values(): pl.pallas_call(functools.partial(lag_kernel, tiles, channels, rows), out_...  6.79 us
    ppermute x3, waiting for transfers between devices, shards(): lax.ppermute(squares, 'ch', [(place, (place + step) % ways) for place in...  2.8 us
    dynamic_slice x1, local copies, waits for them, and re-layouts, shards(): lax.dynamic_slice_in_dim(out_grads, target * channels, channels, 1)  2.54 us
    ppermute x3, starting transfers between devices, shards(): lax.ppermute(squares, 'ch', [(place, (place + step) % ways) for place in...  1.8 us
  transfers between devices with their start and end apart: 10, of which 6 were waited for; matrix products, arithmetic and copies ran while one was open for 10% of the time, Pallas kernels for 0%

profile of v1, /device:TPU:0, one launch (start us, length us, event | category | flops | bytes accessed | tf_op | source)
XLA Modules:
  0.0 76.6 jit_solution(13027650965211487147)
XLA Ops:
  0.0 2.5 %constant_dynamic-slice_fusion = (f32[256,128]{1,0:T(8,128)}, f32[256,128]{1,0:T(8,128)}, f32[256,128]{1,0:T(8,128)S(1)}, f32[256,128]{1,0:T(8,128)S(1)}, f32[25...) fusion(f32[256,1024]{1,0:T(8,128)} %param.8, ...), kind=kLoop, calls=%fused_computation.13 | loop fusion | bytes 4194336 | tf_op jit(solution)/shard_map/dynamic_slice | solution.py:145
  2.5 0.7 pad_maximum_fusion.6
  3.3 5.0 %collective-permute-start.5 = (f32[256,256]{1,0:T(8,128)}, f32[256,256]{1,0:T(8,128)S(1)}, u32[]{:S(2)}, u32[]{:S(2)}) collective-permute-start(f32[256,256]{1,0:T(8,128)} %pad_maximum_fusion.6), channel_id=1, source_target_pairs={{0,24},{4,28},{8,16},{12,20},{16,8},{20,12},{24,0},{28,4},{1,25},{... | collective-permute-start | bytes 786440 | tf_op jit(solution)/shard_map/ppermute | solution.py:149
  8.3 0.7 pad_maximum_fusion.1
  9.0 1.5 %collective-permute-start = (f32[256,256]{1,0:T(8,128)}, f32[256,256]{1,0:T(8,128)S(1)}, u32[]{:S(2)}, u32[]{:S(2)}) collective-permute-start(f32[256,256]{1,0:T(8,128)} %pad_maximum_fusion.1), channel_id=1, source_target_pairs={{0,4},{4,0},{8,12},{12,8},{16,20},{20,16},{24,28},{28,24},{1,5},{5... | collective-permute-start | bytes 786440 | tf_op jit(solution)/shard_map/ppermute | solution.py:149
  10.5 0.7 pad_maximum_fusion.2
  11.2 0.0 collective-permute-start.1
  11.3 0.0 copy-start.4
  11.3 0.7 pad_maximum_fusion.3
  12.0 2.0 %collective-permute-start.2 = (f32[256,256]{1,0:T(8,128)}, f32[256,256]{1,0:T(8,128)}, u32[]{:S(2)}, u32[]{:S(2)}) collective-permute-start(f32[256,256]{1,0:T(8,128)} %pad_maximum_fusion.3), channel_id=1, source_target_pairs={{0,12},{4,8},{8,4},{12,0},{16,28},{20,24},{24,20},{28,16},{1,13},{... | collective-permute-start | bytes 786440 | tf_op jit(solution)/shard_map/ppermute | solution.py:149
  14.0 0.7 pad_maximum_fusion.4
  14.7 0.0 collective-permute-start.3
  14.7 0.1 stack.35
  14.8 1.7 %pad_maximum_fusion.7 = f32[256,256]{1,0:T(8,128)} fusion(f32[256,128]{1,0:T(8,128)} %get-tuple-element.13, f32[256,128]{1,0:T(8,128)} %get-tuple-element.28), kind=kLoop, calls=%fused_computation.8 | loop fusion | flops 65536 | bytes 524288 | tf_op jit(solution)/shard_map/concatenate | solution.py:142
  16.5 1.7 %pad_maximum_fusion.5 = f32[256,256]{1,0:T(8,128)} fusion(f32[256,128]{1,0:T(8,128)} %get-tuple-element.14, f32[256,128]{1,0:T(8,128)} %get-tuple-element.27), kind=kLoop, calls=%fused_computation.6 | loop fusion | flops 65536 | bytes 524288 | tf_op jit(solution)/shard_map/concatenate | solution.py:142
  18.2 0.0 collective-permute-done.5.refs_6_
  18.2 5.0 %collective-permute-start.4 = (f32[256,256]{1,0:T(8,128)}, f32[256,256]{1,0:T(8,128)}, u32[]{:S(2)}, u32[]{:S(2)}) collective-permute-start(f32[256,256]{1,0:T(8,128)} %pad_maximum_fusion.5), channel_id=1, source_target_pairs={{0,20},{4,16},{8,28},{12,24},{16,4},{20,0},{24,12},{28,8},{1,21},{... | collective-permute-start | bytes 786440 | tf_op jit(solution)/shard_map/ppermute | solution.py:149
  23.3 1.1 %collective-permute-start.6 = (f32[256,256]{1,0:T(8,128)}, f32[256,256]{1,0:T(8,128)}, u32[]{:S(2)}, u32[]{:S(2)}) collective-permute-start(f32[256,256]{1,0:T(8,128)} %pad_maximum_fusion.7), channel_id=1, source_target_pairs={{0,28},{4,24},{8,20},{12,16},{16,12},{20,8},{24,4},{28,0},{1,29},{... | collective-permute-start | bytes 786440 | tf_op jit(solution)/shard_map/ppermute | solution.py:149
  24.4 0.6 gather_fusion
  25.1 0.9 %pad_maximum_fusion.refs_0_ = f32[256,256]{1,0:T(8,128)S(1)} fusion(f32[256,128]{1,0:T(8,128)S(1)} %get-tuple-element.19, f32[256,128]{1,0:T(8,128)} %get-tuple-element.22), kind=kLoop, calls=%fused_computation.1 | loop fusion | flops 65536 | bytes 524288 | tf_op jit(solution)/shard_map/concatenate | solution.py:142
  26.0 1.6 %collective-permute-done.1.refs_2_ = f32[256,256]{1,0:T(8,128)S(1)} collective-permute-done((f32[256,256]{1,0:T(8,128)}, f32[256,256]{1,0:T(8,128)S(1)}, u32[]{:S(2)}, u32[]{:S(2)}) %collective-permute-start.1) | collective-permute-done | bytes 262176 | tf_op jit(solution)/shard_map/ppermute | solution.py:149
  27.6 6.2 %collective-permute-done.2.refs_3_ = f32[256,256]{1,0:T(8,128)} collective-permute-done((f32[256,256]{1,0:T(8,128)}, f32[256,256]{1,0:T(8,128)}, u32[]{:S(2)}, u32[]{:S(2)}) %collective-permute-start.2) | collective-permute-done | bytes 262176 | tf_op jit(solution)/shard_map/ppermute | solution.py:149
  33.8 9.4 %collective-permute-done.3.refs_4_ = f32[256,256]{1,0:T(8,128)} collective-permute-done((f32[256,256]{1,0:T(8,128)}, f32[256,256]{1,0:T(8,128)}, u32[]{:S(2)}, u32[]{:S(2)}) %collective-permute-start.3) | collective-permute-done | bytes 262176 | tf_op jit(solution)/shard_map/ppermute | solution.py:149
  43.2 6.5 %collective-permute-done.4.refs_5_ = f32[256,256]{1,0:T(8,128)} collective-permute-done((f32[256,256]{1,0:T(8,128)}, f32[256,256]{1,0:T(8,128)}, u32[]{:S(2)}, u32[]{:S(2)}) %collective-permute-start.4) | collective-permute-done | bytes 262176 | tf_op jit(solution)/shard_map/ppermute | solution.py:149
  49.8 6.8 %shard_map.73 = f32[8,16,256]{2,1,0:T(8,128)S(1)} custom-call(s32[8]{0:T(128)S(1)} %gather_fusion, s32[8]{0:T(128)S(1)} %copy-done.4, bf16[512,768]{1,0:T(8,128)(2,1)S(1)} %copy-done.2, bf16[1536,512]{1,0:T(8,128)(2,1)S(1)} %copy-done.1, bf16[1024,64]{1,0:T(8,128)(2,1)S(1)} %copy-done.3, f32[256,256]{1,0:T(8,128)S(1)} %pad_maximum_fusion.refs_0_, ...), custom_call_target="tpu_custom_call" | custom-call | flops 805306368 | bytes 2097152 | tf_op jit(solution)/shard_map/pallas_call | solution.py:103
  56.6 14.6 %all_to_all.5 = f32[8,16,256]{2,1,0:T(8,128)S(1)} all-to-all(f32[8,16,256]{2,1,0:T(8,128)S(1)} %shard_map.73), channel_id=1, replica_groups=mesh['seq'=8,'ch'=4] {'seq'}, dimensions={0} | all-to-all | bytes 262144 | tf_op jit(solution)/shard_map/all_to_all | solution.py:154
  71.2 0.0 collective-permute-start.9
  71.3 1.6 %collective-permute-start.8 = (f32[128]{0:T(128)S(1)}, f32[128]{0:T(128)S(1)}, u32[]{:S(2)}, u32[]{:S(2)}) collective-permute-start(f32[128]{0:T(128)S(1)} %slice_reduce_fusion), channel_id=1, source_target_pairs={{0,2},{1,3},{2,0},{3,1},{4,6},{5,7},{6,4},{7,5},{8,10},{9,11},{10,... | collective-permute-start | bytes 1544 | tf_op jit(solution)/shard_map/ppermute | solution.py:159
  72.9 0.2 collective-permute-start.7
  73.0 1.9 %collective-permute-done.8 = f32[128]{0:T(128)S(1)} collective-permute-done((f32[128]{0:T(128)S(1)}, f32[128]{0:T(128)S(1)}, u32[]{:S(2)}, u32[]{:S(2)}) %collective-permute-start.8) | collective-permute-done | bytes 544 | tf_op jit(solution)/shard_map/ppermute | solution.py:159
  74.9 0.9 %collective-permute-done.7 = f32[128]{0:T(128)S(1)} collective-permute-done((f32[128]{0:T(128)S(1)}, f32[128]{0:T(128)S(1)}, u32[]{:S(2)}, u32[]{:S(2)}) %collective-permute-start.7) | collective-permute-done | bytes 544 | tf_op jit(solution)/shard_map/ppermute | solution.py:159
  75.9 0.6 fusion
  (16 shorter events, 0.1 us)
Async XLA Ops:
  0.0 24.4 %copy-start = (s32[8]{0:T(128)S(1)}, s32[8]{0:T(128)}, u32[]{:S(2)}) copy-start(s32[8]{0:T(128)} %param.9) | copy-start | bytes 100
  3.3 14.9 %collective-permute-start.5 = (f32[256,256]{1,0:T(8,128)}, f32[256,256]{1,0:T(8,128)S(1)}, u32[]{:S(2)}, u32[]{:S(2)}) collective-permute-start(f32[256,256]{1,0:T(8,128)} %pad_maximum_fusion.6), channel_id=1, source_target_pairs={{0,24},{4,28},{8,16},{12,20},{16,8},{20,12},{24,0},{28,4},{1,25},{... | collective-permute-start | bytes 786440 | tf_op jit(solution)/shard_map/ppermute | solution.py:149
  9.0 14.2 %collective-permute-start = (f32[256,256]{1,0:T(8,128)}, f32[256,256]{1,0:T(8,128)S(1)}, u32[]{:S(2)}, u32[]{:S(2)}) collective-permute-start(f32[256,256]{1,0:T(8,128)} %pad_maximum_fusion.1), channel_id=1, source_target_pairs={{0,4},{4,0},{8,12},{12,8},{16,20},{20,16},{24,28},{28,24},{1,5},{5... | collective-permute-start | bytes 786440 | tf_op jit(solution)/shard_map/ppermute | solution.py:149
  11.2 16.4 %collective-permute-start.1 = (f32[256,256]{1,0:T(8,128)}, f32[256,256]{1,0:T(8,128)S(1)}, u32[]{:S(2)}, u32[]{:S(2)}) collective-permute-start(f32[256,256]{1,0:T(8,128)} %pad_maximum_fusion.2), channel_id=1, source_target_pairs={{0,8},{4,12},{8,0},{12,4},{16,24},{20,28},{24,16},{28,20},{1,9},{5... | collective-permute-start | bytes 786440 | tf_op jit(solution)/shard_map/ppermute | solution.py:149
  11.2 38.5 %copy-start.1 = (bf16[1536,512]{1,0:T(8,128)(2,1)S(1)}, bf16[1536,512]{1,0:T(8,128)(2,1)}, u32[]{:S(2)}) copy-start(bf16[1536,512]{1,0:T(8,128)(2,1)} %constant.42.clone.inverse_ref) | copy-start | bytes 4718596
  11.2 38.5 %copy-start.2 = (bf16[512,768]{1,0:T(8,128)(2,1)S(1)}, bf16[512,768]{1,0:T(8,128)(2,1)}, u32[]{:S(2)}) copy-start(bf16[512,768]{1,0:T(8,128)(2,1)} %constant.41.clone.forward_ref) | copy-start | bytes 2359300
  11.2 38.5 %copy-start.3 = (bf16[1024,64]{1,0:T(8,128)(2,1)S(1)}, bf16[1024,64]{1,0:T(8,128)(2,1)}, u32[]{:S(2)}) copy-start(bf16[1024,64]{1,0:T(8,128)(2,1)} %constant.43.clone.group_ref) | copy-start | bytes 393220
  11.3 38.5 %copy-start.4 = (s32[8]{0:T(128)S(1)}, s32[8]{0:T(128)}, u32[]{:S(2)}) copy-start(s32[8]{0:T(128)} %lag_ref.1) | copy-start | bytes 100
  12.0 21.8 %collective-permute-start.2 = (f32[256,256]{1,0:T(8,128)}, f32[256,256]{1,0:T(8,128)}, u32[]{:S(2)}, u32[]{:S(2)}) collective-permute-start(f32[256,256]{1,0:T(8,128)} %pad_maximum_fusion.3), channel_id=1, source_target_pairs={{0,12},{4,8},{8,4},{12,0},{16,28},{20,24},{24,20},{28,16},{1,13},{... | collective-permute-start | bytes 786440 | tf_op jit(solution)/shard_map/ppermute | solution.py:149
  14.7 28.5 %collective-permute-start.3 = (f32[256,256]{1,0:T(8,128)}, f32[256,256]{1,0:T(8,128)}, u32[]{:S(2)}, u32[]{:S(2)}) collective-permute-start(f32[256,256]{1,0:T(8,128)} %pad_maximum_fusion.4), channel_id=1, source_target_pairs={{0,16},{4,20},{8,24},{12,28},{16,0},{20,4},{24,8},{28,12},{1,17},{... | collective-permute-start | bytes 786440 | tf_op jit(solution)/shard_map/ppermute | solution.py:149
  18.2 31.5 %collective-permute-start.4 = (f32[256,256]{1,0:T(8,128)}, f32[256,256]{1,0:T(8,128)}, u32[]{:S(2)}, u32[]{:S(2)}) collective-permute-start(f32[256,256]{1,0:T(8,128)} %pad_maximum_fusion.5), channel_id=1, source_target_pairs={{0,20},{4,16},{8,28},{12,24},{16,4},{20,0},{24,12},{28,8},{1,21},{... | collective-permute-start | bytes 786440 | tf_op jit(solution)/shard_map/ppermute | solution.py:149
  23.3 26.5 %collective-permute-start.6 = (f32[256,256]{1,0:T(8,128)}, f32[256,256]{1,0:T(8,128)}, u32[]{:S(2)}, u32[]{:S(2)}) collective-permute-start(f32[256,256]{1,0:T(8,128)} %pad_maximum_fusion.7), channel_id=1, source_target_pairs={{0,28},{4,24},{8,20},{12,16},{16,12},{20,8},{24,4},{28,0},{1,29},{... | collective-permute-start | bytes 786440 | tf_op jit(solution)/shard_map/ppermute | solution.py:149
  71.2 1.8 %collective-permute-start.9 = (f32[128]{0:T(128)S(1)}, f32[128]{0:T(128)S(1)}, u32[]{:S(2)}, u32[]{:S(2)}) collective-permute-start(f32[128]{0:T(128)S(1)} %slice_reduce_fusion), channel_id=1, source_target_pairs={{0,3},{1,0},{2,1},{3,2},{4,7},{5,4},{6,5},{7,6},{8,11},{9,8},{10,9... | collective-permute-start | bytes 1544 | tf_op jit(solution)/shard_map/ppermute | solution.py:159
  71.3 3.6 %collective-permute-start.8 = (f32[128]{0:T(128)S(1)}, f32[128]{0:T(128)S(1)}, u32[]{:S(2)}, u32[]{:S(2)}) collective-permute-start(f32[128]{0:T(128)S(1)} %slice_reduce_fusion), channel_id=1, source_target_pairs={{0,2},{1,3},{2,0},{3,1},{4,6},{5,7},{6,4},{7,5},{8,10},{9,11},{10,... | collective-permute-start | bytes 1544 | tf_op jit(solution)/shard_map/ppermute | solution.py:159
  72.9 3.0 %collective-permute-start.7 = (f32[128]{0:T(128)S(1)}, f32[128]{0:T(128)S(1)}, u32[]{:S(2)}, u32[]{:S(2)}) collective-permute-start(f32[128]{0:T(128)S(1)} %slice_reduce_fusion), channel_id=1, source_target_pairs={{0,1},{1,2},{2,3},{3,0},{4,5},{5,6},{6,7},{7,4},{8,9},{9,10},{10,1... | collective-permute-start | bytes 1544 | tf_op jit(solution)/shard_map/ppermute | solution.py:159

commit v2 on v1

v2 whole, which is shorter than its diff:
```python
import functools
import math

import jax
import jax.numpy as jnp
import ml_dtypes
import numpy as np
from jax import lax
from jax.experimental import pallas as pl
from jax.experimental.pallas import tpu as pltpu
from jax.sharding import PartitionSpec as P

GROUP = 16
target_ratio = 0.5
epsilon = 1e-12


def halves(table):
    high = table.astype(ml_dtypes.bfloat16)
    low = (table - high.astype(np.float64)).astype(ml_dtypes.bfloat16)
    return np.concatenate([high, high, low], axis=0)


def forward_table(rows):
    angles = np.outer(np.arange(rows), 2 * np.arange(rows) + 1) % (4 * rows) * (math.pi / (2 * rows))
    return halves(np.concatenate([np.cos(angles), -np.sin(angles)], axis=1))


def inverse_table(rows):
    angles = np.outer(2 * np.arange(rows) + 1, np.arange(rows)) % (4 * rows) * (math.pi / (2 * rows))
    return halves(np.concatenate([np.cos(angles), np.sin(angles)], axis=0) / rows)


def split(values):
    high = values.astype(jnp.bfloat16)
    low = (values - high.astype(jnp.float32)).astype(jnp.bfloat16)
    return jnp.concatenate([high, low, high], axis=1)


def partner(count, place, step, back=False):
    if count & (count - 1) == 0:
        return place ^ step
    return (place - step if back else place + step) % count


def cut_kernel(count, channels, steps, me_ref, inputs_ref, grads_ref, *refs):
    blocks, (held, in_sems, out_sems) = refs[:-3], refs[-3:]
    arriving, leaving = [], []
    for index, step in enumerate(steps):
        start = pl.multiple_of(partner(count, me_ref[0], step) * channels, channels)
        for half, ref in enumerate((inputs_ref, grads_ref)):
            arriving.append(
                pltpu.make_async_copy(
                    ref.at[:, pl.ds(start, channels)],
                    held.at[index, :, pl.ds(half * channels, channels)],
                    in_sems.at[2 * index + half],
                )
            )
        leaving.append(pltpu.make_async_copy(held.at[index], blocks[index], out_sems.at[index]))
    for copy in arriving:
        copy.start()
    for index, copy in enumerate(leaving):
        arriving[2 * index].wait()
        arriving[2 * index + 1].wait()
        copy.start()
    for copy in leaving:
        copy.wait()


def cut(inputs, out_grads, me, count, steps):
    rows, channels = inputs.shape[0], inputs.shape[1] // count
    if channels % 128:
        blocks = []
        for step in steps:
            start = partner(count, me[0], step) * channels
            pair = [lax.dynamic_slice_in_dim(whole, start, channels, 1) for whole in (inputs, out_grads)]
            blocks.append(jnp.concatenate(pair, axis=1))
        return blocks
    anywhere = pl.BlockSpec(memory_space=pl.ANY)
    return pl.pallas_call(
        functools.partial(cut_kernel, count, channels, steps),
        out_shape=[jax.ShapeDtypeStruct((rows, 2 * channels), jnp.float32) for _ in steps],
        in_specs=[pl.BlockSpec(memory_space=pltpu.SMEM), anywhere, anywhere],
        out_specs=[anywhere for _ in steps],
        scratch_shapes=[
            pltpu.VMEM((len(steps), rows, 2 * channels), jnp.float32),
            pltpu.SemaphoreType.DMA((2 * len(steps),)),
            pltpu.SemaphoreType.DMA((len(steps),)),
        ],
        cost_estimate=pl.CostEstimate(flops=0, bytes_accessed=len(steps) * rows * channels * 16, transcendentals=0),
    )(me, inputs, out_grads)


def absorb_kernel(count, channels, rows, new, olds, last, me_ref, order_ref, lag_ref, forward_ref, *refs):
    refs = list(refs)
    take = lambda many: [refs.pop(0) for _ in range(many)]
    inverse_ref = take(1)[0] if last else None
    blocks, spectra = take(len(new)), take(len(olds))
    carried = take(1)[0] if olds else None
    out_ref = take(1)[0]
    fresh = take(1)[0]
    sums, turned, tile_of = take(3)
    width = turned.shape[2]
    groups = channels // GROUP
    chunk = max(8, groups)

    if carried is None:
        sums[...] = jnp.zeros_like(sums)
    else:
        sums[...] = carried[...]
    for index, step in enumerate(new):
        flipped = blocks[index][...].T
        columns = []
        for part in range(rows // width):
            turned[part] = flipped[:, part * width : (part + 1) * width]
            members = [
                turned[part, pl.ds(half * channels + member, groups, stride=GROUP), :]
                for half in range(2)
                for member in range(GROUP)
            ]
            columns.append(jnp.concatenate(members, axis=0))
        fresh[index] = jnp.dot(
            split(jnp.concatenate(columns, axis=1)), forward_ref[...], preferred_element_type=jnp.float32
        )
    slots = list(new) + [step for old in olds for step in old]
    for index, step in enumerate(slots):
        tile_of[index] = order_ref[partner(count, me_ref[0], step, back=True)]

    def pair(ref, first, new_index, index):
        new_tile, tile = tile_of[new_index], tile_of[first + index]
        later = new_tile > tile
        new_base = jnp.where(later, channels, 0)
        base = jnp.where(later, 0, channels)
        total_real = total_imag = None
        for start in range(0, channels, chunk):
            new_rows = pl.ds(pl.multiple_of(new_base + start, chunk), chunk)
            its_rows = pl.ds(pl.multiple_of(base + start, chunk), chunk)
            new_real, new_imag = fresh[new_index, new_rows, :rows], fresh[new_index, new_rows, rows:]
            real, imag = ref[index, its_rows, :rows], ref[index, its_rows, rows:]
            term_real = new_real * real + new_imag * imag
            term_imag = new_real * imag - new_imag * real
            total_real = term_real if total_real is None else total_real + term_real
            total_imag = term_imag if total_imag is None else total_imag + term_imag
        total_imag = total_imag * jnp.where(later, -1.0, 1.0)
        both = jnp.concatenate([total_real, total_imag], axis=1)
        if chunk > groups:
            both = sum(both[row : row + groups] for row in range(0, chunk, groups))
        offset = jnp.abs(new_tile - tile)
        sums[offset] = sums[offset] + both

    def each_new(new_index, carry):
        def each(ref, first):
            def body(index, carry):
                pair(ref, first, new_index, index)
                return carry

            return body

        lax.fori_loop(0, new_index + 1, each(fresh, 0), 0)
        first = len(new)
        for ref, old in zip(spectra, olds):
            lax.fori_loop(0, len(old), each(ref, first), 0)
            first += len(old)
        return carry

    lax.fori_loop(0, len(new), each_new, 0)
    if not last:
        out_ref[...] = sums[...]
        return
    real = jnp.concatenate([sums[offset, :, :rows] for offset in range(count)], axis=0)
    imag = jnp.concatenate([sums[offset, :, rows:] for offset in range(count)], axis=0)
    sign = 1.0 - 2.0 * (lax.broadcasted_iota(jnp.int32, real.shape, 1) % 2).astype(jnp.float32)
    none = jnp.zeros((groups, rows), jnp.float32)
    next_real = jnp.concatenate([real[groups:], none], axis=0) * sign
    next_imag = jnp.concatenate([imag[groups:], none], axis=0) * sign
    lags = jnp.dot(
        split(jnp.concatenate([real + next_imag, next_real - imag], axis=1)),
        inverse_ref[...],
        preferred_element_type=jnp.float32,
    )
    squares = jnp.broadcast_to(jnp.sum(lags * lags, keepdims=True), (8, rows))
    for offset in range(count):
        sums[offset, :, :rows] = lags[offset * groups : (offset + 1) * groups]
    for place in range(count):
        out_ref[place, :groups, :] = sums[lag_ref[place], :, :rows]
        out_ref[place, groups:, :] = squares


def absorb(blocks, new, spectra, olds, carried, me, tile_order, lag_order, count, last):
    rows, channels = blocks[0].shape[0], blocks[0].shape[1] // 2
    groups = channels // GROUP
    width = math.gcd(rows, 128)
    vmem = pl.BlockSpec(memory_space=pltpu.VMEM)
    smem = pl.BlockSpec(memory_space=pltpu.SMEM)
    tables = [jnp.asarray(forward_table(rows))] + ([jnp.asarray(inverse_table(rows))] if last else [])
    operands = tables + list(blocks) + list(spectra) + ([carried] if olds else [])
    out = (count, groups + 8, rows) if last else (count, groups, 2 * rows)
    fresh = jax.ShapeDtypeStruct((len(new), 2 * channels, 2 * rows), jnp.float32)
    result = pl.pallas_call(
        functools.partial(absorb_kernel, count, channels, rows, new, olds, last),
        out_shape=[jax.ShapeDtypeStruct(out, jnp.float32)] + ([] if last else [fresh]),
        in_specs=[smem, smem, smem] + [vmem] * len(operands),
        out_specs=[vmem] + ([] if last else [vmem]),
        scratch_shapes=([pltpu.VMEM(fresh.shape, jnp.float32)] if last else [])
        + [
            pltpu.VMEM((count, groups, 2 * rows), jnp.float32),
            pltpu.VMEM((rows // width, 2 * channels, width), jnp.float32),
            pltpu.SMEM((count,), jnp.int32),
        ],
        compiler_params=pltpu.CompilerParams(vmem_limit_bytes=20 * 2**20),
        cost_estimate=pl.CostEstimate(
            flops=24 * len(new) * rows * rows * channels, bytes_accessed=len(new) * rows * channels * 24, transcendentals=0
        ),
    )(me, tile_order, lag_order, *operands)
    return result[0] if last else result


def shards(inputs, out_grads, tile_order, lag_order):
    count = lax.axis_size("seq")
    rows = inputs.shape[0]
    channels = inputs.shape[1] // count
    groups = channels // GROUP
    me = lax.axis_index("seq").reshape(1)
    half = max(1, count // 2)
    far, near = list(range(count - 1, half - 1, -1)), list(range(half))
    blocks = dict(zip(far + near, cut(inputs, out_grads, me, count, far + near)))
    for step in far + near[1:]:
        pairs = [(place, partner(count, place, step)) for place in range(count)]
        blocks[step] = lax.ppermute(blocks[step], "seq", pairs)
    batch = max(1, len(far) // 4)
    later = far[:-batch]
    arrivals = [near[first : first + batch] + later[first : first + batch] for first in range(0, len(later), batch)]
    arrivals = [near[:batch] + far[:batch], near[batch:2*batch] + far[batch:2*batch], near[2*batch:] + far[2*batch:-batch], far[-batch:]]
    spectra, olds, carried = [], [], None
    for new in arrivals:
        last = new is arrivals[-1]
        made = absorb(
            [blocks[step] for step in new], new, spectra, list(olds), carried, me, tile_order, lag_order, count, last
        )
        if not last:
            carried, fresh = made
            spectra.append(fresh)
            olds.append(new)
    owned = lax.all_to_all(made, "seq", split_axis=0, concat_axis=0, tiled=True)
    squares = jnp.sum(owned[:, groups, :128], axis=0)
    ways = lax.axis_size("ch")
    total = squares
    for step in range(1, ways):
        total = total + lax.ppermute(squares, "ch", [(place, (place + step) % ways) for place in range(ways)])
    lags = owned[:, :groups, :].reshape(count * groups, rows)
    entries = ways * count * groups * count * rows
    factor = target_ratio * math.sqrt(entries) / jnp.sqrt(total[:1] + epsilon)
    return lags * factor


def solution(mesh):
    return jax.shard_map(
        shards,
        mesh=mesh,
        in_specs=(P("seq", "ch"), P("seq", "ch"), P(), P()),
        out_specs=P("ch", "seq"),
        check_vma=False,
    )
```

time: 76.8 us -> 72.2 us (0.940)
  starting transfers between devices: 16.5 us -> 24.7 us
  other arithmetic: 8.62 us -> 0.67 us
  blocking collectives: 14.6 us -> 10.9 us
  Pallas kernels: 6.79 us -> 10.4 us
  waiting for transfers between devices: 26.5 us -> 24 us
  local copies, waits for them, and re-layouts: 3.31 us -> 0.96 us
    ppermute x7, starting transfers between devices: 14.7 us -> 22.9 us  [shards(): blocks[step] = lax.ppermute(blocks[step], 'seq', pairs)]
    concatenate x8 -> x0, other arithmetic: 7.94 us -> none  [shards(): jnp.concatenate([lax.dynamic_slice_in_dim(inputs, target * channels, chan...]
    all_to_all x1, blocking collectives: 14.6 us -> 10.9 us  [shards(): owned = lax.all_to_all(made, 'seq', split_axis=0, concat_axis=0, tiled=True)]
    pallas_call x1 -> x5, Pallas kernels: 6.79 us -> 10.4 us  [the longest x4 7.78 us: absorb(): pl.pallas_call(functools.partial(absorb_kernel, count, channels, rows, ne...]
    dynamic_slice x1 -> x0, local copies, waits for them, and re-layouts: 2.54 us -> none  [shards(): lax.dynamic_slice_in_dim(out_grads, target * channels, channels, 1)]
    ppermute x7, waiting for transfers between devices: 23.7 us -> 21.2 us  [shards(): blocks[step] = lax.ppermute(blocks[step], 'seq', pairs)]
    unnamed x10, local copies, waits for them, and re-layouts: 0.02 us -> 0.96 us
  transfers between devices with their start and end apart: 10 -> 10, of which waited for: 6 -> 5; matrix products, arithmetic and copies ran while one was open for 10% -> 0% of each run, Pallas kernels for 0% -> 8%
where the time goes in v2:
time: 72.2 us; the launch traced here: 72 us
  starting transfers between devices  24.7 us (34%)
  waiting for transfers between devices  24 us (33%)
  blocking collectives  10.9 us (15%)
  Pallas kernels  10.4 us (14%)
  local copies, waits for them, and re-layouts  0.96 us (1%)
    ppermute x7, starting transfers between devices, shards(): blocks[step] = lax.ppermute(blocks[step], 'seq', pairs)  22.9 us
    ppermute x7, waiting for transfers between devices, shards(): blocks[step] = lax.ppermute(blocks[step], 'seq', pairs)  21.2 us
    all_to_all x1, blocking collectives, shards(): owned = lax.all_to_all(made, 'seq', split_axis=0, concat_axis=0, tiled=True)  10.9 us
    pallas_call x4, Pallas kernels, absorb(): pl.pallas_call(functools.partial(absorb_kernel, count, channels, rows, ne...  7.78 us
    ppermute x3, waiting for transfers between devices, shards(): lax.ppermute(squares, 'ch', [(place, (place + step) % ways) for place in...  2.8 us
    pallas_call x1, Pallas kernels, cut(): pl.pallas_call(functools.partial(cut_kernel, count, channels, steps), out...  2.66 us
    ppermute x3, starting transfers between devices, shards(): lax.ppermute(squares, 'ch', [(place, (place + step) % ways) for place in...  1.8 us
  transfers between devices with their start and end apart: 10, of which 5 were waited for; matrix products, arithmetic and copies ran while one was open for 0% of the time, Pallas kernels for 8%

profile of v2, /device:TPU:0, one launch (start us, length us, event | category | flops | bytes accessed | tf_op | source)
XLA Modules:
  0.0 72.0 jit_solution(1619699924438087093)
XLA Ops:
  0.0 2.7 %shard_map.91 = (f32[256,256]{1,0:T(8,128)}, f32[256,256]{1,0:T(8,128)}, f32[256,256]{1,0:T(8,128)}, f32[256,256]{1,0:T(8,128)}, f32[256,256]{1,0:T(8,128)}, /*i...) custom-call(s32[1]{0:T(128)} %bitcast.me_ref, f32[256,1024]{1,0:T(8,128)} %inputs_ref.1, f32[256,1024]{1,0:T(8,128)} %grads_ref.1), custom_call_target="tpu_custom_call" | custom-call | bytes 4194304 | tf_op jit(solution)/shard_map/pallas_call | solution.py:80
  2.7 6.1 %collective-permute-start.1 = (f32[256,256]{1,0:T(8,128)}, f32[256,256]{1,0:T(8,128)S(1)}, u32[]{:S(2)}, u32[]{:S(2)}) collective-permute-start(f32[256,256]{1,0:T(8,128)} %get-tuple-element.21), channel_id=1, source_target_pairs={{0,28},{4,24},{8,20},{12,16},{16,12},{20,8},{24,4},{28,0},{1,29},{... | collective-permute-start | bytes 786440 | tf_op jit(solution)/shard_map/ppermute | solution.py:229
  8.7 0.5 collective-permute-start.2
  9.3 0.1 collective-permute-start.3
  9.4 0.0 collective-permute-start.4
  9.4 3.1 %collective-permute-start.5 = (f32[256,256]{1,0:T(8,128)}, f32[256,256]{1,0:T(8,128)S(1)}, u32[]{:S(2)}, u32[]{:S(2)}) collective-permute-start(f32[256,256]{1,0:T(8,128)} %get-tuple-element.28), channel_id=1, source_target_pairs={{0,12},{4,8},{8,4},{12,0},{16,28},{20,24},{24,20},{28,16},{1,13},{... | collective-permute-start | bytes 786440 | tf_op jit(solution)/shard_map/ppermute | solution.py:229
  12.4 3.8 %collective-permute-done.1.refs_1_ = f32[256,256]{1,0:T(8,128)S(1)} collective-permute-done((f32[256,256]{1,0:T(8,128)}, f32[256,256]{1,0:T(8,128)S(1)}, u32[]{:S(2)}, u32[]{:S(2)}) %collective-permute-start.1) | collective-permute-done | bytes 262176 | tf_op jit(solution)/shard_map/ppermute | solution.py:229
  16.3 13.2 %collective-permute-start.6 = (f32[256,256]{1,0:T(8,128)}, f32[256,256]{1,0:T(8,128)S(1)}, u32[]{:S(2)}, u32[]{:S(2)}) collective-permute-start(f32[256,256]{1,0:T(8,128)} %get-tuple-element.29), channel_id=1, source_target_pairs={{0,20},{4,16},{8,28},{12,24},{16,4},{20,0},{24,12},{28,8},{1,21},{... | collective-permute-start | bytes 786440 | tf_op jit(solution)/shard_map/ppermute | solution.py:229
  29.4 0.0 collective-permute-done.2.refs_0_
  29.4 0.0 collective-permute-start
  29.4 0.0 copy-done
  29.5 0.0 copy-done.3
  29.5 0.0 copy-done.2
  29.5 0.0 copy-start.4
  29.5 0.9 %copy-done.4 = f32[256,256]{1,0:T(8,128)S(1)} copy-done((f32[256,256]{1,0:T(8,128)S(1)}, f32[256,256]{1,0:T(8,128)}, u32[]{:S(2)}) %copy-start.4) | copy-done | bytes 262168
  30.4 1.5 %shard_map.92 = (f32[8,8,512]{2,1,0:T(8,128)S(1)}, f32[2,256,512]{2,1,0:T(8,128)S(1)}) custom-call(s32[1]{0:T(128)} %bitcast.me_ref, s32[8]{0:T(128)S(1)} %copy-done.2, s32[8]{0:T(128)S(1)} %copy-done.3, bf16[768,512]{1,0:T(8,128)(2,1)S(1)} %copy-done, f32[256,256]{1,0:T(8,128)S(1)} %copy-done.4, f32[256,256]{1,0:T(8,128)S(1)} %collective-permute-done.1.refs_1_), custom_call_target="tpu_custom_call" | custom-call | flops 402653184 | bytes 1572864 | tf_op jit(solution)/shard_map/pallas_call | solution.py:199
  31.9 0.0 collective-permute-done.3.refs_1_
  31.9 1.7 %shard_map.93 = (f32[8,8,512]{2,1,0:T(8,128)S(1)}, f32[2,256,512]{2,1,0:T(8,128)S(1)}) custom-call(s32[1]{0:T(128)} %bitcast.me_ref, s32[8]{0:T(128)S(1)} %copy-done.2, s32[8]{0:T(128)S(1)} %copy-done.3, bf16[768,512]{1,0:T(8,128)(2,1)S(1)} %copy-done, f32[256,256]{1,0:T(8,128)S(1)} %collective-permute-done.2.refs_0_, ...), custom_call_target="tpu_custom_call" | custom-call | flops 402653184 | bytes 1572864 | tf_op jit(solution)/shard_map/pallas_call | solution.py:199
  33.7 0.0 collective-permute-done.4.refs_0_
  33.7 0.0 collective-permute-done.5.refs_1_
  33.7 15.4 %collective-permute-done.6.refs_2_ = f32[256,256]{1,0:T(8,128)S(1)} collective-permute-done((f32[256,256]{1,0:T(8,128)}, f32[256,256]{1,0:T(8,128)S(1)}, u32[]{:S(2)}, u32[]{:S(2)}) %collective-permute-start.6) | collective-permute-done | bytes 262176 | tf_op jit(solution)/shard_map/ppermute | solution.py:229
  49.1 2.7 %shard_map.94 = (f32[8,8,512]{2,1,0:T(8,128)S(1)}, f32[3,256,512]{2,1,0:T(8,128)S(1)}) custom-call(s32[1]{0:T(128)} %bitcast.me_ref, s32[8]{0:T(128)S(1)} %copy-done.2, s32[8]{0:T(128)S(1)} %copy-done.3, bf16[768,512]{1,0:T(8,128)(2,1)S(1)} %copy-done, f32[256,256]{1,0:T(8,128)S(1)} %collective-permute-done.4.refs_0_, ...), custom_call_target="tpu_custom_call" | custom-call | flops 603979776 | bytes 2359296 | tf_op jit(solution)/shard_map/pallas_call | solution.py:199
  51.7 2.0 %collective-permute-done.refs_1_ = f32[256,256]{1,0:T(8,128)S(1)} collective-permute-done((f32[256,256]{1,0:T(8,128)}, f32[256,256]{1,0:T(8,128)S(1)}, u32[]{:S(2)}, u32[]{:S(2)}) %collective-permute-start) | collective-permute-done | bytes 262176 | tf_op jit(solution)/shard_map/ppermute | solution.py:229
  53.7 1.9 %shard_map.95 = f32[8,16,256]{2,1,0:T(8,128)S(1)} custom-call(s32[1]{0:T(128)} %bitcast.me_ref, s32[8]{0:T(128)S(1)} %copy-done.2, s32[8]{0:T(128)S(1)} %copy-done.3, bf16[768,512]{1,0:T(8,128)(2,1)S(1)} %copy-done, bf16[1536,256]{1,0:T(8,128)(2,1)S(1)} %copy-done.1, f32[256,256]{1,0:T(8,128)S(1)} %collective-permute-done.refs_1_, ...), custom_call_target="tpu_custom_call" | custom-call | flops 201326592 | bytes 786432 | tf_op jit(solution)/shard_map/pallas_call | solution.py:199
  55.7 10.9 %all_to_all.5 = f32[8,16,256]{2,1,0:T(8,128)S(1)} all-to-all(f32[8,16,256]{2,1,0:T(8,128)S(1)} %shard_map.95), channel_id=1, replica_groups=mesh['seq'=8,'ch'=4] {'seq'}, dimensions={0} | all-to-all | bytes 262144 | tf_op jit(solution)/shard_map/all_to_all | solution.py:244
  66.6 0.0 collective-permute-start.9
  66.7 1.6 %collective-permute-start.8 = (f32[128]{0:T(128)S(1)}, f32[128]{0:T(128)S(1)}, u32[]{:S(2)}, u32[]{:S(2)}) collective-permute-start(f32[128]{0:T(128)S(1)} %slice_reduce_fusion), channel_id=1, source_target_pairs={{0,2},{1,3},{2,0},{3,1},{4,6},{5,7},{6,4},{7,5},{8,10},{9,11},{10,... | collective-permute-start | bytes 1544 | tf_op jit(solution)/shard_map/ppermute | solution.py:249
  68.3 0.2 collective-permute-start.7
  68.4 0.0 collective-permute-done.9
  68.4 1.9 %collective-permute-done.8 = f32[128]{0:T(128)S(1)} collective-permute-done((f32[128]{0:T(128)S(1)}, f32[128]{0:T(128)S(1)}, u32[]{:S(2)}, u32[]{:S(2)}) %collective-permute-start.8) | collective-permute-done | bytes 544 | tf_op jit(solution)/shard_map/ppermute | solution.py:249
  70.3 0.9 %collective-permute-done.7 = f32[128]{0:T(128)S(1)} collective-permute-done((f32[128]{0:T(128)S(1)}, f32[128]{0:T(128)S(1)}, u32[]{:S(2)}, u32[]{:S(2)}) %collective-permute-start.7) | collective-permute-done | bytes 544 | tf_op jit(solution)/shard_map/ppermute | solution.py:249
  71.3 0.6 fusion
  (7 shorter events, 0.0 us)
Async XLA Ops:
  0.0 29.4 %copy-start = (bf16[768,512]{1,0:T(8,128)(2,1)S(1)}, bf16[768,512]{1,0:T(8,128)(2,1)}, u32[]{:S(2)}) copy-start(bf16[768,512]{1,0:T(8,128)(2,1)} %constant.16.clone.forward_ref) | copy-start | bytes 2359300
  0.0 29.4 %copy-start.3 = (s32[8]{0:T(128)S(1)}, s32[8]{0:T(128)}, u32[]{:S(2)}) copy-start(s32[8]{0:T(128)} %lag_ref.7) | copy-start | bytes 100
  0.0 29.5 %copy-start.2 = (s32[8]{0:T(128)S(1)}, s32[8]{0:T(128)}, u32[]{:S(2)}) copy-start(s32[8]{0:T(128)} %order_ref.7) | copy-start | bytes 100
  2.7 13.6 %collective-permute-start.1 = (f32[256,256]{1,0:T(8,128)}, f32[256,256]{1,0:T(8,128)S(1)}, u32[]{:S(2)}, u32[]{:S(2)}) collective-permute-start(f32[256,256]{1,0:T(8,128)} %get-tuple-element.21), channel_id=1, source_target_pairs={{0,28},{4,24},{8,20},{12,16},{16,12},{20,8},{24,4},{28,0},{1,29},{... | collective-permute-start | bytes 786440 | tf_op jit(solution)/shard_map/ppermute | solution.py:229
  8.7 20.7 %collective-permute-start.2 = (f32[256,256]{1,0:T(8,128)}, f32[256,256]{1,0:T(8,128)S(1)}, u32[]{:S(2)}, u32[]{:S(2)}) collective-permute-start(f32[256,256]{1,0:T(8,128)} %get-tuple-element.23), channel_id=1, source_target_pairs={{0,4},{4,0},{8,12},{12,8},{16,20},{20,16},{24,28},{28,24},{1,5},{5... | collective-permute-start | bytes 786440 | tf_op jit(solution)/shard_map/ppermute | solution.py:229
  9.3 22.6 %collective-permute-start.3 = (f32[256,256]{1,0:T(8,128)}, f32[256,256]{1,0:T(8,128)S(1)}, u32[]{:S(2)}, u32[]{:S(2)}) collective-permute-start(f32[256,256]{1,0:T(8,128)} %get-tuple-element.24), channel_id=1, source_target_pairs={{0,24},{4,28},{8,16},{12,20},{16,8},{20,12},{24,0},{28,4},{1,25},{... | collective-permute-start | bytes 786440 | tf_op jit(solution)/shard_map/ppermute | solution.py:229
  9.4 24.3 %collective-permute-start.4 = (f32[256,256]{1,0:T(8,128)}, f32[256,256]{1,0:T(8,128)S(1)}, u32[]{:S(2)}, u32[]{:S(2)}) collective-permute-start(f32[256,256]{1,0:T(8,128)} %get-tuple-element.27), channel_id=1, source_target_pairs={{0,8},{4,12},{8,0},{12,4},{16,24},{20,28},{24,16},{28,20},{1,9},{5... | collective-permute-start | bytes 786440 | tf_op jit(solution)/shard_map/ppermute | solution.py:229
  9.4 24.3 %collective-permute-start.5 = (f32[256,256]{1,0:T(8,128)}, f32[256,256]{1,0:T(8,128)S(1)}, u32[]{:S(2)}, u32[]{:S(2)}) collective-permute-start(f32[256,256]{1,0:T(8,128)} %get-tuple-element.28), channel_id=1, source_target_pairs={{0,12},{4,8},{8,4},{12,0},{16,28},{20,24},{24,20},{28,16},{1,13},{... | collective-permute-start | bytes 786440 | tf_op jit(solution)/shard_map/ppermute | solution.py:229
  16.3 32.8 %collective-permute-start.6 = (f32[256,256]{1,0:T(8,128)}, f32[256,256]{1,0:T(8,128)S(1)}, u32[]{:S(2)}, u32[]{:S(2)}) collective-permute-start(f32[256,256]{1,0:T(8,128)} %get-tuple-element.29), channel_id=1, source_target_pairs={{0,20},{4,16},{8,28},{12,24},{16,4},{20,0},{24,12},{28,8},{1,21},{... | collective-permute-start | bytes 786440 | tf_op jit(solution)/shard_map/ppermute | solution.py:229
  29.4 24.3 %collective-permute-start = (f32[256,256]{1,0:T(8,128)}, f32[256,256]{1,0:T(8,128)S(1)}, u32[]{:S(2)}, u32[]{:S(2)}) collective-permute-start(f32[256,256]{1,0:T(8,128)} %get-tuple-element.19), channel_id=1, source_target_pairs={{0,16},{4,20},{8,24},{12,28},{16,0},{20,4},{24,8},{28,12},{1,17},{... | collective-permute-start | bytes 786440 | tf_op jit(solution)/shard_map/ppermute | solution.py:229
  29.5 1.0 %copy-start.4 = (f32[256,256]{1,0:T(8,128)S(1)}, f32[256,256]{1,0:T(8,128)}, u32[]{:S(2)}) copy-start(f32[256,256]{1,0:T(8,128)} %get-tuple-element.20.refs_0_) | copy-start | bytes 786436
  49.1 4.7 %copy-start.1 = (bf16[1536,256]{1,0:T(8,128)(2,1)S(1)}, bf16[1536,256]{1,0:T(8,128)(2,1)}, u32[]{:S(2)}) copy-start(bf16[1536,256]{1,0:T(8,128)(2,1)} %constant.17.clone.refs_0_) | copy-start | bytes 2359300
  66.6 1.8 %collective-permute-start.9 = (f32[128]{0:T(128)S(1)}, f32[128]{0:T(128)S(1)}, u32[]{:S(2)}, u32[]{:S(2)}) collective-permute-start(f32[128]{0:T(128)S(1)} %slice_reduce_fusion), channel_id=1, source_target_pairs={{0,3},{1,0},{2,1},{3,2},{4,7},{5,4},{6,5},{7,6},{8,11},{9,8},{10,9... | collective-permute-start | bytes 1544 | tf_op jit(solution)/shard_map/ppermute | solution.py:249
  66.7 3.6 %collective-permute-start.8 = (f32[128]{0:T(128)S(1)}, f32[128]{0:T(128)S(1)}, u32[]{:S(2)}, u32[]{:S(2)}) collective-permute-start(f32[128]{0:T(128)S(1)} %slice_reduce_fusion), channel_id=1, source_target_pairs={{0,2},{1,3},{2,0},{3,1},{4,6},{5,7},{6,4},{7,5},{8,10},{9,11},{10,... | collective-permute-start | bytes 1544 | tf_op jit(solution)/shard_map/ppermute | solution.py:249
  68.3 3.0 %collective-permute-start.7 = (f32[128]{0:T(128)S(1)}, f32[128]{0:T(128)S(1)}, u32[]{:S(2)}, u32[]{:S(2)}) collective-permute-start(f32[128]{0:T(128)S(1)} %slice_reduce_fusion), channel_id=1, source_target_pairs={{0,1},{1,2},{2,3},{3,0},{4,5},{5,6},{6,7},{7,4},{8,9},{9,10},{10,1... | collective-permute-start | bytes 1544 | tf_op jit(solution)/shard_map/ppermute | solution.py:249

commit v3 on v2

--- a/solution.py
+++ b/solution.py
@@ -44,26 +44,21 @@
 
 
 def cut_kernel(count, channels, steps, me_ref, inputs_ref, grads_ref, *refs):
-    blocks, (held, in_sems, out_sems) = refs[:-3], refs[-3:]
-    arriving, leaving = [], []
+    blocks, sems = refs[:-1], refs[-1]
+    copies = []
     for index, step in enumerate(steps):
         start = pl.multiple_of(partner(count, me_ref[0], step) * channels, channels)
         for half, ref in enumerate((inputs_ref, grads_ref)):
-            arriving.append(
+            copies.append(
                 pltpu.make_async_copy(
                     ref.at[:, pl.ds(start, channels)],
-                    held.at[index, :, pl.ds(half * channels, channels)],
-                    in_sems.at[2 * index + half],
+                    blocks[index].at[:, pl.ds(half * channels, channels)],
+                    sems.at[2 * index + half],
                 )
             )
-        leaving.append(pltpu.make_async_copy(held.at[index], blocks[index], out_sems.at[index]))
-    for copy in arriving:
+    for copy in copies:
         copy.start()
-    for index, copy in enumerate(leaving):
-        arriving[2 * index].wait()
-        arriving[2 * index + 1].wait()
-        copy.start()
-    for copy in leaving:
+    for copy in copies:
         copy.wait()
 
 
@@ -79,14 +74,10 @@
     anywhere = pl.BlockSpec(memory_space=pl.ANY)
     return pl.pallas_call(
         functools.partial(cut_kernel, count, channels, steps),
-        out_shape=[jax.ShapeDtypeStruct((rows, 2 * channels), jnp.float32) for _ in steps],
+        out_shape=[pltpu.VMEM((rows, 2 * channels), jnp.float32) for _ in steps],
         in_specs=[pl.BlockSpec(memory_space=pltpu.SMEM), anywhere, anywhere],
-        out_specs=[anywhere for _ in steps],
-        scratch_shapes=[
-            pltpu.VMEM((len(steps), rows, 2 * channels), jnp.float32),
-            pltpu.SemaphoreType.DMA((2 * len(steps),)),
-            pltpu.SemaphoreType.DMA((len(steps),)),
-        ],
+        out_specs=[pl.BlockSpec(memory_space=pltpu.VMEM) for _ in steps],
+        scratch_shapes=[pltpu.SemaphoreType.DMA((2 * len(steps),))],
         cost_estimate=pl.CostEstimate(flops=0, bytes_accessed=len(steps) * rows * channels * 16, transcendentals=0),
     )(me, inputs, out_grads)
 
@@ -223,14 +214,18 @@
     me = lax.axis_index("seq").reshape(1)
     half = max(1, count // 2)
     far, near = list(range(count - 1, half - 1, -1)), list(range(half))
-    blocks = dict(zip(far + near, cut(inputs, out_grads, me, count, far + near)))
+    first = cut(inputs, out_grads, me, count, far[:1])
+    then, first = lax.optimization_barrier((me, first))
+    blocks = dict(zip(far + near, first + cut(inputs, out_grads, then, count, far[1:] + near)))
     for step in far + near[1:]:
         pairs = [(place, partner(count, place, step)) for place in range(count)]
         blocks[step] = lax.ppermute(blocks[step], "seq", pairs)
-    batch = max(1, len(far) // 4)
-    later = far[:-batch]
-    arrivals = [near[first : first + batch] + later[first : first + batch] for first in range(0, len(later), batch)]
-    arrivals = [near[:batch] + far[:batch], near[batch:2*batch] + far[batch:2*batch], near[2*batch:] + far[2*batch:-batch], far[-batch:]]
+    batch = max(1, count // 8)
+    arrivals = [near[:batch] + far[:batch]]
+    arrivals.append(near[batch : 2 * batch] + far[batch : 2 * batch])
+    arrivals.append(near[2 * batch :])
+    arrivals.append(far[2 * batch : -batch])
+    arrivals.append(far[-batch:])
     spectra, olds, carried = [], [], None
     for new in arrivals:
         last = new is arrivals[-1]

time: 72.2 us -> 70.2 us (0.972)
  waiting for transfers between devices: 24 us -> 21.1 us
    ppermute x7, waiting for transfers between devices: 21.2 us -> 18.3 us  [shards(): blocks[step] = lax.ppermute(blocks[step], 'seq', pairs)]
    pallas_call x4 -> x5, Pallas kernels: 7.78 us -> 8.47 us  [absorb(): pl.pallas_call(functools.partial(absorb_kernel, count, channels, rows, ne...]
    pallas_call x1 -> x2, Pallas kernels: 2.66 us -> 2.65 us  [cut(): pl.pallas_call(functools.partial(cut_kernel, count, channels, steps), out...]
  transfers between devices with their start and end apart: 10 -> 10, of which waited for: 5 -> 5; matrix products, arithmetic and copies ran while one was open for 0% -> 0% of each run, Pallas kernels for 8% -> 12%
where the time goes in v3:
time: 70.2 us; the launch traced here: 70 us
  starting transfers between devices  25.3 us (36%)
  waiting for transfers between devices  21.1 us (30%)
  Pallas kernels  11.1 us (16%)
  blocking collectives  10.9 us (16%)
    ppermute x7, starting transfers between devices, shards(): blocks[step] = lax.ppermute(blocks[step], 'seq', pairs)  23.6 us
    ppermute x7, waiting for transfers between devices, shards(): blocks[step] = lax.ppermute(blocks[step], 'seq', pairs)  18.3 us
    all_to_all x1, blocking collectives, shards(): owned = lax.all_to_all(made, 'seq', split_axis=0, concat_axis=0, tiled=True)  10.9 us
    pallas_call x5, Pallas kernels, absorb(): pl.pallas_call(functools.partial(absorb_kernel, count, channels, rows, ne...  8.47 us
    ppermute x3, waiting for transfers between devices, shards(): lax.ppermute(squares, 'ch', [(place, (place + step) % ways) for place in...  2.8 us
    pallas_call x2, Pallas kernels, cut(): pl.pallas_call(functools.partial(cut_kernel, count, channels, steps), out...  2.65 us
    ppermute x3, starting transfers between devices, shards(): lax.ppermute(squares, 'ch', [(place, (place + step) % ways) for place in...  1.8 us
  transfers between devices with their start and end apart: 10, of which 5 were waited for; matrix products, arithmetic and copies ran while one was open for 0% of the time, Pallas kernels for 12%

profile of v3, /device:TPU:0, one launch (start us, length us, event | category | flops | bytes accessed | tf_op | source)
XLA Modules:
  0.0 70.0 jit_solution(2193485038257451884)
XLA Ops:
  0.0 1.0 %shard_map.100 = f32[256,256]{1,0:T(8,128)S(1)} custom-call(s32[1]{0:T(128)} %bitcast.me_ref, f32[256,1024]{1,0:T(8,128)} %inputs_ref.3, f32[256,1024]{1,0:T(8,128)} %grads_ref.3), custom_call_target="tpu_custom_call" | custom-call | bytes 524288 | tf_op jit(solution)/shard_map/pallas_call | solution.py:75
  1.0 0.0 copy-start
  1.0 6.0 %collective-permute-start.1 = (f32[256,256]{1,0:T(8,128)S(1)}, f32[256,256]{1,0:T(8,128)S(1)}, u32[]{:S(2)}, u32[]{:S(2)}) collective-permute-start(f32[256,256]{1,0:T(8,128)S(1)} %shard_map.100), channel_id=1, source_target_pairs={{0,28},{4,24},{8,20},{12,16},{16,12},{20,8},{24,4},{28,0},{1,29},{... | collective-permute-start | bytes 786440 | tf_op jit(solution)/shard_map/ppermute | solution.py:222
  7.0 1.7 %shard_map.101 = (f32[256,256]{1,0:T(8,128)S(1)}, f32[256,256]{1,0:T(8,128)S(1)}, f32[256,256]{1,0:T(8,128)S(1)}, f32[256,256]{1,0:T(8,128)S(1)}, f32[256,256]{1...) custom-call(s32[1]{0:T(128)} %bitcast.me_ref, f32[256,1024]{1,0:T(8,128)} %inputs_ref.3, ...), custom_call_target="tpu_custom_call" | custom-call | bytes 3670016 | tf_op jit(solution)/shard_map/pallas_call | solution.py:75
  8.7 0.6 collective-permute-start.2
  9.3 0.1 collective-permute-start.3
  9.4 0.0 collective-permute-start.4
  9.4 3.1 %collective-permute-start.5 = (f32[256,256]{1,0:T(8,128)S(1)}, f32[256,256]{1,0:T(8,128)S(1)}, u32[]{:S(2)}, u32[]{:S(2)}) collective-permute-start(f32[256,256]{1,0:T(8,128)S(1)} %get-tuple-element.32), channel_id=1, source_target_pairs={{0,12},{4,8},{8,4},{12,0},{16,28},{20,24},{24,20},{28,16},{1,13},{... | collective-permute-start | bytes 786440 | tf_op jit(solution)/shard_map/ppermute | solution.py:222
  12.5 1.3 %collective-permute-done.1.refs_1_ = f32[256,256]{1,0:T(8,128)S(1)} collective-permute-done((f32[256,256]{1,0:T(8,128)S(1)}, f32[256,256]{1,0:T(8,128)S(1)}, u32[]{:S(2)}, u32[]{:S(2)}) %collective-permute-start.1) | collective-permute-done | bytes 262176 | tf_op jit(solution)/shard_map/ppermute | solution.py:222
  13.8 13.7 %collective-permute-start.6 = (f32[256,256]{1,0:T(8,128)S(1)}, f32[256,256]{1,0:T(8,128)S(1)}, u32[]{:S(2)}, u32[]{:S(2)}) collective-permute-start(f32[256,256]{1,0:T(8,128)S(1)} %get-tuple-element.35), channel_id=1, source_target_pairs={{0,20},{4,16},{8,28},{12,24},{16,4},{20,0},{24,12},{28,8},{1,21},{... | collective-permute-start | bytes 786440 | tf_op jit(solution)/shard_map/ppermute | solution.py:222
  27.5 0.0 collective-permute-done.2.refs_0_
  27.5 0.0 collective-permute-start
  27.6 0.6 copy-done.2
  28.2 0.0 copy-done.3
  28.2 1.5 %shard_map.102 = (f32[8,8,512]{2,1,0:T(8,128)S(1)}, f32[2,256,512]{2,1,0:T(8,128)S(1)}) custom-call(s32[1]{0:T(128)} %bitcast.me_ref, s32[8]{0:T(128)S(1)} %copy-done.2, s32[8]{0:T(128)S(1)} %copy-done.3, bf16[768,512]{1,0:T(8,128)(2,1)S(1)} %copy-done, f32[256,256]{1,0:T(8,128)S(1)} %get-tuple-element.24.refs_0_, f32[256,256]{1,0:T(8,128)S(1)} %collective-permute-done.1.refs_1_), custom_call_target="tpu_custom_call" | custom-call | flops 402653184 | bytes 1572864 | tf_op jit(solution)/shard_map/pallas_call | solution.py:190
  29.7 0.0 collective-permute-done.3.refs_1_
  29.7 1.7 %shard_map.103 = (f32[8,8,512]{2,1,0:T(8,128)S(1)}, f32[2,256,512]{2,1,0:T(8,128)S(1)}) custom-call(s32[1]{0:T(128)} %bitcast.me_ref, s32[8]{0:T(128)S(1)} %copy-done.2, s32[8]{0:T(128)S(1)} %copy-done.3, bf16[768,512]{1,0:T(8,128)(2,1)S(1)} %copy-done, f32[256,256]{1,0:T(8,128)S(1)} %collective-permute-done.2.refs_0_, ...), custom_call_target="tpu_custom_call" | custom-call | flops 402653184 | bytes 1572864 | tf_op jit(solution)/shard_map/pallas_call | solution.py:190
  31.4 0.0 collective-permute-done.4.refs_0_
  31.4 0.0 collective-permute-done.5.refs_1_
  31.5 2.0 %shard_map.104 = (f32[8,8,512]{2,1,0:T(8,128)S(1)}, f32[2,256,512]{2,1,0:T(8,128)S(1)}) custom-call(s32[1]{0:T(128)} %bitcast.me_ref, s32[8]{0:T(128)S(1)} %copy-done.2, s32[8]{0:T(128)S(1)} %copy-done.3, bf16[768,512]{1,0:T(8,128)(2,1)S(1)} %copy-done, f32[256,256]{1,0:T(8,128)S(1)} %collective-permute-done.4.refs_0_, ...), custom_call_target="tpu_custom_call" | custom-call | flops 402653184 | bytes 1572864 | tf_op jit(solution)/shard_map/pallas_call | solution.py:190
  33.5 13.7 %collective-permute-done.6.refs_0_ = f32[256,256]{1,0:T(8,128)S(1)} collective-permute-done((f32[256,256]{1,0:T(8,128)S(1)}, f32[256,256]{1,0:T(8,128)S(1)}, u32[]{:S(2)}, u32[]{:S(2)}) %collective-permute-start.6) | collective-permute-done | bytes 262176 | tf_op jit(solution)/shard_map/ppermute | solution.py:222
  47.2 1.4 %shard_map.105 = (f32[8,8,512]{2,1,0:T(8,128)S(1)}, f32[1,256,512]{2,1,0:T(8,128)S(1)}) custom-call(s32[1]{0:T(128)} %bitcast.me_ref, s32[8]{0:T(128)S(1)} %copy-done.2, s32[8]{0:T(128)S(1)} %copy-done.3, bf16[768,512]{1,0:T(8,128)(2,1)S(1)} %copy-done, f32[256,256]{1,0:T(8,128)S(1)} %collective-permute-done.6.refs_0_, ...), custom_call_target="tpu_custom_call" | custom-call | flops 201326592 | bytes 786432 | tf_op jit(solution)/shard_map/pallas_call | solution.py:190
  48.6 3.3 %collective-permute-done.refs_1_ = f32[256,256]{1,0:T(8,128)S(1)} collective-permute-done((f32[256,256]{1,0:T(8,128)S(1)}, f32[256,256]{1,0:T(8,128)S(1)}, u32[]{:S(2)}, u32[]{:S(2)}) %collective-permute-start) | collective-permute-done | bytes 262176 | tf_op jit(solution)/shard_map/ppermute | solution.py:222
  51.8 1.9 %shard_map.106 = f32[8,16,256]{2,1,0:T(8,128)S(1)} custom-call(s32[1]{0:T(128)} %bitcast.me_ref, s32[8]{0:T(128)S(1)} %copy-done.2, s32[8]{0:T(128)S(1)} %copy-done.3, bf16[768,512]{1,0:T(8,128)(2,1)S(1)} %copy-done, bf16[1536,256]{1,0:T(8,128)(2,1)S(1)} %copy-done.1, f32[256,256]{1,0:T(8,128)S(1)} %collective-permute-done.refs_1_, ...), custom_call_target="tpu_custom_call" | custom-call | flops 201326592 | bytes 786432 | tf_op jit(solution)/shard_map/pallas_call | solution.py:190
  53.7 10.9 %all_to_all.5 = f32[8,16,256]{2,1,0:T(8,128)S(1)} all-to-all(f32[8,16,256]{2,1,0:T(8,128)S(1)} %shard_map.106), channel_id=1, replica_groups=mesh['seq'=8,'ch'=4] {'seq'}, dimensions={0} | all-to-all | bytes 262144 | tf_op jit(solution)/shard_map/all_to_all | solution.py:239
  64.7 0.0 collective-permute-start.9
  64.7 1.6 %collective-permute-start.8 = (f32[128]{0:T(128)S(1)}, f32[128]{0:T(128)S(1)}, u32[]{:S(2)}, u32[]{:S(2)}) collective-permute-start(f32[128]{0:T(128)S(1)} %slice_reduce_fusion), channel_id=1, source_target_pairs={{0,2},{1,3},{2,0},{3,1},{4,6},{5,7},{6,4},{7,5},{8,10},{9,11},{10,... | collective-permute-start | bytes 1544 | tf_op jit(solution)/shard_map/ppermute | solution.py:244
  66.3 0.2 collective-permute-start.7
  66.5 0.0 collective-permute-done.9
  66.5 1.9 %collective-permute-done.8 = f32[128]{0:T(128)S(1)} collective-permute-done((f32[128]{0:T(128)S(1)}, f32[128]{0:T(128)S(1)}, u32[]{:S(2)}, u32[]{:S(2)}) %collective-permute-start.8) | collective-permute-done | bytes 544 | tf_op jit(solution)/shard_map/ppermute | solution.py:244
  68.3 0.9 %collective-permute-done.7 = f32[128]{0:T(128)S(1)} collective-permute-done((f32[128]{0:T(128)S(1)}, f32[128]{0:T(128)S(1)}, u32[]{:S(2)}, u32[]{:S(2)}) %collective-permute-start.7) | collective-permute-done | bytes 544 | tf_op jit(solution)/shard_map/ppermute | solution.py:244
  69.4 0.6 fusion
  (7 shorter events, 0.0 us)
Async XLA Ops:
  1.0 26.6 %copy-start = (bf16[768,512]{1,0:T(8,128)(2,1)S(1)}, bf16[768,512]{1,0:T(8,128)(2,1)}, u32[]{:S(2)}) copy-start(bf16[768,512]{1,0:T(8,128)(2,1)} %constant.16.clone.forward_ref) | copy-start | bytes 2359300
  1.0 12.8 %collective-permute-start.1 = (f32[256,256]{1,0:T(8,128)S(1)}, f32[256,256]{1,0:T(8,128)S(1)}, u32[]{:S(2)}, u32[]{:S(2)}) collective-permute-start(f32[256,256]{1,0:T(8,128)S(1)} %shard_map.100), channel_id=1, source_target_pairs={{0,28},{4,24},{8,20},{12,16},{16,12},{20,8},{24,4},{28,0},{1,29},{... | collective-permute-start | bytes 786440 | tf_op jit(solution)/shard_map/ppermute | solution.py:222
  8.7 18.8 %collective-permute-start.2 = (f32[256,256]{1,0:T(8,128)S(1)}, f32[256,256]{1,0:T(8,128)S(1)}, u32[]{:S(2)}, u32[]{:S(2)}) collective-permute-start(f32[256,256]{1,0:T(8,128)S(1)} %get-tuple-element.27), channel_id=1, source_target_pairs={{0,4},{4,0},{8,12},{12,8},{16,20},{20,16},{24,28},{28,24},{1,5},{5... | collective-permute-start | bytes 786440 | tf_op jit(solution)/shard_map/ppermute | solution.py:222
  9.3 20.4 %collective-permute-start.3 = (f32[256,256]{1,0:T(8,128)S(1)}, f32[256,256]{1,0:T(8,128)S(1)}, u32[]{:S(2)}, u32[]{:S(2)}) collective-permute-start(f32[256,256]{1,0:T(8,128)S(1)} %get-tuple-element.28), channel_id=1, source_target_pairs={{0,24},{4,28},{8,16},{12,20},{16,8},{20,12},{24,0},{28,4},{1,25},{... | collective-permute-start | bytes 786440 | tf_op jit(solution)/shard_map/ppermute | solution.py:222
  9.4 22.0 %collective-permute-start.4 = (f32[256,256]{1,0:T(8,128)S(1)}, f32[256,256]{1,0:T(8,128)S(1)}, u32[]{:S(2)}, u32[]{:S(2)}) collective-permute-start(f32[256,256]{1,0:T(8,128)S(1)} %get-tuple-element.31), channel_id=1, source_target_pairs={{0,8},{4,12},{8,0},{12,4},{16,24},{20,28},{24,16},{28,20},{1,9},{5... | collective-permute-start | bytes 786440 | tf_op jit(solution)/shard_map/ppermute | solution.py:222
  9.4 22.0 %collective-permute-start.5 = (f32[256,256]{1,0:T(8,128)S(1)}, f32[256,256]{1,0:T(8,128)S(1)}, u32[]{:S(2)}, u32[]{:S(2)}) collective-permute-start(f32[256,256]{1,0:T(8,128)S(1)} %get-tuple-element.32), channel_id=1, source_target_pairs={{0,12},{4,8},{8,4},{12,0},{16,28},{20,24},{24,20},{28,16},{1,13},{... | collective-permute-start | bytes 786440 | tf_op jit(solution)/shard_map/ppermute | solution.py:222
  13.8 33.4 %collective-permute-start.6 = (f32[256,256]{1,0:T(8,128)S(1)}, f32[256,256]{1,0:T(8,128)S(1)}, u32[]{:S(2)}, u32[]{:S(2)}) collective-permute-start(f32[256,256]{1,0:T(8,128)S(1)} %get-tuple-element.35), channel_id=1, source_target_pairs={{0,20},{4,16},{8,28},{12,24},{16,4},{20,0},{24,12},{28,8},{1,21},{... | collective-permute-start | bytes 786440 | tf_op jit(solution)/shard_map/ppermute | solution.py:222
  27.5 0.7 copy-start.2
  27.5 0.7 copy-start.3
  27.5 24.3 %collective-permute-start = (f32[256,256]{1,0:T(8,128)S(1)}, f32[256,256]{1,0:T(8,128)S(1)}, u32[]{:S(2)}, u32[]{:S(2)}) collective-permute-start(f32[256,256]{1,0:T(8,128)S(1)} %get-tuple-element.23), channel_id=1, source_target_pairs={{0,16},{4,20},{8,24},{12,28},{16,0},{20,4},{24,8},{28,12},{1,17},{... | collective-permute-start | bytes 786440 | tf_op jit(solution)/shard_map/ppermute | solution.py:222
  47.2 4.7 %copy-start.1 = (bf16[1536,256]{1,0:T(8,128)(2,1)S(1)}, bf16[1536,256]{1,0:T(8,128)(2,1)}, u32[]{:S(2)}) copy-start(bf16[1536,256]{1,0:T(8,128)(2,1)} %constant.17.clone.refs_0_) | copy-start | bytes 2359300
  64.7 1.8 %collective-permute-start.9 = (f32[128]{0:T(128)S(1)}, f32[128]{0:T(128)S(1)}, u32[]{:S(2)}, u32[]{:S(2)}) collective-permute-start(f32[128]{0:T(128)S(1)} %slice_reduce_fusion), channel_id=1, source_target_pairs={{0,3},{1,0},{2,1},{3,2},{4,7},{5,4},{6,5},{7,6},{8,11},{9,8},{10,9... | collective-permute-start | bytes 1544 | tf_op jit(solution)/shard_map/ppermute | solution.py:244
  64.7 3.6 %collective-permute-start.8 = (f32[128]{0:T(128)S(1)}, f32[128]{0:T(128)S(1)}, u32[]{:S(2)}, u32[]{:S(2)}) collective-permute-start(f32[128]{0:T(128)S(1)} %slice_reduce_fusion), channel_id=1, source_target_pairs={{0,2},{1,3},{2,0},{3,1},{4,6},{5,7},{6,4},{7,5},{8,10},{9,11},{10,... | collective-permute-start | bytes 1544 | tf_op jit(solution)/shard_map/ppermute | solution.py:244
  66.3 3.0 %collective-permute-start.7 = (f32[128]{0:T(128)S(1)}, f32[128]{0:T(128)S(1)}, u32[]{:S(2)}, u32[]{:S(2)}) collective-permute-start(f32[128]{0:T(128)S(1)} %slice_reduce_fusion), channel_id=1, source_target_pairs={{0,1},{1,2},{2,3},{3,0},{4,5},{5,6},{6,7},{7,4},{8,9},{9,10},{10,1... | collective-permute-start | bytes 1544 | tf_op jit(solution)/shard_map/ppermute | solution.py:244

commit v4 on v3

--- a/solution.py
+++ b/solution.py
@@ -43,11 +43,12 @@
     return (place - step if back else place + step) % count
 
 
-def cut_kernel(count, channels, steps, me_ref, inputs_ref, grads_ref, *refs):
+def cut_kernel(count, channels, steps, inputs_ref, grads_ref, *refs):
+    me = lax.axis_index("seq")
     blocks, sems = refs[:-1], refs[-1]
     copies = []
     for index, step in enumerate(steps):
-        start = pl.multiple_of(partner(count, me_ref[0], step) * channels, channels)
+        start = pl.multiple_of(partner(count, me, step) * channels, channels)
         for half, ref in enumerate((inputs_ref, grads_ref)):
             copies.append(
                 pltpu.make_async_copy(
@@ -62,27 +63,28 @@
         copy.wait()
 
 
-def cut(inputs, out_grads, me, count, steps):
+def cut(inputs, out_grads, count, steps):
     rows, channels = inputs.shape[0], inputs.shape[1] // count
     if channels % 128:
         blocks = []
         for step in steps:
-            start = partner(count, me[0], step) * channels
+            start = partner(count, lax.axis_index("seq"), step) * channels
             pair = [lax.dynamic_slice_in_dim(whole, start, channels, 1) for whole in (inputs, out_grads)]
             blocks.append(jnp.concatenate(pair, axis=1))
         return blocks
     anywhere = pl.BlockSpec(memory_space=pl.ANY)
     return pl.pallas_call(
         functools.partial(cut_kernel, count, channels, steps),
-        out_shape=[pltpu.VMEM((rows, 2 * channels), jnp.float32) for _ in steps],
-        in_specs=[pl.BlockSpec(memory_space=pltpu.SMEM), anywhere, anywhere],
+        out_shape=[jax.ShapeDtypeStruct((rows, 2 * channels), jnp.float32) for _ in steps],
+        in_specs=[anywhere, anywhere],
         out_specs=[pl.BlockSpec(memory_space=pltpu.VMEM) for _ in steps],
         scratch_shapes=[pltpu.SemaphoreType.DMA((2 * len(steps),))],
+        compiler_params=pltpu.CompilerParams(vmem_limit_bytes=6 * 2**20),
         cost_estimate=pl.CostEstimate(flops=0, bytes_accessed=len(steps) * rows * channels * 16, transcendentals=0),
-    )(me, inputs, out_grads)
-
-
-def absorb_kernel(count, channels, rows, new, olds, last, me_ref, order_ref, lag_ref, forward_ref, *refs):
+    )(*(pltpu.with_memory_space_constraint(whole, pltpu.HBM) for whole in (inputs, out_grads)))
+
+
+def absorb_kernel(count, channels, rows, new, olds, inner, last, order_ref, lag_ref, forward_ref, *refs):
     refs = list(refs)
     take = lambda many: [refs.pop(0) for _ in range(many)]
     inverse_ref = take(1)[0] if last else None
@@ -115,7 +117,7 @@
         )
     slots = list(new) + [step for old in olds for step in old]
     for index, step in enumerate(slots):
-        tile_of[index] = order_ref[partner(count, me_ref[0], step, back=True)]
+        tile_of[index] = order_ref[partner(count, lax.axis_index("seq"), step, back=True)]
 
     def pair(ref, first, new_index, index):
         new_tile, tile = tile_of[new_index], tile_of[first + index]
@@ -169,15 +171,42 @@
         inverse_ref[...],
         preferred_element_type=jnp.float32,
     )
-    squares = jnp.broadcast_to(jnp.sum(lags * lags, keepdims=True), (8, rows))
+    squares = jnp.broadcast_to(jnp.sum(lags * lags, keepdims=True), (1, out_ref.shape[2] - groups * rows))
     for offset in range(count):
         sums[offset, :, :rows] = lags[offset * groups : (offset + 1) * groups]
+    ways = out_ref.shape[0] // count
+    way = lax.axis_index("ch") // inner
+    for piece in range(count * ways):
+        out_ref[piece, :, groups * rows :] = squares
+        out_ref[piece, :, : groups * rows] = jnp.zeros((1, groups * rows), jnp.float32)
     for place in range(count):
-        out_ref[place, :groups, :] = sums[lag_ref[place], :, :rows]
-        out_ref[place, groups:, :] = squares
-
-
-def absorb(blocks, new, spectra, olds, carried, me, tile_order, lag_order, count, last):
+        block = sums[lag_ref[place], :, :rows]
+        for group in range(groups):
+            out_ref[place * ways + way, :, group * rows : (group + 1) * rows] = block[group : group + 1]
+
+
+def gather_kernel(count, groups, rows, inner, owned_ref, out_ref):
+    ways = owned_ref.shape[0] // count
+    way = lax.axis_index("ch") // inner
+    for place in range(count):
+        for group in range(groups):
+            row = owned_ref[place * ways + way, :, group * rows : (group + 1) * rows]
+            out_ref[place * groups + group : place * groups + group + 1, :] = row
+
+
+def gather(owned, count, groups, rows, inner):
+    vmem = pl.BlockSpec(memory_space=pltpu.VMEM)
+    return pl.pallas_call(
+        functools.partial(gather_kernel, count, groups, rows, inner),
+        out_shape=jax.ShapeDtypeStruct((count * groups, rows), jnp.float32),
+        in_specs=[vmem],
+        out_specs=vmem,
+        compiler_params=pltpu.CompilerParams(vmem_limit_bytes=4 * 2**20),
+        cost_estimate=pl.CostEstimate(flops=0, bytes_accessed=count * groups * rows * 8, transcendentals=0),
+    )(owned)
+
+
+def absorb(blocks, new, spectra, olds, carried, tile_order, lag_order, count, ways, inner, last):
     rows, channels = blocks[0].shape[0], blocks[0].shape[1] // 2
     groups = channels // GROUP
     width = math.gcd(rows, 128)
@@ -185,12 +214,12 @@
     smem = pl.BlockSpec(memory_space=pltpu.SMEM)
     tables = [jnp.asarray(forward_table(rows))] + ([jnp.asarray(inverse_table(rows))] if last else [])
     operands = tables + list(blocks) + list(spectra) + ([carried] if olds else [])
-    out = (count, groups + 8, rows) if last else (count, groups, 2 * rows)
+    out = (count * ways, 1, groups * rows + 128) if last else (count, groups, 2 * rows)
     fresh = jax.ShapeDtypeStruct((len(new), 2 * channels, 2 * rows), jnp.float32)
     result = pl.pallas_call(
-        functools.partial(absorb_kernel, count, channels, rows, new, olds, last),
+        functools.partial(absorb_kernel, count, channels, rows, new, olds, inner, last),
         out_shape=[jax.ShapeDtypeStruct(out, jnp.float32)] + ([] if last else [fresh]),
-        in_specs=[smem, smem, smem] + [vmem] * len(operands),
+        in_specs=[smem, smem] + [vmem] * len(operands),
         out_specs=[vmem] + ([] if last else [vmem]),
         scratch_shapes=([pltpu.VMEM(fresh.shape, jnp.float32)] if last else [])
         + [
@@ -202,7 +231,7 @@
         cost_estimate=pl.CostEstimate(
             flops=24 * len(new) * rows * rows * channels, bytes_accessed=len(new) * rows * channels * 24, transcendentals=0
         ),
-    )(me, tile_order, lag_order, *operands)
+    )(tile_order, lag_order, *operands)
     return result[0] if last else result
 
 
@@ -211,12 +240,14 @@
     rows = inputs.shape[0]
     channels = inputs.shape[1] // count
     groups = channels // GROUP
-    me = lax.axis_index("seq").reshape(1)
+    ways = lax.axis_size("ch")
+    inner = 2 if ways % 2 == 0 else 1
+    outer = ways // inner
     half = max(1, count // 2)
     far, near = list(range(count - 1, half - 1, -1)), list(range(half))
-    first = cut(inputs, out_grads, me, count, far[:1])
-    then, first = lax.optimization_barrier((me, first))
-    blocks = dict(zip(far + near, first + cut(inputs, out_grads, then, count, far[1:] + near)))
+    first = cut(inputs, out_grads, count, far[:1])
+    inputs, out_grads, first = lax.optimization_barrier((inputs, out_grads, first))
+    blocks = dict(zip(far + near, first + cut(inputs, out_grads, count, far[1:] + near)))
     for step in far + near[1:]:
         pairs = [(place, partner(count, place, step)) for place in range(count)]
         blocks[step] = lax.ppermute(blocks[step], "seq", pairs)
@@ -230,19 +261,34 @@
     for new in arrivals:
         last = new is arrivals[-1]
         made = absorb(
-            [blocks[step] for step in new], new, spectra, list(olds), carried, me, tile_order, lag_order, count, last
+            [blocks[step] for step in new],
+            new,
+            spectra,
+            list(olds),
+            carried,
+            tile_order,
+            lag_order,
+            count,
+            outer,
+            inner,
+            last,
         )
         if not last:
             carried, fresh = made
             spectra.append(fresh)
             olds.append(new)
-    owned = lax.all_to_all(made, "seq", split_axis=0, concat_axis=0, tiled=True)
-    squares = jnp.sum(owned[:, groups, :128], axis=0)
-    ways = lax.axis_size("ch")
-    total = squares
-    for step in range(1, ways):
-        total = total + lax.ppermute(squares, "ch", [(place, (place + step) % ways) for place in range(ways)])
-    lags = owned[:, :groups, :].reshape(count * groups, rows)
+    together = [
+        [place * ways + way * inner + core for place in range(count) for way in range(outer)] for core in range(inner)
+    ]
+    owned = lax.all_to_all(
+        made, ("seq", "ch"), split_axis=0, concat_axis=0, axis_index_groups=together, tiled=True
+    )
+    squares = owned[:, :, groups * rows :]
+    if inner == 2:
+        pairs = [(place, place ^ 1) for place in range(ways)]
+        squares = squares + lax.ppermute(squares, "ch", pairs)
+    total = jnp.sum(squares, axis=(0, 1))
+    lags = gather(owned, count, groups, rows, inner)
     entries = ways * count * groups * count * rows
     factor = target_ratio * math.sqrt(entries) / jnp.sqrt(total[:1] + epsilon)
     return lags * factor

time: 70.2 us -> 68.3 us (0.973)
  starting transfers between devices: 25.3 us -> 23.6 us
  waiting for transfers between devices: 21.1 us -> 19.5 us
  blocking collectives: 10.9 us -> 12.4 us
    ppermute x3 -> x1, starting transfers between devices: 1.8 us -> 0.01 us  [shards(): squares = squares + lax.ppermute(squares, 'ch', pairs)]
    ppermute x3 -> x1, waiting for transfers between devices: 2.8 us -> 1.11 us  [shards(): squares = squares + lax.ppermute(squares, 'ch', pairs)]
    all_to_all x1, blocking collectives: 10.9 us -> 12.4 us  [shards(): lax.all_to_all(made, ('seq', 'ch'), split_axis=0, concat_axis=0, axis_ind...]
  transfers between devices with their start and end apart: 10 -> 8, of which waited for: 5 -> 4; matrix products, arithmetic and copies ran while one was open for 0% -> 0% of each run, Pallas kernels for 12% -> 12%
where the time goes in v4:
time: 68.3 us; the launch traced here: 68.1 us
  starting transfers between devices  23.6 us (35%)
  waiting for transfers between devices  19.5 us (29%)
  blocking collectives  12.4 us (18%)
  Pallas kernels  11.1 us (16%)
    ppermute x7, starting transfers between devices, shards(): blocks[step] = lax.ppermute(blocks[step], 'seq', pairs)  23.6 us
    ppermute x7, waiting for transfers between devices, shards(): blocks[step] = lax.ppermute(blocks[step], 'seq', pairs)  18.3 us
    all_to_all x1, blocking collectives, shards(): lax.all_to_all(made, ('seq', 'ch'), split_axis=0, concat_axis=0, axis_ind...  12.4 us
    pallas_call x5, Pallas kernels, absorb(): pl.pallas_call(functools.partial(absorb_kernel, count, channels, rows, ne...  8.43 us
    pallas_call x2, Pallas kernels, cut(): pl.pallas_call(functools.partial(cut_kernel, count, channels, steps), out...  2.65 us
  transfers between devices with their start and end apart: 8, of which 4 were waited for; matrix products, arithmetic and copies ran while one was open for 0% of the time, Pallas kernels for 12%

profile of v4, /device:TPU:0, one launch (start us, length us, event | category | flops | bytes accessed | tf_op | source)
XLA Modules:
  0.0 68.1 jit_solution(10209803767314069293)
XLA Ops:
  0.0 1.0 %shard_map.100 = f32[256,256]{1,0:T(8,128)S(1)} custom-call(f32[256,1024]{1,0:T(8,128)} %inputs_ref.2, f32[256,1024]{1,0:T(8,128)} %grads_ref.2), custom_call_target="tpu_custom_call" | custom-call | bytes 524288 | tf_op jit(solution)/shard_map/pallas_call | solution.py:76
  1.0 0.0 copy-start
  1.0 6.0 %collective-permute-start.1 = (f32[256,256]{1,0:T(8,128)S(1)}, f32[256,256]{1,0:T(8,128)S(1)}, u32[]{:S(2)}, u32[]{:S(2)}) collective-permute-start(f32[256,256]{1,0:T(8,128)S(1)} %shard_map.100), channel_id=1, source_target_pairs={{0,28},{4,24},{8,20},{12,16},{16,12},{20,8},{24,4},{28,0},{1,29},{... | collective-permute-start | bytes 786440 | tf_op jit(solution)/shard_map/ppermute | solution.py:253
  7.0 1.7 %shard_map.101 = (f32[256,256]{1,0:T(8,128)S(1)}, f32[256,256]{1,0:T(8,128)S(1)}, f32[256,256]{1,0:T(8,128)S(1)}, f32[256,256]{1,0:T(8,128)S(1)}, f32[256,256]{1...) custom-call(f32[256,1024]{1,0:T(8,128)} %inputs_ref.2, f32[256,1024]{1,0:T(8,128)} %grads_ref.2), custom_call_target="tpu_custom_call" | custom-call | bytes 3670016 | tf_op jit(solution)/shard_map/pallas_call | solution.py:76
  8.7 0.6 collective-permute-start.2
  9.3 0.1 collective-permute-start.3
  9.4 0.0 collective-permute-start.4
  9.4 3.1 %collective-permute-start.5 = (f32[256,256]{1,0:T(8,128)S(1)}, f32[256,256]{1,0:T(8,128)S(1)}, u32[]{:S(2)}, u32[]{:S(2)}) collective-permute-start(f32[256,256]{1,0:T(8,128)S(1)} %get-tuple-element.34), channel_id=1, source_target_pairs={{0,12},{4,8},{8,4},{12,0},{16,28},{20,24},{24,20},{28,16},{1,13},{... | collective-permute-start | bytes 786440 | tf_op jit(solution)/shard_map/ppermute | solution.py:253
  12.5 1.3 %collective-permute-done.1.refs_1_ = f32[256,256]{1,0:T(8,128)S(1)} collective-permute-done((f32[256,256]{1,0:T(8,128)S(1)}, f32[256,256]{1,0:T(8,128)S(1)}, u32[]{:S(2)}, u32[]{:S(2)}) %collective-permute-start.1) | collective-permute-done | bytes 262176 | tf_op jit(solution)/shard_map/ppermute | solution.py:253
  13.8 13.7 %collective-permute-start.6 = (f32[256,256]{1,0:T(8,128)S(1)}, f32[256,256]{1,0:T(8,128)S(1)}, u32[]{:S(2)}, u32[]{:S(2)}) collective-permute-start(f32[256,256]{1,0:T(8,128)S(1)} %get-tuple-element.37), channel_id=1, source_target_pairs={{0,20},{4,16},{8,28},{12,24},{16,4},{20,0},{24,12},{28,8},{1,21},{... | collective-permute-start | bytes 786440 | tf_op jit(solution)/shard_map/ppermute | solution.py:253
  27.5 0.0 collective-permute-done.2.refs_0_
  27.5 0.0 copy-start.2
  27.5 0.0 copy-start.3
  27.5 0.0 collective-permute-start
  27.6 0.0 copy-done
  27.6 0.6 copy-done.2
  28.2 0.0 copy-done.3
  28.2 1.5 %shard_map.102 = (f32[8,8,512]{2,1,0:T(8,128)S(1)}, f32[2,256,512]{2,1,0:T(8,128)S(1)}) custom-call(s32[8]{0:T(128)S(1)} %copy-done.2, s32[8]{0:T(128)S(1)} %copy-done.3, bf16[768,512]{1,0:T(8,128)(2,1)S(1)} %copy-done, f32[256,256]{1,0:T(8,128)S(1)} %get-tuple-element.26.refs_0_, f32[256,256]{1,0:T(8,128)S(1)} %collective-permute-done.1.refs_1_), custom_call_target="tpu_custom_call" | custom-call | flops 402653184 | bytes 1572864 | tf_op jit(solution)/shard_map/pallas_call | solution.py:219
  29.7 0.0 collective-permute-done.3.refs_1_
  29.7 1.7 %shard_map.103 = (f32[8,8,512]{2,1,0:T(8,128)S(1)}, f32[2,256,512]{2,1,0:T(8,128)S(1)}) custom-call(s32[8]{0:T(128)S(1)} %copy-done.2, s32[8]{0:T(128)S(1)} %copy-done.3, bf16[768,512]{1,0:T(8,128)(2,1)S(1)} %copy-done, f32[256,256]{1,0:T(8,128)S(1)} %collective-permute-done.2.refs_0_, f32[256,256]{1,0:T(8,128)S(1)} %collective-permute-done.3.refs_1_, ...), custom_call_target="tpu_custom_call" | custom-call | flops 402653184 | bytes 1572864 | tf_op jit(solution)/shard_map/pallas_call | solution.py:219
  31.4 0.0 collective-permute-done.4.refs_0_
  31.4 0.0 collective-permute-done.5.refs_1_
  31.4 2.0 %shard_map.104 = (f32[8,8,512]{2,1,0:T(8,128)S(1)}, f32[2,256,512]{2,1,0:T(8,128)S(1)}) custom-call(s32[8]{0:T(128)S(1)} %copy-done.2, s32[8]{0:T(128)S(1)} %copy-done.3, bf16[768,512]{1,0:T(8,128)(2,1)S(1)} %copy-done, f32[256,256]{1,0:T(8,128)S(1)} %collective-permute-done.4.refs_0_, f32[256,256]{1,0:T(8,128)S(1)} %collective-permute-done.5.refs_1_, ...), custom_call_target="tpu_custom_call" | custom-call | flops 402653184 | bytes 1572864 | tf_op jit(solution)/shard_map/pallas_call | solution.py:219
  33.4 13.8 %collective-permute-done.6.refs_0_ = f32[256,256]{1,0:T(8,128)S(1)} collective-permute-done((f32[256,256]{1,0:T(8,128)S(1)}, f32[256,256]{1,0:T(8,128)S(1)}, u32[]{:S(2)}, u32[]{:S(2)}) %collective-permute-start.6) | collective-permute-done | bytes 262176 | tf_op jit(solution)/shard_map/ppermute | solution.py:253
  47.2 1.4 %shard_map.105 = (f32[8,8,512]{2,1,0:T(8,128)S(1)}, f32[1,256,512]{2,1,0:T(8,128)S(1)}) custom-call(s32[8]{0:T(128)S(1)} %copy-done.2, s32[8]{0:T(128)S(1)} %copy-done.3, bf16[768,512]{1,0:T(8,128)(2,1)S(1)} %copy-done, f32[256,256]{1,0:T(8,128)S(1)} %collective-permute-done.6.refs_0_, f32[2,256,512]{2,1,0:T(8,128)S(1)} %get-tuple-element.28.refs_2_.refs_1_, ...), custom_call_target="tpu_custom_call" | custom-call | flops 201326592 | bytes 786432 | tf_op jit(solution)/shard_map/pallas_call | solution.py:219
  48.6 3.3 %collective-permute-done.refs_1_ = f32[256,256]{1,0:T(8,128)S(1)} collective-permute-done((f32[256,256]{1,0:T(8,128)S(1)}, f32[256,256]{1,0:T(8,128)S(1)}, u32[]{:S(2)}, u32[]{:S(2)}) %collective-permute-start) | collective-permute-done | bytes 262176 | tf_op jit(solution)/shard_map/ppermute | solution.py:253
  51.8 0.0 copy-done.1
  51.8 1.9 %shard_map.106 = f32[16,1,2176]{2,1,0:T(1,128)S(1)} custom-call(s32[8]{0:T(128)S(1)} %copy-done.2, s32[8]{0:T(128)S(1)} %copy-done.3, bf16[768,512]{1,0:T(8,128)(2,1)S(1)} %copy-done, bf16[1536,256]{1,0:T(8,128)(2,1)S(1)} %copy-done.1, f32[256,256]{1,0:T(8,128)S(1)} %collective-permute-done.refs_1_, f32[2,256,512]{2,1,0:T(8,128)S(1)} %get-tuple-element.28.refs_2_.refs_1_, ...), custom_call_target="tpu_custom_call" | custom-call | flops 201326592 | bytes 786432 | tf_op jit(solution)/shard_map/pallas_call | solution.py:219
  53.7 12.4 %all_to_all.5.owned_ref = f32[16,1,2176]{2,1,0:T(1,128)S(1)} all-to-all(f32[16,1,2176]{2,1,0:T(1,128)S(1)} %shard_map.106), channel_id=1, replica_groups={{0,2,4,6,8,10,12,14,16,18,20,22,24,26,28,30},{1,3,5,7,9,11,13,15,17,19,..., dimensions={0} | all-to-all | bytes 278528 | tf_op jit(solution)/shard_map/all_to_all | solution.py:283
  66.2 0.0 collective-permute-start.7
  66.3 1.1 %collective-permute-done.7 = f32[16,1,128]{2,1,0:T(1,128)S(1)} collective-permute-done((f32[16,1,128]{2,1,0:T(1,128)S(1)}, f32[16,1,128]{2,1,0:T(1,128)S(1)}, u32[]{:S(2)}, u32[]{:S(2)}) %collective-permute-start.7) | collective-permute-done | bytes 8224 | tf_op jit(solution)/shard_map/ppermute | solution.py:289
  67.5 0.6 broadcast_multiply_fusion
  (4 shorter events, 0.1 us)
Async XLA Ops:
  1.0 26.6 %copy-start = (bf16[768,512]{1,0:T(8,128)(2,1)S(1)}, bf16[768,512]{1,0:T(8,128)(2,1)}, u32[]{:S(2)}) copy-start(bf16[768,512]{1,0:T(8,128)(2,1)} %constant.10.clone.forward_ref) | copy-start | bytes 2359300
  1.0 12.8 %collective-permute-start.1 = (f32[256,256]{1,0:T(8,128)S(1)}, f32[256,256]{1,0:T(8,128)S(1)}, u32[]{:S(2)}, u32[]{:S(2)}) collective-permute-start(f32[256,256]{1,0:T(8,128)S(1)} %shard_map.100), channel_id=1, source_target_pairs={{0,28},{4,24},{8,20},{12,16},{16,12},{20,8},{24,4},{28,0},{1,29},{... | collective-permute-start | bytes 786440 | tf_op jit(solution)/shard_map/ppermute | solution.py:253
  8.7 18.8 %collective-permute-start.2 = (f32[256,256]{1,0:T(8,128)S(1)}, f32[256,256]{1,0:T(8,128)S(1)}, u32[]{:S(2)}, u32[]{:S(2)}) collective-permute-start(f32[256,256]{1,0:T(8,128)S(1)} %get-tuple-element.29), channel_id=1, source_target_pairs={{0,4},{4,0},{8,12},{12,8},{16,20},{20,16},{24,28},{28,24},{1,5},{5... | collective-permute-start | bytes 786440 | tf_op jit(solution)/shard_map/ppermute | solution.py:253
  9.3 20.4 %collective-permute-start.3 = (f32[256,256]{1,0:T(8,128)S(1)}, f32[256,256]{1,0:T(8,128)S(1)}, u32[]{:S(2)}, u32[]{:S(2)}) collective-permute-start(f32[256,256]{1,0:T(8,128)S(1)} %get-tuple-element.30), channel_id=1, source_target_pairs={{0,24},{4,28},{8,16},{12,20},{16,8},{20,12},{24,0},{28,4},{1,25},{... | collective-permute-start | bytes 786440 | tf_op jit(solution)/shard_map/ppermute | solution.py:253
  9.4 22.0 %collective-permute-start.4 = (f32[256,256]{1,0:T(8,128)S(1)}, f32[256,256]{1,0:T(8,128)S(1)}, u32[]{:S(2)}, u32[]{:S(2)}) collective-permute-start(f32[256,256]{1,0:T(8,128)S(1)} %get-tuple-element.33), channel_id=1, source_target_pairs={{0,8},{4,12},{8,0},{12,4},{16,24},{20,28},{24,16},{28,20},{1,9},{5... | collective-permute-start | bytes 786440 | tf_op jit(solution)/shard_map/ppermute | solution.py:253
  9.4 22.0 %collective-permute-start.5 = (f32[256,256]{1,0:T(8,128)S(1)}, f32[256,256]{1,0:T(8,128)S(1)}, u32[]{:S(2)}, u32[]{:S(2)}) collective-permute-start(f32[256,256]{1,0:T(8,128)S(1)} %get-tuple-element.34), channel_id=1, source_target_pairs={{0,12},{4,8},{8,4},{12,0},{16,28},{20,24},{24,20},{28,16},{1,13},{... | collective-permute-start | bytes 786440 | tf_op jit(solution)/shard_map/ppermute | solution.py:253
  13.8 33.4 %collective-permute-start.6 = (f32[256,256]{1,0:T(8,128)S(1)}, f32[256,256]{1,0:T(8,128)S(1)}, u32[]{:S(2)}, u32[]{:S(2)}) collective-permute-start(f32[256,256]{1,0:T(8,128)S(1)} %get-tuple-element.37), channel_id=1, source_target_pairs={{0,20},{4,16},{8,28},{12,24},{16,4},{20,0},{24,12},{28,8},{1,21},{... | collective-permute-start | bytes 786440 | tf_op jit(solution)/shard_map/ppermute | solution.py:253
  27.5 0.7 copy-start.2
  27.5 0.7 copy-start.3
  27.5 24.3 %collective-permute-start = (f32[256,256]{1,0:T(8,128)S(1)}, f32[256,256]{1,0:T(8,128)S(1)}, u32[]{:S(2)}, u32[]{:S(2)}) collective-permute-start(f32[256,256]{1,0:T(8,128)S(1)} %get-tuple-element.25), channel_id=1, source_target_pairs={{0,16},{4,20},{8,24},{12,28},{16,0},{20,4},{24,8},{28,12},{1,17},{... | collective-permute-start | bytes 786440 | tf_op jit(solution)/shard_map/ppermute | solution.py:253
  47.2 4.7 %copy-start.1 = (bf16[1536,256]{1,0:T(8,128)(2,1)S(1)}, bf16[1536,256]{1,0:T(8,128)(2,1)}, u32[]{:S(2)}) copy-start(bf16[1536,256]{1,0:T(8,128)(2,1)} %constant.11.clone.refs_0_) | copy-start | bytes 2359300
  66.2 1.2 %collective-permute-start.7 = (f32[16,1,128]{2,1,0:T(1,128)S(1)}, f32[16,1,128]{2,1,0:T(1,128)S(1)}, u32[]{:S(2)}, u32[]{:S(2)}) collective-permute-start(f32[16,1,128]{2,1,0:T(1,128)S(1)} %slice.8), channel_id=1, source_target_pairs={{0,1},{1,0},{2,3},{3,2},{4,5},{5,4},{6,7},{7,6},{8,9},{9,8},{10,11... | collective-permute-start | bytes 24584 | tf_op jit(solution)/shard_map/ppermute | solution.py:289

commit v5 on v4

--- a/solution.py
+++ b/solution.py
@@ -84,7 +84,7 @@
     )(*(pltpu.with_memory_space_constraint(whole, pltpu.HBM) for whole in (inputs, out_grads)))
 
 
-def absorb_kernel(count, channels, rows, new, olds, inner, last, order_ref, lag_ref, forward_ref, *refs):
+def absorb_kernel(count, channels, rows, new, olds, inner, last, order_from, lag_from, forward_ref, *refs):
     refs = list(refs)
     take = lambda many: [refs.pop(0) for _ in range(many)]
     inverse_ref = take(1)[0] if last else None
@@ -92,8 +92,13 @@
     carried = take(1)[0] if olds else None
     out_ref = take(1)[0]
     fresh = take(1)[0]
-    sums, turned, tile_of = take(3)
+    sums, turned, order_ref, lag_ref, tile_of, sems = take(6)
     width = turned.shape[2]
+    scalars = [pltpu.make_async_copy(order_from, order_ref, sems.at[0])]
+    if last:
+        scalars.append(pltpu.make_async_copy(lag_from, lag_ref, sems.at[1]))
+    for copy in scalars:
+        copy.start()
     groups = channels // GROUP
     chunk = max(8, groups)
 
@@ -115,48 +120,56 @@
         fresh[index] = jnp.dot(
             split(jnp.concatenate(columns, axis=1)), forward_ref[...], preferred_element_type=jnp.float32
         )
+    for copy in scalars:
+        copy.wait()
     slots = list(new) + [step for old in olds for step in old]
     for index, step in enumerate(slots):
         tile_of[index] = order_ref[partner(count, lax.axis_index("seq"), step, back=True)]
 
-    def pair(ref, first, new_index, index):
-        new_tile, tile = tile_of[new_index], tile_of[first + index]
-        later = new_tile > tile
-        new_base = jnp.where(later, channels, 0)
-        base = jnp.where(later, 0, channels)
-        total_real = total_imag = None
-        for start in range(0, channels, chunk):
-            new_rows = pl.ds(pl.multiple_of(new_base + start, chunk), chunk)
-            its_rows = pl.ds(pl.multiple_of(base + start, chunk), chunk)
-            new_real, new_imag = fresh[new_index, new_rows, :rows], fresh[new_index, new_rows, rows:]
-            real, imag = ref[index, its_rows, :rows], ref[index, its_rows, rows:]
-            term_real = new_real * real + new_imag * imag
-            term_imag = new_real * imag - new_imag * real
-            total_real = term_real if total_real is None else total_real + term_real
-            total_imag = term_imag if total_imag is None else total_imag + term_imag
-        total_imag = total_imag * jnp.where(later, -1.0, 1.0)
-        both = jnp.concatenate([total_real, total_imag], axis=1)
-        if chunk > groups:
-            both = sum(both[row : row + groups] for row in range(0, chunk, groups))
-        offset = jnp.abs(new_tile - tile)
-        sums[offset] = sums[offset] + both
-
-    def each_new(new_index, carry):
-        def each(ref, first):
-            def body(index, carry):
-                pair(ref, first, new_index, index)
-                return carry
-
-            return body
-
-        lax.fori_loop(0, new_index + 1, each(fresh, 0), 0)
-        first = len(new)
-        for ref, old in zip(spectra, olds):
-            lax.fori_loop(0, len(old), each(ref, first), 0)
-            first += len(old)
-        return carry
-
-    lax.fori_loop(0, len(new), each_new, 0)
+    def meet(new_index, others):
+        new_tile = tile_of[new_index]
+        tiles = [tile_of[place] for place, _, _ in others]
+        later = [jnp.full((chunk, rows), (new_tile > tile).astype(jnp.int32)) > 0 for tile in tiles]
+        bases = [jnp.where(new_tile > tile, 0, channels) for tile in tiles]
+
+        def step(index, totals):
+            start = index * chunk
+            input_rows = slice(start, start + chunk)
+            grad_rows = slice(channels + start, channels + start + chunk)
+            input_real, input_imag = fresh[new_index, input_rows, :rows], fresh[new_index, input_rows, rows:]
+            grad_real, grad_imag = fresh[new_index, grad_rows, :rows], fresh[new_index, grad_rows, rows:]
+            out = []
+            for (_, ref, slot), is_later, base, (total_real, total_imag) in zip(others, later, bases, totals):
+                its_rows = pl.ds(pl.multiple_of(base + start, chunk), chunk)
+                real, imag = ref[slot, its_rows, :rows], ref[slot, its_rows, rows:]
+                new_real = jnp.where(is_later, grad_real, input_real)
+                new_imag = jnp.where(is_later, grad_imag, input_imag)
+                out.append(
+                    (
+                        total_real + (new_real * real + new_imag * imag),
+                        total_imag + (new_real * imag - new_imag * real),
+                    )
+                )
+            return out
+
+        zero = jnp.zeros((chunk, rows), jnp.float32)
+        totals = [(zero, zero) for _ in others]
+        for index in range(channels // chunk):
+            totals = step(index, totals)
+        for tile, (total_real, total_imag) in zip(tiles, totals):
+            total_imag = total_imag * jnp.where(new_tile > tile, -1.0, 1.0)
+            both = jnp.concatenate([total_real, total_imag], axis=1)
+            if chunk > groups:
+                both = sum(both[row : row + groups] for row in range(0, chunk, groups))
+            offset = jnp.abs(new_tile - tile)
+            sums[offset] = sums[offset] + both
+
+    earlier = [(ref, slot) for ref, old in zip(spectra, olds) for slot in range(len(old))]
+    for new_index in range(len(new)):
+        others = [(place, fresh, place) for place in range(new_index + 1)]
+        others += [(len(new) + place, ref, slot) for place, (ref, slot) in enumerate(earlier)]
+        for first in range(0, len(others), 4):
+            meet(new_index, others[first : first + 4])
     if not last:
         out_ref[...] = sums[...]
         return
@@ -211,7 +224,7 @@
     groups = channels // GROUP
     width = math.gcd(rows, 128)
     vmem = pl.BlockSpec(memory_space=pltpu.VMEM)
-    smem = pl.BlockSpec(memory_space=pltpu.SMEM)
+    anywhere = pl.BlockSpec(memory_space=pl.ANY)
     tables = [jnp.asarray(forward_table(rows))] + ([jnp.asarray(inverse_table(rows))] if last else [])
     operands = tables + list(blocks) + list(spectra) + ([carried] if olds else [])
     out = (count * ways, 1, groups * rows + 128) if last else (count, groups, 2 * rows)
@@ -219,13 +232,16 @@
     result = pl.pallas_call(
         functools.partial(absorb_kernel, count, channels, rows, new, olds, inner, last),
         out_shape=[jax.ShapeDtypeStruct(out, jnp.float32)] + ([] if last else [fresh]),
-        in_specs=[smem, smem] + [vmem] * len(operands),
+        in_specs=[anywhere, anywhere] + [vmem] * len(operands),
         out_specs=[vmem] + ([] if last else [vmem]),
         scratch_shapes=([pltpu.VMEM(fresh.shape, jnp.float32)] if last else [])
         + [
             pltpu.VMEM((count, groups, 2 * rows), jnp.float32),
             pltpu.VMEM((rows // width, 2 * channels, width), jnp.float32),
             pltpu.SMEM((count,), jnp.int32),
+            pltpu.SMEM((count,), jnp.int32),
+            pltpu.SMEM((count,), jnp.int32),
+            pltpu.SemaphoreType.DMA((2,)),
         ],
         compiler_params=pltpu.CompilerParams(vmem_limit_bytes=20 * 2**20),
         cost_estimate=pl.CostEstimate(

time: 68.3 us -> 67.8 us (level)
  Pallas kernels: 11.1 us -> 8.14 us
  waiting for transfers between devices: 19.5 us -> 21.9 us
    pallas_call x5, Pallas kernels: 8.43 us -> 5.45 us  [absorb(): pl.pallas_call(functools.partial(absorb_kernel, count, channels, rows, ne...]
    ppermute x7, waiting for transfers between devices: 18.3 us -> 20.8 us  [shards(): blocks[step] = lax.ppermute(blocks[step], 'seq', pairs)]
  transfers between devices with their start and end apart: 8 -> 8, of which waited for: 4 -> 5; matrix products, arithmetic and copies ran while one was open for 0% -> 0% of each run, Pallas kernels for 12% -> 9%
where the time goes in v5:
time: 67.8 us; the launch traced here: 67.6 us
  starting transfers between devices  23.6 us (35%)
  waiting for transfers between devices  21.9 us (32%)
  blocking collectives  12.4 us (18%)
  Pallas kernels  8.14 us (12%)
    ppermute x7, starting transfers between devices, shards(): blocks[step] = lax.ppermute(blocks[step], 'seq', pairs)  23.6 us
    ppermute x7, waiting for transfers between devices, shards(): blocks[step] = lax.ppermute(blocks[step], 'seq', pairs)  20.8 us
    all_to_all x1, blocking collectives, shards(): lax.all_to_all(made, ('seq', 'ch'), split_axis=0, concat_axis=0, axis_ind...  12.4 us
    pallas_call x5, Pallas kernels, absorb(): pl.pallas_call(functools.partial(absorb_kernel, count, channels, rows, ne...  5.45 us
    pallas_call x2, Pallas kernels, cut(): pl.pallas_call(functools.partial(cut_kernel, count, channels, steps), out...  2.65 us
  transfers between devices with their start and end apart: 8, of which 5 were waited for; matrix products, arithmetic and copies ran while one was open for 0% of the time, Pallas kernels for 9%

profile of v5, /device:TPU:0, one launch (start us, length us, event | category | flops | bytes accessed | tf_op | source)
XLA Modules:
  0.0 67.6 jit_solution(181929961858427286)
XLA Ops:
  0.0 1.0 %shard_map.100 = f32[256,256]{1,0:T(8,128)S(1)} custom-call(f32[256,1024]{1,0:T(8,128)} %inputs_ref.2, f32[256,1024]{1,0:T(8,128)} %grads_ref.2), custom_call_target="tpu_custom_call" | custom-call | bytes 524288 | tf_op jit(solution)/shard_map/pallas_call | solution.py:76
  1.0 0.0 copy-start
  1.0 6.0 %collective-permute-start.1 = (f32[256,256]{1,0:T(8,128)S(1)}, f32[256,256]{1,0:T(8,128)S(1)}, u32[]{:S(2)}, u32[]{:S(2)}) collective-permute-start(f32[256,256]{1,0:T(8,128)S(1)} %shard_map.100), channel_id=1, source_target_pairs={{0,28},{4,24},{8,20},{12,16},{16,12},{20,8},{24,4},{28,0},{1,29},{... | collective-permute-start | bytes 786440 | tf_op jit(solution)/shard_map/ppermute | solution.py:269
  7.0 1.7 %shard_map.101 = (f32[256,256]{1,0:T(8,128)S(1)}, f32[256,256]{1,0:T(8,128)S(1)}, f32[256,256]{1,0:T(8,128)S(1)}, f32[256,256]{1,0:T(8,128)S(1)}, f32[256,256]{1...) custom-call(f32[256,1024]{1,0:T(8,128)} %inputs_ref.2, f32[256,1024]{1,0:T(8,128)} %grads_ref.2), custom_call_target="tpu_custom_call" | custom-call | bytes 3670016 | tf_op jit(solution)/shard_map/pallas_call | solution.py:76
  8.7 0.6 collective-permute-start.2
  9.3 0.1 collective-permute-start.3
  9.4 0.0 collective-permute-start.4
  9.4 3.1 %collective-permute-start.5 = (f32[256,256]{1,0:T(8,128)S(1)}, f32[256,256]{1,0:T(8,128)S(1)}, u32[]{:S(2)}, u32[]{:S(2)}) collective-permute-start(f32[256,256]{1,0:T(8,128)S(1)} %get-tuple-element.34), channel_id=1, source_target_pairs={{0,12},{4,8},{8,4},{12,0},{16,28},{20,24},{24,20},{28,16},{1,13},{... | collective-permute-start | bytes 786440 | tf_op jit(solution)/shard_map/ppermute | solution.py:269
  12.5 1.3 %collective-permute-done.1.refs_1_ = f32[256,256]{1,0:T(8,128)S(1)} collective-permute-done((f32[256,256]{1,0:T(8,128)S(1)}, f32[256,256]{1,0:T(8,128)S(1)}, u32[]{:S(2)}, u32[]{:S(2)}) %collective-permute-start.1) | collective-permute-done | bytes 262176 | tf_op jit(solution)/shard_map/ppermute | solution.py:269
  13.8 13.7 %collective-permute-start.6 = (f32[256,256]{1,0:T(8,128)S(1)}, f32[256,256]{1,0:T(8,128)S(1)}, u32[]{:S(2)}, u32[]{:S(2)}) collective-permute-start(f32[256,256]{1,0:T(8,128)S(1)} %get-tuple-element.37), channel_id=1, source_target_pairs={{0,20},{4,16},{8,28},{12,24},{16,4},{20,0},{24,12},{28,8},{1,21},{... | collective-permute-start | bytes 786440 | tf_op jit(solution)/shard_map/ppermute | solution.py:269
  27.5 0.0 collective-permute-done.2.refs_0_
  27.5 0.0 copy-start.2
  27.5 0.0 copy-start.3
  27.5 0.0 collective-permute-start
  27.6 0.0 copy-done
  27.6 0.6 copy-done.2
  28.2 0.0 copy-done.3
  28.2 0.9 %shard_map.102 = (f32[8,8,512]{2,1,0:T(8,128)S(1)}, f32[2,256,512]{2,1,0:T(8,128)S(1)}) custom-call(s32[8]{0:T(128)S(1)} %copy-done.2, s32[8]{0:T(128)S(1)} %copy-done.3, bf16[768,512]{1,0:T(8,128)(2,1)S(1)} %copy-done, f32[256,256]{1,0:T(8,128)S(1)} %get-tuple-element.26.refs_0_, f32[256,256]{1,0:T(8,128)S(1)} %collective-permute-done.1.refs_1_), custom_call_target="tpu_custom_call" | custom-call | flops 402653184 | bytes 1572864 | tf_op jit(solution)/shard_map/pallas_call | solution.py:232
  29.1 0.0 collective-permute-done.3.refs_1_
  29.1 1.0 %shard_map.103 = (f32[8,8,512]{2,1,0:T(8,128)S(1)}, f32[2,256,512]{2,1,0:T(8,128)S(1)}) custom-call(s32[8]{0:T(128)S(1)} %copy-done.2, s32[8]{0:T(128)S(1)} %copy-done.3, bf16[768,512]{1,0:T(8,128)(2,1)S(1)} %copy-done, f32[256,256]{1,0:T(8,128)S(1)} %collective-permute-done.2.refs_0_, f32[256,256]{1,0:T(8,128)S(1)} %collective-permute-done.3.refs_1_, ...), custom_call_target="tpu_custom_call" | custom-call | flops 402653184 | bytes 1572864 | tf_op jit(solution)/shard_map/pallas_call | solution.py:232
  30.1 0.0 collective-permute-done.4.refs_0_
  30.2 1.1 %collective-permute-done.5.refs_1_ = f32[256,256]{1,0:T(8,128)S(1)} collective-permute-done((f32[256,256]{1,0:T(8,128)S(1)}, f32[256,256]{1,0:T(8,128)S(1)}, u32[]{:S(2)}, u32[]{:S(2)}) %collective-permute-start.5) | collective-permute-done | bytes 262176 | tf_op jit(solution)/shard_map/ppermute | solution.py:269
  31.2 1.3 %shard_map.104 = (f32[8,8,512]{2,1,0:T(8,128)S(1)}, f32[2,256,512]{2,1,0:T(8,128)S(1)}) custom-call(s32[8]{0:T(128)S(1)} %copy-done.2, s32[8]{0:T(128)S(1)} %copy-done.3, bf16[768,512]{1,0:T(8,128)(2,1)S(1)} %copy-done, f32[256,256]{1,0:T(8,128)S(1)} %collective-permute-done.4.refs_0_, f32[256,256]{1,0:T(8,128)S(1)} %collective-permute-done.5.refs_1_, ...), custom_call_target="tpu_custom_call" | custom-call | flops 402653184 | bytes 1572864 | tf_op jit(solution)/shard_map/pallas_call | solution.py:232
  32.5 14.7 %collective-permute-done.6.refs_0_ = f32[256,256]{1,0:T(8,128)S(1)} collective-permute-done((f32[256,256]{1,0:T(8,128)S(1)}, f32[256,256]{1,0:T(8,128)S(1)}, u32[]{:S(2)}, u32[]{:S(2)}) %collective-permute-start.6) | collective-permute-done | bytes 262176 | tf_op jit(solution)/shard_map/ppermute | solution.py:269
  47.2 0.9 %shard_map.105 = (f32[8,8,512]{2,1,0:T(8,128)S(1)}, f32[1,256,512]{2,1,0:T(8,128)S(1)}) custom-call(s32[8]{0:T(128)S(1)} %copy-done.2, s32[8]{0:T(128)S(1)} %copy-done.3, bf16[768,512]{1,0:T(8,128)(2,1)S(1)} %copy-done, f32[256,256]{1,0:T(8,128)S(1)} %collective-permute-done.6.refs_0_, f32[2,256,512]{2,1,0:T(8,128)S(1)} %get-tuple-element.28.refs_2_.refs_1_, ...), custom_call_target="tpu_custom_call" | custom-call | flops 201326592 | bytes 786432 | tf_op jit(solution)/shard_map/pallas_call | solution.py:232
  48.1 3.7 %collective-permute-done.refs_1_ = f32[256,256]{1,0:T(8,128)S(1)} collective-permute-done((f32[256,256]{1,0:T(8,128)S(1)}, f32[256,256]{1,0:T(8,128)S(1)}, u32[]{:S(2)}, u32[]{:S(2)}) %collective-permute-start) | collective-permute-done | bytes 262176 | tf_op jit(solution)/shard_map/ppermute | solution.py:269
  51.8 0.0 copy-done.1
  51.8 1.4 %shard_map.106 = f32[16,1,2176]{2,1,0:T(1,128)S(1)} custom-call(s32[8]{0:T(128)S(1)} %copy-done.2, s32[8]{0:T(128)S(1)} %copy-done.3, bf16[768,512]{1,0:T(8,128)(2,1)S(1)} %copy-done, bf16[1536,256]{1,0:T(8,128)(2,1)S(1)} %copy-done.1, f32[256,256]{1,0:T(8,128)S(1)} %collective-permute-done.refs_1_, f32[2,256,512]{2,1,0:T(8,128)S(1)} %get-tuple-element.28.refs_2_.refs_1_, ...), custom_call_target="tpu_custom_call" | custom-call | flops 201326592 | bytes 786432 | tf_op jit(solution)/shard_map/pallas_call | solution.py:232
  53.2 12.4 %all_to_all.5.owned_ref = f32[16,1,2176]{2,1,0:T(1,128)S(1)} all-to-all(f32[16,1,2176]{2,1,0:T(1,128)S(1)} %shard_map.106), channel_id=1, replica_groups={{0,2,4,6,8,10,12,14,16,18,20,22,24,26,28,30},{1,3,5,7,9,11,13,15,17,19,..., dimensions={0} | all-to-all | bytes 278528 | tf_op jit(solution)/shard_map/all_to_all | solution.py:299
  65.7 0.0 collective-permute-start.7
  65.7 1.1 %collective-permute-done.7 = f32[16,1,128]{2,1,0:T(1,128)S(1)} collective-permute-done((f32[16,1,128]{2,1,0:T(1,128)S(1)}, f32[16,1,128]{2,1,0:T(1,128)S(1)}, u32[]{:S(2)}, u32[]{:S(2)}) %collective-permute-start.7) | collective-permute-done | bytes 8224 | tf_op jit(solution)/shard_map/ppermute | solution.py:305
  67.0 0.6 broadcast_multiply_fusion
  (4 shorter events, 0.1 us)
Async XLA Ops:
  1.0 26.6 %copy-start = (bf16[768,512]{1,0:T(8,128)(2,1)S(1)}, bf16[768,512]{1,0:T(8,128)(2,1)}, u32[]{:S(2)}) copy-start(bf16[768,512]{1,0:T(8,128)(2,1)} %constant.10.clone.forward_ref) | copy-start | bytes 2359300
  1.0 12.8 %collective-permute-start.1 = (f32[256,256]{1,0:T(8,128)S(1)}, f32[256,256]{1,0:T(8,128)S(1)}, u32[]{:S(2)}, u32[]{:S(2)}) collective-permute-start(f32[256,256]{1,0:T(8,128)S(1)} %shard_map.100), channel_id=1, source_target_pairs={{0,28},{4,24},{8,20},{12,16},{16,12},{20,8},{24,4},{28,0},{1,29},{... | collective-permute-start | bytes 786440 | tf_op jit(solution)/shard_map/ppermute | solution.py:269
  8.7 18.8 %collective-permute-start.2 = (f32[256,256]{1,0:T(8,128)S(1)}, f32[256,256]{1,0:T(8,128)S(1)}, u32[]{:S(2)}, u32[]{:S(2)}) collective-permute-start(f32[256,256]{1,0:T(8,128)S(1)} %get-tuple-element.29), channel_id=1, source_target_pairs={{0,4},{4,0},{8,12},{12,8},{16,20},{20,16},{24,28},{28,24},{1,5},{5... | collective-permute-start | bytes 786440 | tf_op jit(solution)/shard_map/ppermute | solution.py:269
  9.3 19.8 %collective-permute-start.3 = (f32[256,256]{1,0:T(8,128)S(1)}, f32[256,256]{1,0:T(8,128)S(1)}, u32[]{:S(2)}, u32[]{:S(2)}) collective-permute-start(f32[256,256]{1,0:T(8,128)S(1)} %get-tuple-element.30), channel_id=1, source_target_pairs={{0,24},{4,28},{8,16},{12,20},{16,8},{20,12},{24,0},{28,4},{1,25},{... | collective-permute-start | bytes 786440 | tf_op jit(solution)/shard_map/ppermute | solution.py:269
  9.4 20.7 %collective-permute-start.4 = (f32[256,256]{1,0:T(8,128)S(1)}, f32[256,256]{1,0:T(8,128)S(1)}, u32[]{:S(2)}, u32[]{:S(2)}) collective-permute-start(f32[256,256]{1,0:T(8,128)S(1)} %get-tuple-element.33), channel_id=1, source_target_pairs={{0,8},{4,12},{8,0},{12,4},{16,24},{20,28},{24,16},{28,20},{1,9},{5... | collective-permute-start | bytes 786440 | tf_op jit(solution)/shard_map/ppermute | solution.py:269
  9.4 21.8 %collective-permute-start.5 = (f32[256,256]{1,0:T(8,128)S(1)}, f32[256,256]{1,0:T(8,128)S(1)}, u32[]{:S(2)}, u32[]{:S(2)}) collective-permute-start(f32[256,256]{1,0:T(8,128)S(1)} %get-tuple-element.34), channel_id=1, source_target_pairs={{0,12},{4,8},{8,4},{12,0},{16,28},{20,24},{24,20},{28,16},{1,13},{... | collective-permute-start | bytes 786440 | tf_op jit(solution)/shard_map/ppermute | solution.py:269
  13.8 33.4 %collective-permute-start.6 = (f32[256,256]{1,0:T(8,128)S(1)}, f32[256,256]{1,0:T(8,128)S(1)}, u32[]{:S(2)}, u32[]{:S(2)}) collective-permute-start(f32[256,256]{1,0:T(8,128)S(1)} %get-tuple-element.37), channel_id=1, source_target_pairs={{0,20},{4,16},{8,28},{12,24},{16,4},{20,0},{24,12},{28,8},{1,21},{... | collective-permute-start | bytes 786440 | tf_op jit(solution)/shard_map/ppermute | solution.py:269
  27.5 0.7 copy-start.2
  27.5 0.7 copy-start.3
  27.5 24.3 %collective-permute-start = (f32[256,256]{1,0:T(8,128)S(1)}, f32[256,256]{1,0:T(8,128)S(1)}, u32[]{:S(2)}, u32[]{:S(2)}) collective-permute-start(f32[256,256]{1,0:T(8,128)S(1)} %get-tuple-element.25), channel_id=1, source_target_pairs={{0,16},{4,20},{8,24},{12,28},{16,0},{20,4},{24,8},{28,12},{1,17},{... | collective-permute-start | bytes 786440 | tf_op jit(solution)/shard_map/ppermute | solution.py:269
  47.2 4.7 %copy-start.1 = (bf16[1536,256]{1,0:T(8,128)(2,1)S(1)}, bf16[1536,256]{1,0:T(8,128)(2,1)}, u32[]{:S(2)}) copy-start(bf16[1536,256]{1,0:T(8,128)(2,1)} %constant.11.clone.refs_0_) | copy-start | bytes 2359300
  65.7 1.2 %collective-permute-start.7 = (f32[16,1,128]{2,1,0:T(1,128)S(1)}, f32[16,1,128]{2,1,0:T(1,128)S(1)}, u32[]{:S(2)}, u32[]{:S(2)}) collective-permute-start(f32[16,1,128]{2,1,0:T(1,128)S(1)} %slice.8), channel_id=1, source_target_pairs={{0,1},{1,0},{2,3},{3,2},{4,5},{5,4},{6,7},{7,6},{8,9},{9,8},{10,11... | collective-permute-start | bytes 24584 | tf_op jit(solution)/shard_map/ppermute | solution.py:305

commit v6 on v5

--- a/solution.py
+++ b/solution.py
@@ -195,7 +195,7 @@
     for place in range(count):
         block = sums[lag_ref[place], :, :rows]
         for group in range(groups):
-            out_ref[place * ways + way, :, group * rows : (group + 1) * rows] = block[group : group + 1]
+            out_ref[(ways - 1 - way) * count + (count - 1 - place), :, group * rows : (group + 1) * rows] = block[group : group + 1]
 
 
 def gather_kernel(count, groups, rows, inner, owned_ref, out_ref):
@@ -203,7 +203,7 @@
     way = lax.axis_index("ch") // inner
     for place in range(count):
         for group in range(groups):
-            row = owned_ref[place * ways + way, :, group * rows : (group + 1) * rows]
+            row = owned_ref[(ways - 1 - way) * count + (count - 1 - place), :, group * rows : (group + 1) * rows]
             out_ref[place * groups + group : place * groups + group + 1, :] = row
 
 
@@ -268,11 +268,15 @@
         pairs = [(place, partner(count, place, step)) for place in range(count)]
         blocks[step] = lax.ppermute(blocks[step], "seq", pairs)
     batch = max(1, count // 8)
-    arrivals = [near[:batch] + far[:batch]]
-    arrivals.append(near[batch : 2 * batch] + far[batch : 2 * batch])
-    arrivals.append(near[2 * batch :])
-    arrivals.append(far[2 * batch : -batch])
-    arrivals.append(far[-batch:])
+    early, late = far[:-batch], far[-batch:]
+    arrivals = [
+        near[:batch] + early[:batch],
+        near[batch : 2 * batch] + early[batch : 2 * batch],
+        near[2 * batch :],
+        early[2 * batch :],
+        late,
+    ]
+    arrivals = [new for new in arrivals if new]
     spectra, olds, carried = [], [], None
     for new in arrivals:
         last = new is arrivals[-1]
@@ -294,7 +298,7 @@
             spectra.append(fresh)
             olds.append(new)
     together = [
-        [place * ways + way * inner + core for place in range(count) for way in range(outer)] for core in range(inner)
+        [place * ways + way * inner + core for way in reversed(range(outer)) for place in reversed(range(count))] for core in range(inner)
     ]
     owned = lax.all_to_all(
         made, ("seq", "ch"), split_axis=0, concat_axis=0, axis_index_groups=together, tiled=True

time: 67.8 us -> 65.6 us (0.968)
  blocking collectives: 12.4 us -> 10.3 us
    all_to_all x1, blocking collectives: 12.4 us -> 10.3 us  [shards(): lax.all_to_all(made, ('seq', 'ch'), split_axis=0, concat_axis=0, axis_ind...]
where the time goes in v6:
time: 65.6 us; the launch traced here: 65.4 us
  starting transfers between devices  23.6 us (36%)
  waiting for transfers between devices  21.9 us (33%)
  blocking collectives  10.3 us (16%)
  Pallas kernels  8.14 us (12%)
  local copies, waits for them, and re-layouts  0.67 us (1%)
  other arithmetic  0.67 us (1%)
    ppermute x7, starting transfers between devices, shards(): blocks[step] = lax.ppermute(blocks[step], 'seq', pairs)  23.6 us
    ppermute x7, waiting for transfers between devices, shards(): blocks[step] = lax.ppermute(blocks[step], 'seq', pairs)  20.8 us
    all_to_all x1, blocking collectives, shards(): lax.all_to_all(made, ('seq', 'ch'), split_axis=0, concat_axis=0, axis_ind...  10.3 us
    pallas_call x5, Pallas kernels, absorb(): pl.pallas_call(functools.partial(absorb_kernel, count, channels, rows, ne...  5.45 us
    pallas_call x2, Pallas kernels, cut(): pl.pallas_call(functools.partial(cut_kernel, count, channels, steps), out...  2.65 us
  transfers between devices with their start and end apart: 8, of which 5 were waited for; matrix products, arithmetic and copies ran while one was open for 0% of the time, Pallas kernels for 9%

profile of v6, /device:TPU:0, one launch (start us, length us, event | category | flops | bytes accessed | tf_op | source)
XLA Modules:
  0.0 65.4 jit_solution(1556793693580151232)
XLA Ops:
  0.0 1.0 %shard_map.100 = f32[256,256]{1,0:T(8,128)S(1)} custom-call(f32[256,1024]{1,0:T(8,128)} %inputs_ref.2, f32[256,1024]{1,0:T(8,128)} %grads_ref.2), custom_call_target="tpu_custom_call" | custom-call | bytes 524288 | tf_op jit(solution)/shard_map/pallas_call | solution.py:76
  1.0 0.0 copy-start
  1.0 6.0 %collective-permute-start.1 = (f32[256,256]{1,0:T(8,128)S(1)}, f32[256,256]{1,0:T(8,128)S(1)}, u32[]{:S(2)}, u32[]{:S(2)}) collective-permute-start(f32[256,256]{1,0:T(8,128)S(1)} %shard_map.100), channel_id=1, source_target_pairs={{0,28},{4,24},{8,20},{12,16},{16,12},{20,8},{24,4},{28,0},{1,29},{... | collective-permute-start | bytes 786440 | tf_op jit(solution)/shard_map/ppermute | solution.py:269
  7.0 1.7 %shard_map.101 = (f32[256,256]{1,0:T(8,128)S(1)}, f32[256,256]{1,0:T(8,128)S(1)}, f32[256,256]{1,0:T(8,128)S(1)}, f32[256,256]{1,0:T(8,128)S(1)}, f32[256,256]{1...) custom-call(f32[256,1024]{1,0:T(8,128)} %inputs_ref.2, f32[256,1024]{1,0:T(8,128)} %grads_ref.2), custom_call_target="tpu_custom_call" | custom-call | bytes 3670016 | tf_op jit(solution)/shard_map/pallas_call | solution.py:76
  8.7 0.6 collective-permute-start.2
  9.3 0.1 collective-permute-start.3
  9.4 0.0 collective-permute-start.4
  9.4 3.1 %collective-permute-start.5 = (f32[256,256]{1,0:T(8,128)S(1)}, f32[256,256]{1,0:T(8,128)S(1)}, u32[]{:S(2)}, u32[]{:S(2)}) collective-permute-start(f32[256,256]{1,0:T(8,128)S(1)} %get-tuple-element.34), channel_id=1, source_target_pairs={{0,12},{4,8},{8,4},{12,0},{16,28},{20,24},{24,20},{28,16},{1,13},{... | collective-permute-start | bytes 786440 | tf_op jit(solution)/shard_map/ppermute | solution.py:269
  12.5 1.3 %collective-permute-done.1.refs_1_ = f32[256,256]{1,0:T(8,128)S(1)} collective-permute-done((f32[256,256]{1,0:T(8,128)S(1)}, f32[256,256]{1,0:T(8,128)S(1)}, u32[]{:S(2)}, u32[]{:S(2)}) %collective-permute-start.1) | collective-permute-done | bytes 262176 | tf_op jit(solution)/shard_map/ppermute | solution.py:269
  13.8 13.7 %collective-permute-start.6 = (f32[256,256]{1,0:T(8,128)S(1)}, f32[256,256]{1,0:T(8,128)S(1)}, u32[]{:S(2)}, u32[]{:S(2)}) collective-permute-start(f32[256,256]{1,0:T(8,128)S(1)} %get-tuple-element.37), channel_id=1, source_target_pairs={{0,20},{4,16},{8,28},{12,24},{16,4},{20,0},{24,12},{28,8},{1,21},{... | collective-permute-start | bytes 786440 | tf_op jit(solution)/shard_map/ppermute | solution.py:269
  27.5 0.0 collective-permute-done.2.refs_0_
  27.5 0.0 copy-start.2
  27.5 0.0 copy-start.3
  27.5 0.0 collective-permute-start
  27.6 0.0 copy-done
  27.6 0.6 copy-done.2
  28.2 0.0 copy-done.3
  28.2 0.9 %shard_map.102 = (f32[8,8,512]{2,1,0:T(8,128)S(1)}, f32[2,256,512]{2,1,0:T(8,128)S(1)}) custom-call(s32[8]{0:T(128)S(1)} %copy-done.2, s32[8]{0:T(128)S(1)} %copy-done.3, bf16[768,512]{1,0:T(8,128)(2,1)S(1)} %copy-done, f32[256,256]{1,0:T(8,128)S(1)} %get-tuple-element.26.refs_0_, f32[256,256]{1,0:T(8,128)S(1)} %collective-permute-done.1.refs_1_), custom_call_target="tpu_custom_call" | custom-call | flops 402653184 | bytes 1572864 | tf_op jit(solution)/shard_map/pallas_call | solution.py:232
  29.1 0.0 collective-permute-done.3.refs_1_
  29.1 1.0 %shard_map.103 = (f32[8,8,512]{2,1,0:T(8,128)S(1)}, f32[2,256,512]{2,1,0:T(8,128)S(1)}) custom-call(s32[8]{0:T(128)S(1)} %copy-done.2, s32[8]{0:T(128)S(1)} %copy-done.3, bf16[768,512]{1,0:T(8,128)(2,1)S(1)} %copy-done, f32[256,256]{1,0:T(8,128)S(1)} %collective-permute-done.2.refs_0_, f32[256,256]{1,0:T(8,128)S(1)} %collective-permute-done.3.refs_1_, ...), custom_call_target="tpu_custom_call" | custom-call | flops 402653184 | bytes 1572864 | tf_op jit(solution)/shard_map/pallas_call | solution.py:232
  30.1 0.0 collective-permute-done.4.refs_0_
  30.2 1.1 %collective-permute-done.5.refs_1_ = f32[256,256]{1,0:T(8,128)S(1)} collective-permute-done((f32[256,256]{1,0:T(8,128)S(1)}, f32[256,256]{1,0:T(8,128)S(1)}, u32[]{:S(2)}, u32[]{:S(2)}) %collective-permute-start.5) | collective-permute-done | bytes 262176 | tf_op jit(solution)/shard_map/ppermute | solution.py:269
  31.2 1.3 %shard_map.104 = (f32[8,8,512]{2,1,0:T(8,128)S(1)}, f32[2,256,512]{2,1,0:T(8,128)S(1)}) custom-call(s32[8]{0:T(128)S(1)} %copy-done.2, s32[8]{0:T(128)S(1)} %copy-done.3, bf16[768,512]{1,0:T(8,128)(2,1)S(1)} %copy-done, f32[256,256]{1,0:T(8,128)S(1)} %collective-permute-done.4.refs_0_, f32[256,256]{1,0:T(8,128)S(1)} %collective-permute-done.5.refs_1_, ...), custom_call_target="tpu_custom_call" | custom-call | flops 402653184 | bytes 1572864 | tf_op jit(solution)/shard_map/pallas_call | solution.py:232
  32.5 14.7 %collective-permute-done.6.refs_0_ = f32[256,256]{1,0:T(8,128)S(1)} collective-permute-done((f32[256,256]{1,0:T(8,128)S(1)}, f32[256,256]{1,0:T(8,128)S(1)}, u32[]{:S(2)}, u32[]{:S(2)}) %collective-permute-start.6) | collective-permute-done | bytes 262176 | tf_op jit(solution)/shard_map/ppermute | solution.py:269
  47.2 0.9 %shard_map.105 = (f32[8,8,512]{2,1,0:T(8,128)S(1)}, f32[1,256,512]{2,1,0:T(8,128)S(1)}) custom-call(s32[8]{0:T(128)S(1)} %copy-done.2, s32[8]{0:T(128)S(1)} %copy-done.3, bf16[768,512]{1,0:T(8,128)(2,1)S(1)} %copy-done, f32[256,256]{1,0:T(8,128)S(1)} %collective-permute-done.6.refs_0_, f32[2,256,512]{2,1,0:T(8,128)S(1)} %get-tuple-element.28.refs_2_.refs_1_, ...), custom_call_target="tpu_custom_call" | custom-call | flops 201326592 | bytes 786432 | tf_op jit(solution)/shard_map/pallas_call | solution.py:232
  48.1 3.7 %collective-permute-done.refs_1_ = f32[256,256]{1,0:T(8,128)S(1)} collective-permute-done((f32[256,256]{1,0:T(8,128)S(1)}, f32[256,256]{1,0:T(8,128)S(1)}, u32[]{:S(2)}, u32[]{:S(2)}) %collective-permute-start) | collective-permute-done | bytes 262176 | tf_op jit(solution)/shard_map/ppermute | solution.py:269
  51.8 0.0 copy-done.1
  51.8 1.4 %shard_map.106 = f32[16,1,2176]{2,1,0:T(1,128)S(1)} custom-call(s32[8]{0:T(128)S(1)} %copy-done.2, s32[8]{0:T(128)S(1)} %copy-done.3, bf16[768,512]{1,0:T(8,128)(2,1)S(1)} %copy-done, bf16[1536,256]{1,0:T(8,128)(2,1)S(1)} %copy-done.1, f32[256,256]{1,0:T(8,128)S(1)} %collective-permute-done.refs_1_, f32[2,256,512]{2,1,0:T(8,128)S(1)} %get-tuple-element.28.refs_2_.refs_1_, ...), custom_call_target="tpu_custom_call" | custom-call | flops 201326592 | bytes 786432 | tf_op jit(solution)/shard_map/pallas_call | solution.py:232
  53.2 10.3 %all_to_all.5.owned_ref = f32[16,1,2176]{2,1,0:T(1,128)S(1)} all-to-all(f32[16,1,2176]{2,1,0:T(1,128)S(1)} %shard_map.106), channel_id=1, replica_groups={{30,26,22,18,14,10,6,2,28,24,20,16,12,8,4,0},{31,27,23,19,15,11,7,3,29,..., dimensions={0} | all-to-all | bytes 278528 | tf_op jit(solution)/shard_map/all_to_all | solution.py:303
  63.5 0.0 collective-permute-start.7
  63.6 1.1 %collective-permute-done.7 = f32[16,1,128]{2,1,0:T(1,128)S(1)} collective-permute-done((f32[16,1,128]{2,1,0:T(1,128)S(1)}, f32[16,1,128]{2,1,0:T(1,128)S(1)}, u32[]{:S(2)}, u32[]{:S(2)}) %collective-permute-start.7) | collective-permute-done | bytes 8224 | tf_op jit(solution)/shard_map/ppermute | solution.py:309
  64.8 0.6 broadcast_multiply_fusion
  (4 shorter events, 0.1 us)
Async XLA Ops:
  1.0 26.6 %copy-start = (bf16[768,512]{1,0:T(8,128)(2,1)S(1)}, bf16[768,512]{1,0:T(8,128)(2,1)}, u32[]{:S(2)}) copy-start(bf16[768,512]{1,0:T(8,128)(2,1)} %constant.10.clone.forward_ref) | copy-start | bytes 2359300
  1.0 12.8 %collective-permute-start.1 = (f32[256,256]{1,0:T(8,128)S(1)}, f32[256,256]{1,0:T(8,128)S(1)}, u32[]{:S(2)}, u32[]{:S(2)}) collective-permute-start(f32[256,256]{1,0:T(8,128)S(1)} %shard_map.100), channel_id=1, source_target_pairs={{0,28},{4,24},{8,20},{12,16},{16,12},{20,8},{24,4},{28,0},{1,29},{... | collective-permute-start | bytes 786440 | tf_op jit(solution)/shard_map/ppermute | solution.py:269
  8.7 18.8 %collective-permute-start.2 = (f32[256,256]{1,0:T(8,128)S(1)}, f32[256,256]{1,0:T(8,128)S(1)}, u32[]{:S(2)}, u32[]{:S(2)}) collective-permute-start(f32[256,256]{1,0:T(8,128)S(1)} %get-tuple-element.29), channel_id=1, source_target_pairs={{0,4},{4,0},{8,12},{12,8},{16,20},{20,16},{24,28},{28,24},{1,5},{5... | collective-permute-start | bytes 786440 | tf_op jit(solution)/shard_map/ppermute | solution.py:269
  9.3 19.8 %collective-permute-start.3 = (f32[256,256]{1,0:T(8,128)S(1)}, f32[256,256]{1,0:T(8,128)S(1)}, u32[]{:S(2)}, u32[]{:S(2)}) collective-permute-start(f32[256,256]{1,0:T(8,128)S(1)} %get-tuple-element.30), channel_id=1, source_target_pairs={{0,24},{4,28},{8,16},{12,20},{16,8},{20,12},{24,0},{28,4},{1,25},{... | collective-permute-start | bytes 786440 | tf_op jit(solution)/shard_map/ppermute | solution.py:269
  9.4 20.7 %collective-permute-start.4 = (f32[256,256]{1,0:T(8,128)S(1)}, f32[256,256]{1,0:T(8,128)S(1)}, u32[]{:S(2)}, u32[]{:S(2)}) collective-permute-start(f32[256,256]{1,0:T(8,128)S(1)} %get-tuple-element.33), channel_id=1, source_target_pairs={{0,8},{4,12},{8,0},{12,4},{16,24},{20,28},{24,16},{28,20},{1,9},{5... | collective-permute-start | bytes 786440 | tf_op jit(solution)/shard_map/ppermute | solution.py:269
  9.4 21.8 %collective-permute-start.5 = (f32[256,256]{1,0:T(8,128)S(1)}, f32[256,256]{1,0:T(8,128)S(1)}, u32[]{:S(2)}, u32[]{:S(2)}) collective-permute-start(f32[256,256]{1,0:T(8,128)S(1)} %get-tuple-element.34), channel_id=1, source_target_pairs={{0,12},{4,8},{8,4},{12,0},{16,28},{20,24},{24,20},{28,16},{1,13},{... | collective-permute-start | bytes 786440 | tf_op jit(solution)/shard_map/ppermute | solution.py:269
  13.8 33.4 %collective-permute-start.6 = (f32[256,256]{1,0:T(8,128)S(1)}, f32[256,256]{1,0:T(8,128)S(1)}, u32[]{:S(2)}, u32[]{:S(2)}) collective-permute-start(f32[256,256]{1,0:T(8,128)S(1)} %get-tuple-element.37), channel_id=1, source_target_pairs={{0,20},{4,16},{8,28},{12,24},{16,4},{20,0},{24,12},{28,8},{1,21},{... | collective-permute-start | bytes 786440 | tf_op jit(solution)/shard_map/ppermute | solution.py:269
  27.5 0.7 %copy-start.2 = (s32[8]{0:T(128)S(1)}, s32[8]{0:T(128)}, u32[]{:S(2)}) copy-start(s32[8]{0:T(128)} %order_from.9) | copy-start | bytes 100
  27.5 0.7 %copy-start.3 = (s32[8]{0:T(128)S(1)}, s32[8]{0:T(128)}, u32[]{:S(2)}) copy-start(s32[8]{0:T(128)} %lag_from.9) | copy-start | bytes 100
  27.5 24.3 %collective-permute-start = (f32[256,256]{1,0:T(8,128)S(1)}, f32[256,256]{1,0:T(8,128)S(1)}, u32[]{:S(2)}, u32[]{:S(2)}) collective-permute-start(f32[256,256]{1,0:T(8,128)S(1)} %get-tuple-element.25), channel_id=1, source_target_pairs={{0,16},{4,20},{8,24},{12,28},{16,0},{20,4},{24,8},{28,12},{1,17},{... | collective-permute-start | bytes 786440 | tf_op jit(solution)/shard_map/ppermute | solution.py:269
  47.2 4.7 %copy-start.1 = (bf16[1536,256]{1,0:T(8,128)(2,1)S(1)}, bf16[1536,256]{1,0:T(8,128)(2,1)}, u32[]{:S(2)}) copy-start(bf16[1536,256]{1,0:T(8,128)(2,1)} %constant.11.clone.refs_0_) | copy-start | bytes 2359300
  63.5 1.2 %collective-permute-start.7 = (f32[16,1,128]{2,1,0:T(1,128)S(1)}, f32[16,1,128]{2,1,0:T(1,128)S(1)}, u32[]{:S(2)}, u32[]{:S(2)}) collective-permute-start(f32[16,1,128]{2,1,0:T(1,128)S(1)} %slice.8), channel_id=1, source_target_pairs={{0,1},{1,0},{2,3},{3,2},{4,5},{5,4},{6,7},{7,6},{8,9},{9,8},{10,11... | collective-permute-start | bytes 24584 | tf_op jit(solution)/shard_map/ppermute | solution.py:309

commit v7 on v6

--- a/solution.py
+++ b/solution.py
@@ -195,7 +195,8 @@
     for place in range(count):
         block = sums[lag_ref[place], :, :rows]
         for group in range(groups):
-            out_ref[(ways - 1 - way) * count + (count - 1 - place), :, group * rows : (group + 1) * rows] = block[group : group + 1]
+            piece = (ways - 1 - way) * count + (count - 1 - place)
+            out_ref[piece, :, group * rows : (group + 1) * rows] = block[group : group + 1]
 
 
 def gather_kernel(count, groups, rows, inner, owned_ref, out_ref):
@@ -260,7 +261,9 @@
     inner = 2 if ways % 2 == 0 else 1
     outer = ways // inner
     half = max(1, count // 2)
-    far, near = list(range(count - 1, half - 1, -1)), list(range(half))
+    middle, wide = half // 2, count - half
+    far = [half + step for step in dict.fromkeys([wide // 2, *range(1, wide), 0])]
+    near = list(dict.fromkeys([0, *(step for step in range(1, half) if step != middle), middle]))
     first = cut(inputs, out_grads, count, far[:1])
     inputs, out_grads, first = lax.optimization_barrier((inputs, out_grads, first))
     blocks = dict(zip(far + near, first + cut(inputs, out_grads, count, far[1:] + near)))
@@ -298,7 +301,8 @@
             spectra.append(fresh)
             olds.append(new)
     together = [
-        [place * ways + way * inner + core for way in reversed(range(outer)) for place in reversed(range(count))] for core in range(inner)
+        [place * ways + way * inner + core for way in reversed(range(outer)) for place in reversed(range(count))]
+        for core in range(inner)
     ]
     owned = lax.all_to_all(
         made, ("seq", "ch"), split_axis=0, concat_axis=0, axis_index_groups=together, tiled=True

time: 65.6 us -> 64.8 us (0.988)
  starting transfers between devices: 23.6 us -> 19.3 us
  waiting for transfers between devices: 21.9 us -> 26 us
    ppermute x7, starting transfers between devices: 23.6 us -> 19.3 us  [shards(): blocks[step] = lax.ppermute(blocks[step], 'seq', pairs)]
    ppermute x7, waiting for transfers between devices: 20.8 us -> 24.8 us  [shards(): blocks[step] = lax.ppermute(blocks[step], 'seq', pairs)]
  transfers between devices with their start and end apart: 8 -> 8, of which waited for: 5 -> 6; matrix products, arithmetic and copies ran while one was open for 0% -> 0% of each run, Pallas kernels for 9% -> 9%
where the time goes in v7:
time: 64.8 us; the launch traced here: 64.6 us
  waiting for transfers between devices  26 us (40%)
  starting transfers between devices  19.3 us (30%)
  blocking collectives  10.3 us (16%)
  Pallas kernels  8.17 us (13%)
  other arithmetic  0.67 us (1%)
    ppermute x7, waiting for transfers between devices, shards(): blocks[step] = lax.ppermute(blocks[step], 'seq', pairs)  24.8 us
    ppermute x7, starting transfers between devices, shards(): blocks[step] = lax.ppermute(blocks[step], 'seq', pairs)  19.3 us
    all_to_all x1, blocking collectives, shards(): lax.all_to_all(made, ('seq', 'ch'), split_axis=0, concat_axis=0, axis_ind...  10.3 us
    pallas_call x5, Pallas kernels, absorb(): pl.pallas_call(functools.partial(absorb_kernel, count, channels, rows, ne...  5.47 us
    pallas_call x2, Pallas kernels, cut(): pl.pallas_call(functools.partial(cut_kernel, count, channels, steps), out...  2.65 us
  transfers between devices with their start and end apart: 8, of which 6 were waited for; matrix products, arithmetic and copies ran while one was open for 0% of the time, Pallas kernels for 9%

profile of v7, /device:TPU:0, one launch (start us, length us, event | category | flops | bytes accessed | tf_op | source)
XLA Modules:
  0.0 64.6 jit_solution(16543808564242626691)
XLA Ops:
  0.0 1.0 %shard_map.100 = f32[256,256]{1,0:T(8,128)S(1)} custom-call(f32[256,1024]{1,0:T(8,128)} %inputs_ref.2, f32[256,1024]{1,0:T(8,128)} %grads_ref.2), custom_call_target="tpu_custom_call" | custom-call | bytes 524288 | tf_op jit(solution)/shard_map/pallas_call | solution.py:76
  1.0 0.0 copy-start
  1.0 5.1 %collective-permute-start.1 = (f32[256,256]{1,0:T(8,128)S(1)}, f32[256,256]{1,0:T(8,128)S(1)}, u32[]{:S(2)}, u32[]{:S(2)}) collective-permute-start(f32[256,256]{1,0:T(8,128)S(1)} %shard_map.100), channel_id=1, source_target_pairs={{0,24},{4,28},{8,16},{12,20},{16,8},{20,12},{24,0},{28,4},{1,25},{... | collective-permute-start | bytes 786440 | tf_op jit(solution)/shard_map/ppermute | solution.py:272
  6.1 1.7 %shard_map.101 = (f32[256,256]{1,0:T(8,128)S(1)}, f32[256,256]{1,0:T(8,128)S(1)}, f32[256,256]{1,0:T(8,128)S(1)}, f32[256,256]{1,0:T(8,128)S(1)}, f32[256,256]{1...) custom-call(f32[256,1024]{1,0:T(8,128)} %inputs_ref.2, f32[256,1024]{1,0:T(8,128)} %grads_ref.2), custom_call_target="tpu_custom_call" | custom-call | bytes 3670016 | tf_op jit(solution)/shard_map/pallas_call | solution.py:76
  7.8 1.6 %collective-permute-start.2 = (f32[256,256]{1,0:T(8,128)S(1)}, f32[256,256]{1,0:T(8,128)S(1)}, u32[]{:S(2)}, u32[]{:S(2)}) collective-permute-start(f32[256,256]{1,0:T(8,128)S(1)} %get-tuple-element.29), channel_id=1, source_target_pairs={{0,4},{4,0},{8,12},{12,8},{16,20},{20,16},{24,28},{28,24},{1,5},{5... | collective-permute-start | bytes 786440 | tf_op jit(solution)/shard_map/ppermute | solution.py:272
  9.3 0.0 collective-permute-start.3
  9.4 1.7 %collective-permute-start.4 = (f32[256,256]{1,0:T(8,128)S(1)}, f32[256,256]{1,0:T(8,128)S(1)}, u32[]{:S(2)}, u32[]{:S(2)}) collective-permute-start(f32[256,256]{1,0:T(8,128)S(1)} %get-tuple-element.33), channel_id=1, source_target_pairs={{0,12},{4,8},{8,4},{12,0},{16,28},{20,24},{24,20},{28,16},{1,13},{... | collective-permute-start | bytes 786440 | tf_op jit(solution)/shard_map/ppermute | solution.py:272
  11.0 0.7 %collective-permute-start.5 = (f32[256,256]{1,0:T(8,128)S(1)}, f32[256,256]{1,0:T(8,128)S(1)}, u32[]{:S(2)}, u32[]{:S(2)}) collective-permute-start(f32[256,256]{1,0:T(8,128)S(1)} %get-tuple-element.34), channel_id=1, source_target_pairs={{0,8},{4,12},{8,0},{12,4},{16,24},{20,28},{24,16},{28,20},{1,9},{5... | collective-permute-start | bytes 786440 | tf_op jit(solution)/shard_map/ppermute | solution.py:272
  11.7 1.6 %collective-permute-done.1.refs_1_ = f32[256,256]{1,0:T(8,128)S(1)} collective-permute-done((f32[256,256]{1,0:T(8,128)S(1)}, f32[256,256]{1,0:T(8,128)S(1)}, u32[]{:S(2)}, u32[]{:S(2)}) %collective-permute-start.1) | collective-permute-done | bytes 262176 | tf_op jit(solution)/shard_map/ppermute | solution.py:272
  13.4 4.7 %collective-permute-start.6 = (f32[256,256]{1,0:T(8,128)S(1)}, f32[256,256]{1,0:T(8,128)S(1)}, u32[]{:S(2)}, u32[]{:S(2)}) collective-permute-start(f32[256,256]{1,0:T(8,128)S(1)} %get-tuple-element.37), channel_id=1, source_target_pairs={{0,28},{4,24},{8,20},{12,16},{16,12},{20,8},{24,4},{28,0},{1,29},{... | collective-permute-start | bytes 786440 | tf_op jit(solution)/shard_map/ppermute | solution.py:272
  18.1 3.1 %collective-permute-done.2.refs_0_ = f32[256,256]{1,0:T(8,128)S(1)} collective-permute-done((f32[256,256]{1,0:T(8,128)S(1)}, f32[256,256]{1,0:T(8,128)S(1)}, u32[]{:S(2)}, u32[]{:S(2)}) %collective-permute-start.2) | collective-permute-done | bytes 262176 | tf_op jit(solution)/shard_map/ppermute | solution.py:272
  21.2 0.0 copy-start.2
  21.2 0.0 copy-start.3
  21.2 5.5 %collective-permute-start = (f32[256,256]{1,0:T(8,128)S(1)}, f32[256,256]{1,0:T(8,128)S(1)}, u32[]{:S(2)}, u32[]{:S(2)}) collective-permute-start(f32[256,256]{1,0:T(8,128)S(1)} %get-tuple-element.25), channel_id=1, source_target_pairs={{0,16},{4,20},{8,24},{12,28},{16,0},{20,4},{24,8},{28,12},{1,17},{... | collective-permute-start | bytes 786440 | tf_op jit(solution)/shard_map/ppermute | solution.py:272
  26.7 0.0 copy-done
  26.7 0.0 copy-done.2
  26.7 0.0 copy-done.3
  26.7 0.9 %shard_map.102 = (f32[8,8,512]{2,1,0:T(8,128)S(1)}, f32[2,256,512]{2,1,0:T(8,128)S(1)}) custom-call(s32[8]{0:T(128)S(1)} %copy-done.2, s32[8]{0:T(128)S(1)} %copy-done.3, bf16[768,512]{1,0:T(8,128)(2,1)S(1)} %copy-done, f32[256,256]{1,0:T(8,128)S(1)} %get-tuple-element.26.refs_0_, f32[256,256]{1,0:T(8,128)S(1)} %collective-permute-done.1.refs_1_), custom_call_target="tpu_custom_call" | custom-call | flops 402653184 | bytes 1572864 | tf_op jit(solution)/shard_map/pallas_call | solution.py:233
  27.6 2.7 %collective-permute-done.3.refs_1_ = f32[256,256]{1,0:T(8,128)S(1)} collective-permute-done((f32[256,256]{1,0:T(8,128)S(1)}, f32[256,256]{1,0:T(8,128)S(1)}, u32[]{:S(2)}, u32[]{:S(2)}) %collective-permute-start.3) | collective-permute-done | bytes 262176 | tf_op jit(solution)/shard_map/ppermute | solution.py:272
  30.4 1.0 %shard_map.103 = (f32[8,8,512]{2,1,0:T(8,128)S(1)}, f32[2,256,512]{2,1,0:T(8,128)S(1)}) custom-call(s32[8]{0:T(128)S(1)} %copy-done.2, s32[8]{0:T(128)S(1)} %copy-done.3, bf16[768,512]{1,0:T(8,128)(2,1)S(1)} %copy-done, f32[256,256]{1,0:T(8,128)S(1)} %collective-permute-done.2.refs_0_, f32[256,256]{1,0:T(8,128)S(1)} %collective-permute-done.3.refs_1_, ...), custom_call_target="tpu_custom_call" | custom-call | flops 402653184 | bytes 1572864 | tf_op jit(solution)/shard_map/pallas_call | solution.py:233
  31.4 0.0 collective-permute-done.4.refs_0_
  31.4 0.0 collective-permute-done.5.refs_1_
  31.4 1.3 %shard_map.104 = (f32[8,8,512]{2,1,0:T(8,128)S(1)}, f32[2,256,512]{2,1,0:T(8,128)S(1)}) custom-call(s32[8]{0:T(128)S(1)} %copy-done.2, s32[8]{0:T(128)S(1)} %copy-done.3, bf16[768,512]{1,0:T(8,128)(2,1)S(1)} %copy-done, f32[256,256]{1,0:T(8,128)S(1)} %collective-permute-done.4.refs_0_, f32[256,256]{1,0:T(8,128)S(1)} %collective-permute-done.5.refs_1_, ...), custom_call_target="tpu_custom_call" | custom-call | flops 402653184 | bytes 1572864 | tf_op jit(solution)/shard_map/pallas_call | solution.py:233
  32.7 6.4 %collective-permute-done.6.refs_0_ = f32[256,256]{1,0:T(8,128)S(1)} collective-permute-done((f32[256,256]{1,0:T(8,128)S(1)}, f32[256,256]{1,0:T(8,128)S(1)}, u32[]{:S(2)}, u32[]{:S(2)}) %collective-permute-start.6) | collective-permute-done | bytes 262176 | tf_op jit(solution)/shard_map/ppermute | solution.py:272
  39.1 0.9 %shard_map.105 = (f32[8,8,512]{2,1,0:T(8,128)S(1)}, f32[1,256,512]{2,1,0:T(8,128)S(1)}) custom-call(s32[8]{0:T(128)S(1)} %copy-done.2, s32[8]{0:T(128)S(1)} %copy-done.3, bf16[768,512]{1,0:T(8,128)(2,1)S(1)} %copy-done, f32[256,256]{1,0:T(8,128)S(1)} %collective-permute-done.6.refs_0_, f32[2,256,512]{2,1,0:T(8,128)S(1)} %get-tuple-element.28.refs_2_.refs_1_, ...), custom_call_target="tpu_custom_call" | custom-call | flops 201326592 | bytes 786432 | tf_op jit(solution)/shard_map/pallas_call | solution.py:233
  40.0 10.9 %collective-permute-done.refs_1_ = f32[256,256]{1,0:T(8,128)S(1)} collective-permute-done((f32[256,256]{1,0:T(8,128)S(1)}, f32[256,256]{1,0:T(8,128)S(1)}, u32[]{:S(2)}, u32[]{:S(2)}) %collective-permute-start) | collective-permute-done | bytes 262176 | tf_op jit(solution)/shard_map/ppermute | solution.py:272
  50.9 0.0 copy-done.1
  51.0 1.4 %shard_map.106 = f32[16,1,2176]{2,1,0:T(1,128)S(1)} custom-call(s32[8]{0:T(128)S(1)} %copy-done.2, s32[8]{0:T(128)S(1)} %copy-done.3, bf16[768,512]{1,0:T(8,128)(2,1)S(1)} %copy-done, bf16[1536,256]{1,0:T(8,128)(2,1)S(1)} %copy-done.1, f32[256,256]{1,0:T(8,128)S(1)} %collective-permute-done.refs_1_, f32[2,256,512]{2,1,0:T(8,128)S(1)} %get-tuple-element.28.refs_2_.refs_1_, ...), custom_call_target="tpu_custom_call" | custom-call | flops 201326592 | bytes 786432 | tf_op jit(solution)/shard_map/pallas_call | solution.py:233
  52.3 10.3 %all_to_all.5.owned_ref = f32[16,1,2176]{2,1,0:T(1,128)S(1)} all-to-all(f32[16,1,2176]{2,1,0:T(1,128)S(1)} %shard_map.106), channel_id=1, replica_groups={{30,26,22,18,14,10,6,2,28,24,20,16,12,8,4,0},{31,27,23,19,15,11,7,3,29,..., dimensions={0} | all-to-all | bytes 278528 | tf_op jit(solution)/shard_map/all_to_all | solution.py:307
  62.7 0.0 collective-permute-start.7
  62.7 1.1 %collective-permute-done.7 = f32[16,1,128]{2,1,0:T(1,128)S(1)} collective-permute-done((f32[16,1,128]{2,1,0:T(1,128)S(1)}, f32[16,1,128]{2,1,0:T(1,128)S(1)}, u32[]{:S(2)}, u32[]{:S(2)}) %collective-permute-start.7) | collective-permute-done | bytes 8224 | tf_op jit(solution)/shard_map/ppermute | solution.py:313
  64.0 0.6 broadcast_multiply_fusion
  (4 shorter events, 0.1 us)
Async XLA Ops:
  1.0 25.7 %copy-start = (bf16[768,512]{1,0:T(8,128)(2,1)S(1)}, bf16[768,512]{1,0:T(8,128)(2,1)}, u32[]{:S(2)}) copy-start(bf16[768,512]{1,0:T(8,128)(2,1)} %constant.10.clone.forward_ref) | copy-start | bytes 2359300
  1.0 12.3 %collective-permute-start.1 = (f32[256,256]{1,0:T(8,128)S(1)}, f32[256,256]{1,0:T(8,128)S(1)}, u32[]{:S(2)}, u32[]{:S(2)}) collective-permute-start(f32[256,256]{1,0:T(8,128)S(1)} %shard_map.100), channel_id=1, source_target_pairs={{0,24},{4,28},{8,16},{12,20},{16,8},{20,12},{24,0},{28,4},{1,25},{... | collective-permute-start | bytes 786440 | tf_op jit(solution)/shard_map/ppermute | solution.py:272
  7.8 13.4 %collective-permute-start.2 = (f32[256,256]{1,0:T(8,128)S(1)}, f32[256,256]{1,0:T(8,128)S(1)}, u32[]{:S(2)}, u32[]{:S(2)}) collective-permute-start(f32[256,256]{1,0:T(8,128)S(1)} %get-tuple-element.29), channel_id=1, source_target_pairs={{0,4},{4,0},{8,12},{12,8},{16,20},{20,16},{24,28},{28,24},{1,5},{5... | collective-permute-start | bytes 786440 | tf_op jit(solution)/shard_map/ppermute | solution.py:272
  9.3 21.0 %collective-permute-start.3 = (f32[256,256]{1,0:T(8,128)S(1)}, f32[256,256]{1,0:T(8,128)S(1)}, u32[]{:S(2)}, u32[]{:S(2)}) collective-permute-start(f32[256,256]{1,0:T(8,128)S(1)} %get-tuple-element.30), channel_id=1, source_target_pairs={{0,20},{4,16},{8,28},{12,24},{16,4},{20,0},{24,12},{28,8},{1,21},{... | collective-permute-start | bytes 786440 | tf_op jit(solution)/shard_map/ppermute | solution.py:272
  9.4 22.1 %collective-permute-start.4 = (f32[256,256]{1,0:T(8,128)S(1)}, f32[256,256]{1,0:T(8,128)S(1)}, u32[]{:S(2)}, u32[]{:S(2)}) collective-permute-start(f32[256,256]{1,0:T(8,128)S(1)} %get-tuple-element.33), channel_id=1, source_target_pairs={{0,12},{4,8},{8,4},{12,0},{16,28},{20,24},{24,20},{28,16},{1,13},{... | collective-permute-start | bytes 786440 | tf_op jit(solution)/shard_map/ppermute | solution.py:272
  11.0 20.4 %collective-permute-start.5 = (f32[256,256]{1,0:T(8,128)S(1)}, f32[256,256]{1,0:T(8,128)S(1)}, u32[]{:S(2)}, u32[]{:S(2)}) collective-permute-start(f32[256,256]{1,0:T(8,128)S(1)} %get-tuple-element.34), channel_id=1, source_target_pairs={{0,8},{4,12},{8,0},{12,4},{16,24},{20,28},{24,16},{28,20},{1,9},{5... | collective-permute-start | bytes 786440 | tf_op jit(solution)/shard_map/ppermute | solution.py:272
  13.4 25.7 %collective-permute-start.6 = (f32[256,256]{1,0:T(8,128)S(1)}, f32[256,256]{1,0:T(8,128)S(1)}, u32[]{:S(2)}, u32[]{:S(2)}) collective-permute-start(f32[256,256]{1,0:T(8,128)S(1)} %get-tuple-element.37), channel_id=1, source_target_pairs={{0,28},{4,24},{8,20},{12,16},{16,12},{20,8},{24,4},{28,0},{1,29},{... | collective-permute-start | bytes 786440 | tf_op jit(solution)/shard_map/ppermute | solution.py:272
  21.2 5.5 %copy-start.2 = (s32[8]{0:T(128)S(1)}, s32[8]{0:T(128)}, u32[]{:S(2)}) copy-start(s32[8]{0:T(128)} %order_from.9) | copy-start | bytes 100
  21.2 5.5 %copy-start.3 = (s32[8]{0:T(128)S(1)}, s32[8]{0:T(128)}, u32[]{:S(2)}) copy-start(s32[8]{0:T(128)} %lag_from.9) | copy-start | bytes 100
  21.2 29.7 %collective-permute-start = (f32[256,256]{1,0:T(8,128)S(1)}, f32[256,256]{1,0:T(8,128)S(1)}, u32[]{:S(2)}, u32[]{:S(2)}) collective-permute-start(f32[256,256]{1,0:T(8,128)S(1)} %get-tuple-element.25), channel_id=1, source_target_pairs={{0,16},{4,20},{8,24},{12,28},{16,0},{20,4},{24,8},{28,12},{1,17},{... | collective-permute-start | bytes 786440 | tf_op jit(solution)/shard_map/ppermute | solution.py:272
  39.1 11.9 %copy-start.1 = (bf16[1536,256]{1,0:T(8,128)(2,1)S(1)}, bf16[1536,256]{1,0:T(8,128)(2,1)}, u32[]{:S(2)}) copy-start(bf16[1536,256]{1,0:T(8,128)(2,1)} %constant.11.clone.refs_0_) | copy-start | bytes 2359300
  62.7 1.2 %collective-permute-start.7 = (f32[16,1,128]{2,1,0:T(1,128)S(1)}, f32[16,1,128]{2,1,0:T(1,128)S(1)}, u32[]{:S(2)}, u32[]{:S(2)}) collective-permute-start(f32[16,1,128]{2,1,0:T(1,128)S(1)} %slice.8), channel_id=1, source_target_pairs={{0,1},{1,0},{2,3},{3,2},{4,5},{5,4},{6,7},{7,6},{8,9},{9,8},{10,11... | collective-permute-start | bytes 24584 | tf_op jit(solution)/shard_map/ppermute | solution.py:313

commit v8 on v7

--- a/solution.py
+++ b/solution.py
@@ -41,6 +41,13 @@
     if count & (count - 1) == 0:
         return place ^ step
     return (place - step if back else place + step) % count
+
+
+def turns(count):
+    quarter = max(1, count // 4)
+    quarters = [list(range(first, min(first + quarter, count)))[::-1] for first in range(0, count, quarter)]
+    middle = quarters[1:-1][::-1]
+    return [place for part in middle + quarters[:0:-1][:1] + quarters[:1] for place in part]
 
 
 def cut_kernel(count, channels, steps, inputs_ref, grads_ref, *refs):
@@ -195,7 +202,7 @@
     for place in range(count):
         block = sums[lag_ref[place], :, :rows]
         for group in range(groups):
-            piece = (ways - 1 - way) * count + (count - 1 - place)
+            piece = turns(count).index(place) * ways + ways - 1 - way
             out_ref[piece, :, group * rows : (group + 1) * rows] = block[group : group + 1]
 
 
@@ -204,7 +211,7 @@
     way = lax.axis_index("ch") // inner
     for place in range(count):
         for group in range(groups):
-            row = owned_ref[(ways - 1 - way) * count + (count - 1 - place), :, group * rows : (group + 1) * rows]
+            row = owned_ref[turns(count).index(place) * ways + ways - 1 - way, :, group * rows : (group + 1) * rows]
             out_ref[place * groups + group : place * groups + group + 1, :] = row
 
 
@@ -301,7 +308,7 @@
             spectra.append(fresh)
             olds.append(new)
     together = [
-        [place * ways + way * inner + core for way in reversed(range(outer)) for place in reversed(range(count))]
+        [place * ways + way * inner + core for place in turns(count) for way in reversed(range(outer))]
         for core in range(inner)
     ]
     owned = lax.all_to_all(

time: 64.8 us -> 64.4 us (level)
  no operation moved by 1% of the time
where the time goes in v8:
time: 64.4 us; the launch traced here: 64.2 us
  waiting for transfers between devices  26 us (40%)
  starting transfers between devices  19.3 us (30%)
  blocking collectives  9.95 us (15%)
  Pallas kernels  8.17 us (13%)
  other arithmetic  0.67 us (1%)
    ppermute x7, waiting for transfers between devices, shards(): blocks[step] = lax.ppermute(blocks[step], 'seq', pairs)  24.8 us
    ppermute x7, starting transfers between devices, shards(): blocks[step] = lax.ppermute(blocks[step], 'seq', pairs)  19.3 us
    all_to_all x1, blocking collectives, shards(): lax.all_to_all(made, ('seq', 'ch'), split_axis=0, concat_axis=0, axis_ind...  9.95 us
    pallas_call x5, Pallas kernels, absorb(): pl.pallas_call(functools.partial(absorb_kernel, count, channels, rows, ne...  5.47 us
    pallas_call x2, Pallas kernels, cut(): pl.pallas_call(functools.partial(cut_kernel, count, channels, steps), out...  2.65 us
  transfers between devices with their start and end apart: 8, of which 6 were waited for; matrix products, arithmetic and copies ran while one was open for 0% of the time, Pallas kernels for 9%

profile of v8, /device:TPU:0, one launch (start us, length us, event | category | flops | bytes accessed | tf_op | source)
XLA Modules:
  0.0 64.2 jit_solution(10205005441327313227)
XLA Ops:
  0.0 1.0 %shard_map.100 = f32[256,256]{1,0:T(8,128)S(1)} custom-call(f32[256,1024]{1,0:T(8,128)} %inputs_ref.2, f32[256,1024]{1,0:T(8,128)} %grads_ref.2), custom_call_target="tpu_custom_call" | custom-call | bytes 524288 | tf_op jit(solution)/shard_map/pallas_call | solution.py:83
  1.0 0.0 copy-start
  1.0 5.1 %collective-permute-start.1 = (f32[256,256]{1,0:T(8,128)S(1)}, f32[256,256]{1,0:T(8,128)S(1)}, u32[]{:S(2)}, u32[]{:S(2)}) collective-permute-start(f32[256,256]{1,0:T(8,128)S(1)} %shard_map.100), channel_id=1, source_target_pairs={{0,24},{4,28},{8,16},{12,20},{16,8},{20,12},{24,0},{28,4},{1,25},{... | collective-permute-start | bytes 786440 | tf_op jit(solution)/shard_map/ppermute | solution.py:279
  6.1 1.7 %shard_map.101 = (f32[256,256]{1,0:T(8,128)S(1)}, f32[256,256]{1,0:T(8,128)S(1)}, f32[256,256]{1,0:T(8,128)S(1)}, f32[256,256]{1,0:T(8,128)S(1)}, f32[256,256]{1...) custom-call(f32[256,1024]{1,0:T(8,128)} %inputs_ref.2, f32[256,1024]{1,0:T(8,128)} %grads_ref.2), custom_call_target="tpu_custom_call" | custom-call | bytes 3670016 | tf_op jit(solution)/shard_map/pallas_call | solution.py:83
  7.8 1.6 %collective-permute-start.2 = (f32[256,256]{1,0:T(8,128)S(1)}, f32[256,256]{1,0:T(8,128)S(1)}, u32[]{:S(2)}, u32[]{:S(2)}) collective-permute-start(f32[256,256]{1,0:T(8,128)S(1)} %get-tuple-element.29), channel_id=1, source_target_pairs={{0,4},{4,0},{8,12},{12,8},{16,20},{20,16},{24,28},{28,24},{1,5},{5... | collective-permute-start | bytes 786440 | tf_op jit(solution)/shard_map/ppermute | solution.py:279
  9.3 0.0 collective-permute-start.3
  9.4 1.7 %collective-permute-start.4 = (f32[256,256]{1,0:T(8,128)S(1)}, f32[256,256]{1,0:T(8,128)S(1)}, u32[]{:S(2)}, u32[]{:S(2)}) collective-permute-start(f32[256,256]{1,0:T(8,128)S(1)} %get-tuple-element.33), channel_id=1, source_target_pairs={{0,12},{4,8},{8,4},{12,0},{16,28},{20,24},{24,20},{28,16},{1,13},{... | collective-permute-start | bytes 786440 | tf_op jit(solution)/shard_map/ppermute | solution.py:279
  11.0 0.7 %collective-permute-start.5 = (f32[256,256]{1,0:T(8,128)S(1)}, f32[256,256]{1,0:T(8,128)S(1)}, u32[]{:S(2)}, u32[]{:S(2)}) collective-permute-start(f32[256,256]{1,0:T(8,128)S(1)} %get-tuple-element.34), channel_id=1, source_target_pairs={{0,8},{4,12},{8,0},{12,4},{16,24},{20,28},{24,16},{28,20},{1,9},{5... | collective-permute-start | bytes 786440 | tf_op jit(solution)/shard_map/ppermute | solution.py:279
  11.7 1.6 %collective-permute-done.1.refs_1_ = f32[256,256]{1,0:T(8,128)S(1)} collective-permute-done((f32[256,256]{1,0:T(8,128)S(1)}, f32[256,256]{1,0:T(8,128)S(1)}, u32[]{:S(2)}, u32[]{:S(2)}) %collective-permute-start.1) | collective-permute-done | bytes 262176 | tf_op jit(solution)/shard_map/ppermute | solution.py:279
  13.4 4.7 %collective-permute-start.6 = (f32[256,256]{1,0:T(8,128)S(1)}, f32[256,256]{1,0:T(8,128)S(1)}, u32[]{:S(2)}, u32[]{:S(2)}) collective-permute-start(f32[256,256]{1,0:T(8,128)S(1)} %get-tuple-element.37), channel_id=1, source_target_pairs={{0,28},{4,24},{8,20},{12,16},{16,12},{20,8},{24,4},{28,0},{1,29},{... | collective-permute-start | bytes 786440 | tf_op jit(solution)/shard_map/ppermute | solution.py:279
  18.1 3.1 %collective-permute-done.2.refs_0_ = f32[256,256]{1,0:T(8,128)S(1)} collective-permute-done((f32[256,256]{1,0:T(8,128)S(1)}, f32[256,256]{1,0:T(8,128)S(1)}, u32[]{:S(2)}, u32[]{:S(2)}) %collective-permute-start.2) | collective-permute-done | bytes 262176 | tf_op jit(solution)/shard_map/ppermute | solution.py:279
  21.2 0.0 copy-start.2
  21.2 0.0 copy-start.3
  21.2 5.5 %collective-permute-start = (f32[256,256]{1,0:T(8,128)S(1)}, f32[256,256]{1,0:T(8,128)S(1)}, u32[]{:S(2)}, u32[]{:S(2)}) collective-permute-start(f32[256,256]{1,0:T(8,128)S(1)} %get-tuple-element.25), channel_id=1, source_target_pairs={{0,16},{4,20},{8,24},{12,28},{16,0},{20,4},{24,8},{28,12},{1,17},{... | collective-permute-start | bytes 786440 | tf_op jit(solution)/shard_map/ppermute | solution.py:279
  26.7 0.0 copy-done
  26.7 0.0 copy-done.2
  26.7 0.0 copy-done.3
  26.7 0.9 %shard_map.102 = (f32[8,8,512]{2,1,0:T(8,128)S(1)}, f32[2,256,512]{2,1,0:T(8,128)S(1)}) custom-call(s32[8]{0:T(128)S(1)} %copy-done.2, s32[8]{0:T(128)S(1)} %copy-done.3, bf16[768,512]{1,0:T(8,128)(2,1)S(1)} %copy-done, f32[256,256]{1,0:T(8,128)S(1)} %get-tuple-element.26.refs_0_, f32[256,256]{1,0:T(8,128)S(1)} %collective-permute-done.1.refs_1_), custom_call_target="tpu_custom_call" | custom-call | flops 402653184 | bytes 1572864 | tf_op jit(solution)/shard_map/pallas_call | solution.py:240
  27.6 2.7 %collective-permute-done.3.refs_1_ = f32[256,256]{1,0:T(8,128)S(1)} collective-permute-done((f32[256,256]{1,0:T(8,128)S(1)}, f32[256,256]{1,0:T(8,128)S(1)}, u32[]{:S(2)}, u32[]{:S(2)}) %collective-permute-start.3) | collective-permute-done | bytes 262176 | tf_op jit(solution)/shard_map/ppermute | solution.py:279
  30.4 1.0 %shard_map.103 = (f32[8,8,512]{2,1,0:T(8,128)S(1)}, f32[2,256,512]{2,1,0:T(8,128)S(1)}) custom-call(s32[8]{0:T(128)S(1)} %copy-done.2, s32[8]{0:T(128)S(1)} %copy-done.3, bf16[768,512]{1,0:T(8,128)(2,1)S(1)} %copy-done, f32[256,256]{1,0:T(8,128)S(1)} %collective-permute-done.2.refs_0_, f32[256,256]{1,0:T(8,128)S(1)} %collective-permute-done.3.refs_1_, ...), custom_call_target="tpu_custom_call" | custom-call | flops 402653184 | bytes 1572864 | tf_op jit(solution)/shard_map/pallas_call | solution.py:240
  31.4 0.0 collective-permute-done.4.refs_0_
  31.4 0.0 collective-permute-done.5.refs_1_
  31.4 1.3 %shard_map.104 = (f32[8,8,512]{2,1,0:T(8,128)S(1)}, f32[2,256,512]{2,1,0:T(8,128)S(1)}) custom-call(s32[8]{0:T(128)S(1)} %copy-done.2, s32[8]{0:T(128)S(1)} %copy-done.3, bf16[768,512]{1,0:T(8,128)(2,1)S(1)} %copy-done, f32[256,256]{1,0:T(8,128)S(1)} %collective-permute-done.4.refs_0_, f32[256,256]{1,0:T(8,128)S(1)} %collective-permute-done.5.refs_1_, ...), custom_call_target="tpu_custom_call" | custom-call | flops 402653184 | bytes 1572864 | tf_op jit(solution)/shard_map/pallas_call | solution.py:240
  32.7 6.4 %collective-permute-done.6.refs_0_ = f32[256,256]{1,0:T(8,128)S(1)} collective-permute-done((f32[256,256]{1,0:T(8,128)S(1)}, f32[256,256]{1,0:T(8,128)S(1)}, u32[]{:S(2)}, u32[]{:S(2)}) %collective-permute-start.6) | collective-permute-done | bytes 262176 | tf_op jit(solution)/shard_map/ppermute | solution.py:279
  39.1 0.9 %shard_map.105 = (f32[8,8,512]{2,1,0:T(8,128)S(1)}, f32[1,256,512]{2,1,0:T(8,128)S(1)}) custom-call(s32[8]{0:T(128)S(1)} %copy-done.2, s32[8]{0:T(128)S(1)} %copy-done.3, bf16[768,512]{1,0:T(8,128)(2,1)S(1)} %copy-done, f32[256,256]{1,0:T(8,128)S(1)} %collective-permute-done.6.refs_0_, f32[2,256,512]{2,1,0:T(8,128)S(1)} %get-tuple-element.28.refs_2_.refs_1_, ...), custom_call_target="tpu_custom_call" | custom-call | flops 201326592 | bytes 786432 | tf_op jit(solution)/shard_map/pallas_call | solution.py:240
  40.0 10.9 %collective-permute-done.refs_1_ = f32[256,256]{1,0:T(8,128)S(1)} collective-permute-done((f32[256,256]{1,0:T(8,128)S(1)}, f32[256,256]{1,0:T(8,128)S(1)}, u32[]{:S(2)}, u32[]{:S(2)}) %collective-permute-start) | collective-permute-done | bytes 262176 | tf_op jit(solution)/shard_map/ppermute | solution.py:279
  50.9 0.0 copy-done.1
  51.0 1.4 %shard_map.106 = f32[16,1,2176]{2,1,0:T(1,128)S(1)} custom-call(s32[8]{0:T(128)S(1)} %copy-done.2, s32[8]{0:T(128)S(1)} %copy-done.3, bf16[768,512]{1,0:T(8,128)(2,1)S(1)} %copy-done, bf16[1536,256]{1,0:T(8,128)(2,1)S(1)} %copy-done.1, f32[256,256]{1,0:T(8,128)S(1)} %collective-permute-done.refs_1_, f32[2,256,512]{2,1,0:T(8,128)S(1)} %get-tuple-element.28.refs_2_.refs_1_, ...), custom_call_target="tpu_custom_call" | custom-call | flops 201326592 | bytes 786432 | tf_op jit(solution)/shard_map/pallas_call | solution.py:240
  52.3 9.9 %all_to_all.5.owned_ref = f32[16,1,2176]{2,1,0:T(1,128)S(1)} all-to-all(f32[16,1,2176]{2,1,0:T(1,128)S(1)} %shard_map.106), channel_id=1, replica_groups={{22,20,18,16,14,12,10,8,30,28,26,24,6,4,2,0},{23,21,19,17,15,13,11,9,31..., dimensions={0} | all-to-all | bytes 278528 | tf_op jit(solution)/shard_map/all_to_all | solution.py:314
  62.3 0.0 collective-permute-start.7
  62.4 1.1 %collective-permute-done.7 = f32[16,1,128]{2,1,0:T(1,128)S(1)} collective-permute-done((f32[16,1,128]{2,1,0:T(1,128)S(1)}, f32[16,1,128]{2,1,0:T(1,128)S(1)}, u32[]{:S(2)}, u32[]{:S(2)}) %collective-permute-start.7) | collective-permute-done | bytes 8224 | tf_op jit(solution)/shard_map/ppermute | solution.py:320
  63.6 0.6 broadcast_multiply_fusion
  (4 shorter events, 0.1 us)
Async XLA Ops:
  1.0 25.7 %copy-start = (bf16[768,512]{1,0:T(8,128)(2,1)S(1)}, bf16[768,512]{1,0:T(8,128)(2,1)}, u32[]{:S(2)}) copy-start(bf16[768,512]{1,0:T(8,128)(2,1)} %constant.10.clone.forward_ref) | copy-start | bytes 2359300
  1.0 12.3 %collective-permute-start.1 = (f32[256,256]{1,0:T(8,128)S(1)}, f32[256,256]{1,0:T(8,128)S(1)}, u32[]{:S(2)}, u32[]{:S(2)}) collective-permute-start(f32[256,256]{1,0:T(8,128)S(1)} %shard_map.100), channel_id=1, source_target_pairs={{0,24},{4,28},{8,16},{12,20},{16,8},{20,12},{24,0},{28,4},{1,25},{... | collective-permute-start | bytes 786440 | tf_op jit(solution)/shard_map/ppermute | solution.py:279
  7.8 13.4 %collective-permute-start.2 = (f32[256,256]{1,0:T(8,128)S(1)}, f32[256,256]{1,0:T(8,128)S(1)}, u32[]{:S(2)}, u32[]{:S(2)}) collective-permute-start(f32[256,256]{1,0:T(8,128)S(1)} %get-tuple-element.29), channel_id=1, source_target_pairs={{0,4},{4,0},{8,12},{12,8},{16,20},{20,16},{24,28},{28,24},{1,5},{5... | collective-permute-start | bytes 786440 | tf_op jit(solution)/shard_map/ppermute | solution.py:279
  9.3 21.0 %collective-permute-start.3 = (f32[256,256]{1,0:T(8,128)S(1)}, f32[256,256]{1,0:T(8,128)S(1)}, u32[]{:S(2)}, u32[]{:S(2)}) collective-permute-start(f32[256,256]{1,0:T(8,128)S(1)} %get-tuple-element.30), channel_id=1, source_target_pairs={{0,20},{4,16},{8,28},{12,24},{16,4},{20,0},{24,12},{28,8},{1,21},{... | collective-permute-start | bytes 786440 | tf_op jit(solution)/shard_map/ppermute | solution.py:279
  9.4 22.1 %collective-permute-start.4 = (f32[256,256]{1,0:T(8,128)S(1)}, f32[256,256]{1,0:T(8,128)S(1)}, u32[]{:S(2)}, u32[]{:S(2)}) collective-permute-start(f32[256,256]{1,0:T(8,128)S(1)} %get-tuple-element.33), channel_id=1, source_target_pairs={{0,12},{4,8},{8,4},{12,0},{16,28},{20,24},{24,20},{28,16},{1,13},{... | collective-permute-start | bytes 786440 | tf_op jit(solution)/shard_map/ppermute | solution.py:279
  11.0 20.4 %collective-permute-start.5 = (f32[256,256]{1,0:T(8,128)S(1)}, f32[256,256]{1,0:T(8,128)S(1)}, u32[]{:S(2)}, u32[]{:S(2)}) collective-permute-start(f32[256,256]{1,0:T(8,128)S(1)} %get-tuple-element.34), channel_id=1, source_target_pairs={{0,8},{4,12},{8,0},{12,4},{16,24},{20,28},{24,16},{28,20},{1,9},{5... | collective-permute-start | bytes 786440 | tf_op jit(solution)/shard_map/ppermute | solution.py:279
  13.4 25.7 %collective-permute-start.6 = (f32[256,256]{1,0:T(8,128)S(1)}, f32[256,256]{1,0:T(8,128)S(1)}, u32[]{:S(2)}, u32[]{:S(2)}) collective-permute-start(f32[256,256]{1,0:T(8,128)S(1)} %get-tuple-element.37), channel_id=1, source_target_pairs={{0,28},{4,24},{8,20},{12,16},{16,12},{20,8},{24,4},{28,0},{1,29},{... | collective-permute-start | bytes 786440 | tf_op jit(solution)/shard_map/ppermute | solution.py:279
  21.2 5.5 %copy-start.2 = (s32[8]{0:T(128)S(1)}, s32[8]{0:T(128)}, u32[]{:S(2)}) copy-start(s32[8]{0:T(128)} %order_from.9) | copy-start | bytes 100
  21.2 5.5 %copy-start.3 = (s32[8]{0:T(128)S(1)}, s32[8]{0:T(128)}, u32[]{:S(2)}) copy-start(s32[8]{0:T(128)} %lag_from.9) | copy-start | bytes 100
  21.2 29.7 %collective-permute-start = (f32[256,256]{1,0:T(8,128)S(1)}, f32[256,256]{1,0:T(8,128)S(1)}, u32[]{:S(2)}, u32[]{:S(2)}) collective-permute-start(f32[256,256]{1,0:T(8,128)S(1)} %get-tuple-element.25), channel_id=1, source_target_pairs={{0,16},{4,20},{8,24},{12,28},{16,0},{20,4},{24,8},{28,12},{1,17},{... | collective-permute-start | bytes 786440 | tf_op jit(solution)/shard_map/ppermute | solution.py:279
  39.1 11.9 %copy-start.1 = (bf16[1536,256]{1,0:T(8,128)(2,1)S(1)}, bf16[1536,256]{1,0:T(8,128)(2,1)}, u32[]{:S(2)}) copy-start(bf16[1536,256]{1,0:T(8,128)(2,1)} %constant.11.clone.refs_0_) | copy-start | bytes 2359300
  62.3 1.2 %collective-permute-start.7 = (f32[16,1,128]{2,1,0:T(1,128)S(1)}, f32[16,1,128]{2,1,0:T(1,128)S(1)}, u32[]{:S(2)}, u32[]{:S(2)}) collective-permute-start(f32[16,1,128]{2,1,0:T(1,128)S(1)} %slice.8), channel_id=1, source_target_pairs={{0,1},{1,0},{2,3},{3,2},{4,5},{5,4},{6,7},{7,6},{8,9},{9,8},{10,11... | collective-permute-start | bytes 24584 | tf_op jit(solution)/shard_map/ppermute | solution.py:320

commit v9 on v8

--- a/solution.py
+++ b/solution.py
@@ -271,12 +271,15 @@
     middle, wide = half // 2, count - half
     far = [half + step for step in dict.fromkeys([wide // 2, *range(1, wide), 0])]
     near = list(dict.fromkeys([0, *(step for step in range(1, half) if step != middle), middle]))
-    first = cut(inputs, out_grads, count, far[:1])
-    inputs, out_grads, first = lax.optimization_barrier((inputs, out_grads, first))
-    blocks = dict(zip(far + near, first + cut(inputs, out_grads, count, far[1:] + near)))
-    for step in far + near[1:]:
-        pairs = [(place, partner(count, place, step)) for place in range(count)]
-        blocks[step] = lax.ppermute(blocks[step], "seq", pairs)
+    def exchange(step, block):
+        return lax.ppermute(block, "seq", [(place, partner(count, place, step)) for place in range(count)])
+
+    start = partner(count, lax.axis_index("seq"), far[0]) * channels
+    halves_of_first = [lax.dynamic_slice_in_dim(whole, start, channels, 1) for whole in (inputs, out_grads)]
+    blocks = dict(zip(far[1:] + near, cut(inputs, out_grads, count, far[1:] + near)))
+    blocks[far[0]] = jnp.concatenate([exchange(far[0], part) for part in halves_of_first], axis=1)
+    for step in far[1:] + near[1:]:
+        blocks[step] = exchange(step, blocks[step])
     batch = max(1, count // 8)
     early, late = far[:-batch], far[-batch:]
     arrivals = [

time: 64.4 us -> 64.4 us (level)
  waiting for transfers between devices: 26 us -> 20.4 us
  starting transfers between devices: 19.3 us -> 23.1 us
  local copies, waits for them, and re-layouts: 0.02 us -> 2.49 us
  Pallas kernels: 8.17 us -> 7.18 us
    ppermute x7 -> x8, waiting for transfers between devices: 24.8 us -> 19.3 us  [exchange(): lax.ppermute(block, 'seq', [(place, partner(count, place, step)) for plac...]
    ppermute x7 -> x8, starting transfers between devices: 19.3 us -> 23.1 us  [exchange(): lax.ppermute(block, 'seq', [(place, partner(count, place, step)) for plac...]
    dynamic_slice x0 -> x2, local copies, waits for them, and re-layouts: none -> 1.83 us  [shards(): lax.dynamic_slice_in_dim(whole, start, channels, 1)]
    pallas_call x2 -> x1, Pallas kernels: 2.65 us -> 1.66 us  [cut(): pl.pallas_call(functools.partial(cut_kernel, count, channels, steps), out...]
  transfers between devices with their start and end apart: 8 -> 9, of which waited for: 6 -> 5; matrix products, arithmetic and copies ran while one was open for 0% -> 1% of each run, Pallas kernels for 9% -> 9%
where the time goes in v9:
time: 64.4 us; the launch traced here: 64.1 us
  starting transfers between devices  23.1 us (36%)
  waiting for transfers between devices  20.4 us (32%)
  blocking collectives  10 us (16%)
  Pallas kernels  7.18 us (11%)
  local copies, waits for them, and re-layouts  2.49 us (4%)
  other arithmetic  0.69 us (1%)
    ppermute x8, starting transfers between devices, exchange(): lax.ppermute(block, 'seq', [(place, partner(count, place, step)) for plac...  23.1 us
    ppermute x8, waiting for transfers between devices, exchange(): lax.ppermute(block, 'seq', [(place, partner(count, place, step)) for plac...  19.3 us
    all_to_all x1, blocking collectives, shards(): lax.all_to_all(made, ('seq', 'ch'), split_axis=0, concat_axis=0, axis_ind...  10 us
    pallas_call x5, Pallas kernels, absorb(): pl.pallas_call(functools.partial(absorb_kernel, count, channels, rows, ne...  5.47 us
    dynamic_slice x2, local copies, waits for them, and re-layouts, shards(): lax.dynamic_slice_in_dim(whole, start, channels, 1)  1.83 us
    pallas_call x1, Pallas kernels, cut(): pl.pallas_call(functools.partial(cut_kernel, count, channels, steps), out...  1.66 us
  transfers between devices with their start and end apart: 9, of which 5 were waited for; matrix products, arithmetic and copies ran while one was open for 1% of the time, Pallas kernels for 9%

profile of v9, /device:TPU:0, one launch (start us, length us, event | category | flops | bytes accessed | tf_op | source)
XLA Modules:
  0.0 64.1 jit_solution(11213786257460995924)
XLA Ops:
  0.0 0.9 %constant_dynamic-slice_fusion = f32[256,128]{1,0:T(8,128)S(1)} fusion(f32[256,1024]{1,0:T(8,128)} %grads_ref.1, s32[]{:T(128)S(6)} %select_n.4), kind=kLoop, calls=%fused_computation.3 | loop fusion | bytes 262148 | tf_op jit(solution)/shard_map/dynamic_slice | solution.py:278
  0.9 5.1 %collective-permute-start.2 = (f32[256,128]{1,0:T(8,128)S(1)}, f32[256,128]{1,0:T(8,128)S(1)}, u32[]{:S(2)}, u32[]{:S(2)}) collective-permute-start(f32[256,128]{1,0:T(8,128)S(1)} %constant_dynamic-slice_fusion), channel_id=1, source_target_pairs={{0,24},{4,28},{8,16},{12,20},{16,8},{20,12},{24,0},{28,4},{1,25},{... | collective-permute-start | bytes 393224 | tf_op jit(solution)/shard_map/ppermute | solution.py:275
  6.0 1.7 %shard_map.100 = (f32[256,256]{1,0:T(8,128)S(1)}, f32[256,256]{1,0:T(8,128)S(1)}, f32[256,256]{1,0:T(8,128)S(1)}, f32[256,256]{1,0:T(8,128)S(1)}, f32[256,256]{1...) custom-call(f32[256,1024]{1,0:T(8,128)} %inputs_ref.1, f32[256,1024]{1,0:T(8,128)} %grads_ref.1), custom_call_target="tpu_custom_call" | custom-call | bytes 3670016 | tf_op jit(solution)/shard_map/pallas_call | solution.py:83
  7.7 0.0 copy-start
  7.7 1.6 %collective-permute-start.3 = (f32[256,256]{1,0:T(8,128)S(1)}, f32[256,256]{1,0:T(8,128)S(1)}, u32[]{:S(2)}, u32[]{:S(2)}) collective-permute-start(f32[256,256]{1,0:T(8,128)S(1)} %get-tuple-element.23), channel_id=1, source_target_pairs={{0,4},{4,0},{8,12},{12,8},{16,20},{20,16},{24,28},{28,24},{1,5},{5... | collective-permute-start | bytes 786440 | tf_op jit(solution)/shard_map/ppermute | solution.py:275
  9.3 0.9 %constant_dynamic-slice_fusion.1 = f32[256,128]{1,0:T(8,128)S(1)} fusion(f32[256,1024]{1,0:T(8,128)} %inputs_ref.1, s32[]{:T(128)S(6)} %select_n.4), kind=kLoop, calls=%fused_computation.4 | loop fusion | bytes 262148 | tf_op jit(solution)/shard_map/dynamic_slice | solution.py:278
  10.2 0.3 collective-permute-start.1
  10.5 0.8 %collective-permute-start.4 = (f32[256,256]{1,0:T(8,128)S(1)}, f32[256,256]{1,0:T(8,128)S(1)}, u32[]{:S(2)}, u32[]{:S(2)}) collective-permute-start(f32[256,256]{1,0:T(8,128)S(1)} %get-tuple-element.24), channel_id=1, source_target_pairs={{0,20},{4,16},{8,28},{12,24},{16,4},{20,0},{24,12},{28,8},{1,21},{... | collective-permute-start | bytes 786440 | tf_op jit(solution)/shard_map/ppermute | solution.py:275
  11.2 4.3 %collective-permute-start.5 = (f32[256,256]{1,0:T(8,128)S(1)}, f32[256,256]{1,0:T(8,128)S(1)}, u32[]{:S(2)}, u32[]{:S(2)}) collective-permute-start(f32[256,256]{1,0:T(8,128)S(1)} %get-tuple-element.27), channel_id=1, source_target_pairs={{0,12},{4,8},{8,4},{12,0},{16,28},{20,24},{24,20},{28,16},{1,13},{... | collective-permute-start | bytes 786440 | tf_op jit(solution)/shard_map/ppermute | solution.py:275
  15.5 0.0 collective-permute-done.2
  15.5 3.0 %collective-permute-start.6 = (f32[256,256]{1,0:T(8,128)S(1)}, f32[256,256]{1,0:T(8,128)S(1)}, u32[]{:S(2)}, u32[]{:S(2)}) collective-permute-start(f32[256,256]{1,0:T(8,128)S(1)} %get-tuple-element.28), channel_id=1, source_target_pairs={{0,8},{4,12},{8,0},{12,4},{16,24},{20,28},{24,16},{28,20},{1,9},{5... | collective-permute-start | bytes 786440 | tf_op jit(solution)/shard_map/ppermute | solution.py:275
  18.6 0.0 collective-permute-done.1
  18.6 6.0 %collective-permute-start.7 = (f32[256,256]{1,0:T(8,128)S(1)}, f32[256,256]{1,0:T(8,128)S(1)}, u32[]{:S(2)}, u32[]{:S(2)}) collective-permute-start(f32[256,256]{1,0:T(8,128)S(1)} %get-tuple-element.31), channel_id=1, source_target_pairs={{0,28},{4,24},{8,20},{12,16},{16,12},{20,8},{24,4},{28,0},{1,29},{... | collective-permute-start | bytes 786440 | tf_op jit(solution)/shard_map/ppermute | solution.py:275
  24.6 0.0 collective-permute-done.3.refs_0_
  24.6 2.1 %collective-permute-start = (f32[256,256]{1,0:T(8,128)S(1)}, f32[256,256]{1,0:T(8,128)S(1)}, u32[]{:S(2)}, u32[]{:S(2)}) collective-permute-start(f32[256,256]{1,0:T(8,128)S(1)} %get-tuple-element.20), channel_id=1, source_target_pairs={{0,16},{4,20},{8,24},{12,28},{16,0},{20,4},{24,8},{28,12},{1,17},{... | collective-permute-start | bytes 786440 | tf_op jit(solution)/shard_map/ppermute | solution.py:275
  26.7 0.0 copy-start.2
  26.7 0.0 copy-start.3
  26.7 0.6 copy-done.2
  27.3 0.0 copy-done.3
  27.3 0.9 %shard_map.101 = (f32[8,8,512]{2,1,0:T(8,128)S(1)}, f32[2,256,512]{2,1,0:T(8,128)S(1)}) custom-call(s32[8]{0:T(128)S(1)} %copy-done.2, s32[8]{0:T(128)S(1)} %copy-done.3, bf16[768,512]{1,0:T(8,128)(2,1)S(1)} %copy-done, f32[256,256]{1,0:T(8,128)S(1)} %get-tuple-element.21.refs_0_, f32[256,256]{1,0:T(8,128)S(1)} %pad_maximum_fusion.refs_1_), custom_call_target="tpu_custom_call" | custom-call | flops 402653184 | bytes 1572864 | tf_op jit(solution)/shard_map/pallas_call | solution.py:240
  28.2 2.1 %collective-permute-done.4.refs_1_ = f32[256,256]{1,0:T(8,128)S(1)} collective-permute-done((f32[256,256]{1,0:T(8,128)S(1)}, f32[256,256]{1,0:T(8,128)S(1)}, u32[]{:S(2)}, u32[]{:S(2)}) %collective-permute-start.4) | collective-permute-done | bytes 262176 | tf_op jit(solution)/shard_map/ppermute | solution.py:275
  30.3 1.1 %shard_map.102 = (f32[8,8,512]{2,1,0:T(8,128)S(1)}, f32[2,256,512]{2,1,0:T(8,128)S(1)}) custom-call(s32[8]{0:T(128)S(1)} %copy-done.2, s32[8]{0:T(128)S(1)} %copy-done.3, bf16[768,512]{1,0:T(8,128)(2,1)S(1)} %copy-done, f32[256,256]{1,0:T(8,128)S(1)} %collective-permute-done.3.refs_0_, f32[256,256]{1,0:T(8,128)S(1)} %collective-permute-done.4.refs_1_, ...), custom_call_target="tpu_custom_call" | custom-call | flops 402653184 | bytes 1572864 | tf_op jit(solution)/shard_map/pallas_call | solution.py:240
  31.3 4.1 %collective-permute-done.6.refs_1_ = f32[256,256]{1,0:T(8,128)S(1)} collective-permute-done((f32[256,256]{1,0:T(8,128)S(1)}, f32[256,256]{1,0:T(8,128)S(1)}, u32[]{:S(2)}, u32[]{:S(2)}) %collective-permute-start.6) | collective-permute-done | bytes 262176 | tf_op jit(solution)/shard_map/ppermute | solution.py:275
  35.4 1.3 %shard_map.103 = (f32[8,8,512]{2,1,0:T(8,128)S(1)}, f32[2,256,512]{2,1,0:T(8,128)S(1)}) custom-call(s32[8]{0:T(128)S(1)} %copy-done.2, s32[8]{0:T(128)S(1)} %copy-done.3, bf16[768,512]{1,0:T(8,128)(2,1)S(1)} %copy-done, f32[256,256]{1,0:T(8,128)S(1)} %collective-permute-done.5.refs_0_, f32[256,256]{1,0:T(8,128)S(1)} %collective-permute-done.6.refs_1_, ...), custom_call_target="tpu_custom_call" | custom-call | flops 402653184 | bytes 1572864 | tf_op jit(solution)/shard_map/pallas_call | solution.py:240
  36.7 4.4 %collective-permute-done.7.refs_0_ = f32[256,256]{1,0:T(8,128)S(1)} collective-permute-done((f32[256,256]{1,0:T(8,128)S(1)}, f32[256,256]{1,0:T(8,128)S(1)}, u32[]{:S(2)}, u32[]{:S(2)}) %collective-permute-start.7) | collective-permute-done | bytes 262176 | tf_op jit(solution)/shard_map/ppermute | solution.py:275
  41.0 0.9 %shard_map.104 = (f32[8,8,512]{2,1,0:T(8,128)S(1)}, f32[1,256,512]{2,1,0:T(8,128)S(1)}) custom-call(s32[8]{0:T(128)S(1)} %copy-done.2, s32[8]{0:T(128)S(1)} %copy-done.3, bf16[768,512]{1,0:T(8,128)(2,1)S(1)} %copy-done, f32[256,256]{1,0:T(8,128)S(1)} %collective-permute-done.7.refs_0_, f32[2,256,512]{2,1,0:T(8,128)S(1)} %get-tuple-element.22.refs_2_.refs_1_, ...), custom_call_target="tpu_custom_call" | custom-call | flops 201326592 | bytes 786432 | tf_op jit(solution)/shard_map/pallas_call | solution.py:240
  42.0 8.9 %collective-permute-done.refs_1_ = f32[256,256]{1,0:T(8,128)S(1)} collective-permute-done((f32[256,256]{1,0:T(8,128)S(1)}, f32[256,256]{1,0:T(8,128)S(1)}, u32[]{:S(2)}, u32[]{:S(2)}) %collective-permute-start) | collective-permute-done | bytes 262176 | tf_op jit(solution)/shard_map/ppermute | solution.py:275
  50.8 1.4 %shard_map.105 = f32[16,1,2176]{2,1,0:T(1,128)S(1)} custom-call(s32[8]{0:T(128)S(1)} %copy-done.2, s32[8]{0:T(128)S(1)} %copy-done.3, bf16[768,512]{1,0:T(8,128)(2,1)S(1)} %copy-done, bf16[1536,256]{1,0:T(8,128)(2,1)S(1)} %copy-done.1, f32[256,256]{1,0:T(8,128)S(1)} %collective-permute-done.refs_1_, f32[2,256,512]{2,1,0:T(8,128)S(1)} %get-tuple-element.22.refs_2_.refs_1_, ...), custom_call_target="tpu_custom_call" | custom-call | flops 201326592 | bytes 786432 | tf_op jit(solution)/shard_map/pallas_call | solution.py:240
  52.2 10.0 %all_to_all.5.owned_ref = f32[16,1,2176]{2,1,0:T(1,128)S(1)} all-to-all(f32[16,1,2176]{2,1,0:T(1,128)S(1)} %shard_map.105), channel_id=1, replica_groups={{22,20,18,16,14,12,10,8,30,28,26,24,6,4,2,0},{23,21,19,17,15,13,11,9,31..., dimensions={0} | all-to-all | bytes 278528 | tf_op jit(solution)/shard_map/all_to_all | solution.py:317
  62.2 0.0 collective-permute-start.8
  62.3 1.1 %collective-permute-done.8 = f32[16,1,128]{2,1,0:T(1,128)S(1)} collective-permute-done((f32[16,1,128]{2,1,0:T(1,128)S(1)}, f32[16,1,128]{2,1,0:T(1,128)S(1)}, u32[]{:S(2)}, u32[]{:S(2)}) %collective-permute-start.8) | collective-permute-done | bytes 8224 | tf_op jit(solution)/shard_map/ppermute | solution.py:323
  63.5 0.6 broadcast_multiply_fusion
  (8 shorter events, 0.1 us)
Async XLA Ops:
  0.9 14.6 %collective-permute-start.2 = (f32[256,128]{1,0:T(8,128)S(1)}, f32[256,128]{1,0:T(8,128)S(1)}, u32[]{:S(2)}, u32[]{:S(2)}) collective-permute-start(f32[256,128]{1,0:T(8,128)S(1)} %constant_dynamic-slice_fusion), channel_id=1, source_target_pairs={{0,24},{4,28},{8,16},{12,20},{16,8},{20,12},{24,0},{28,4},{1,25},{... | collective-permute-start | bytes 393224 | tf_op jit(solution)/shard_map/ppermute | solution.py:275
  7.7 19.0 %copy-start = (bf16[768,512]{1,0:T(8,128)(2,1)S(1)}, bf16[768,512]{1,0:T(8,128)(2,1)}, u32[]{:S(2)}) copy-start(bf16[768,512]{1,0:T(8,128)(2,1)} %constant.24.clone.forward_ref) | copy-start | bytes 2359300
  7.7 16.8 %collective-permute-start.3 = (f32[256,256]{1,0:T(8,128)S(1)}, f32[256,256]{1,0:T(8,128)S(1)}, u32[]{:S(2)}, u32[]{:S(2)}) collective-permute-start(f32[256,256]{1,0:T(8,128)S(1)} %get-tuple-element.23), channel_id=1, source_target_pairs={{0,4},{4,0},{8,12},{12,8},{16,20},{20,16},{24,28},{28,24},{1,5},{5... | collective-permute-start | bytes 786440 | tf_op jit(solution)/shard_map/ppermute | solution.py:275
  10.2 8.4 %collective-permute-start.1 = (f32[256,128]{1,0:T(8,128)S(1)}, f32[256,128]{1,0:T(8,128)S(1)}, u32[]{:S(2)}, u32[]{:S(2)}) collective-permute-start(f32[256,128]{1,0:T(8,128)S(1)} %constant_dynamic-slice_fusion.1), channel_id=1, source_target_pairs={{0,24},{4,28},{8,16},{12,20},{16,8},{20,12},{24,0},{28,4},{1,25},{... | collective-permute-start | bytes 393224 | tf_op jit(solution)/shard_map/ppermute | solution.py:275
  10.5 19.8 %collective-permute-start.4 = (f32[256,256]{1,0:T(8,128)S(1)}, f32[256,256]{1,0:T(8,128)S(1)}, u32[]{:S(2)}, u32[]{:S(2)}) collective-permute-start(f32[256,256]{1,0:T(8,128)S(1)} %get-tuple-element.24), channel_id=1, source_target_pairs={{0,20},{4,16},{8,28},{12,24},{16,4},{20,0},{24,12},{28,8},{1,21},{... | collective-permute-start | bytes 786440 | tf_op jit(solution)/shard_map/ppermute | solution.py:275
  11.2 20.1 %collective-permute-start.5 = (f32[256,256]{1,0:T(8,128)S(1)}, f32[256,256]{1,0:T(8,128)S(1)}, u32[]{:S(2)}, u32[]{:S(2)}) collective-permute-start(f32[256,256]{1,0:T(8,128)S(1)} %get-tuple-element.27), channel_id=1, source_target_pairs={{0,12},{4,8},{8,4},{12,0},{16,28},{20,24},{24,20},{28,16},{1,13},{... | collective-permute-start | bytes 786440 | tf_op jit(solution)/shard_map/ppermute | solution.py:275
  15.5 19.9 %collective-permute-start.6 = (f32[256,256]{1,0:T(8,128)S(1)}, f32[256,256]{1,0:T(8,128)S(1)}, u32[]{:S(2)}, u32[]{:S(2)}) collective-permute-start(f32[256,256]{1,0:T(8,128)S(1)} %get-tuple-element.28), channel_id=1, source_target_pairs={{0,8},{4,12},{8,0},{12,4},{16,24},{20,28},{24,16},{28,20},{1,9},{5... | collective-permute-start | bytes 786440 | tf_op jit(solution)/shard_map/ppermute | solution.py:275
  18.6 22.4 %collective-permute-start.7 = (f32[256,256]{1,0:T(8,128)S(1)}, f32[256,256]{1,0:T(8,128)S(1)}, u32[]{:S(2)}, u32[]{:S(2)}) collective-permute-start(f32[256,256]{1,0:T(8,128)S(1)} %get-tuple-element.31), channel_id=1, source_target_pairs={{0,28},{4,24},{8,20},{12,16},{16,12},{20,8},{24,4},{28,0},{1,29},{... | collective-permute-start | bytes 786440 | tf_op jit(solution)/shard_map/ppermute | solution.py:275
  24.6 26.2 %collective-permute-start = (f32[256,256]{1,0:T(8,128)S(1)}, f32[256,256]{1,0:T(8,128)S(1)}, u32[]{:S(2)}, u32[]{:S(2)}) collective-permute-start(f32[256,256]{1,0:T(8,128)S(1)} %get-tuple-element.20), channel_id=1, source_target_pairs={{0,16},{4,20},{8,24},{12,28},{16,0},{20,4},{24,8},{28,12},{1,17},{... | collective-permute-start | bytes 786440 | tf_op jit(solution)/shard_map/ppermute | solution.py:275
  26.7 0.7 %copy-start.2 = (s32[8]{0:T(128)S(1)}, s32[8]{0:T(128)}, u32[]{:S(2)}) copy-start(s32[8]{0:T(128)} %order_from.9) | copy-start | bytes 100
  26.7 0.7 %copy-start.3 = (s32[8]{0:T(128)S(1)}, s32[8]{0:T(128)}, u32[]{:S(2)}) copy-start(s32[8]{0:T(128)} %lag_from.9) | copy-start | bytes 100
  41.0 9.8 %copy-start.1 = (bf16[1536,256]{1,0:T(8,128)(2,1)S(1)}, bf16[1536,256]{1,0:T(8,128)(2,1)}, u32[]{:S(2)}) copy-start(bf16[1536,256]{1,0:T(8,128)(2,1)} %constant.25.clone.refs_0_) | copy-start | bytes 2359300
  62.2 1.2 %collective-permute-start.8 = (f32[16,1,128]{2,1,0:T(1,128)S(1)}, f32[16,1,128]{2,1,0:T(1,128)S(1)}, u32[]{:S(2)}, u32[]{:S(2)}) collective-permute-start(f32[16,1,128]{2,1,0:T(1,128)S(1)} %slice.8), channel_id=1, source_target_pairs={{0,1},{1,0},{2,3},{3,2},{4,5},{5,4},{6,7},{7,6},{8,9},{9,8},{10,11... | collective-permute-start | bytes 24584 | tf_op jit(solution)/shard_map/ppermute | solution.py:323
